TPU v7x, 768 devices: a whole 4x8x12 slice. The times are simulated.
768 devices in a mesh: group: 8 (over y_hi, core), inner: 96 (over z, y_lo, x).
Axes of the slice: x: 4, y: 8 (y_hi: 4, y_lo: 2; y = y_hi * 2 + y_lo), z: 12, core: 2. Of those that a mesh axis runs over, the one named last changes fastest.
Arguments:
- hidden_in: bfloat16 [98304, 8192], P(('group', 'inner')), may hold values from -6 to 6
- cotangent: bfloat16 [98304, 128], P(('group', 'inner')), may hold values from -6 to 6
- params: bfloat16 [96, 11008], P('inner', 'group'), may hold values from -1 to 2, as said below
Outputs:
- key_rows: bfloat16 [98304, 128], P(('group', 'inner'))
- input_grad: bfloat16 [98304, 8192], P(('group', 'inner'))
- param_grad: float32 [96, 11008], P('inner', 'group')
Inputs may be any that keep to these rules, and one draw needn't show every extreme that they name: `params`: the first 1048576 entries of the flat vector are weights of order 8192 ** -0.5, the last 8192 are gains near one.
All inputs are finite; a program needn't handle non-finite values.
Results may differ from a plain program's by a relative error of at most 0.017.
Values may be sent and summed in bfloat16 or wider, within the bound.
No kernel may reach another device: no remote copies, remote signals or barrier semaphores. Data moves between devices by JAX's collectives and lax.ppermute only.
A program may use at most 64 MiB of HBM per device.

v0:
```python
import jax
import jax.numpy as jnp
from jax import lax
from jax.sharding import PartitionSpec as P


def unpack(gathered, width, head_size):
    flat_params = gathered.reshape(-1)
    weight = flat_params[: width * head_size].reshape(width, head_size)
    norm_gain = flat_params[width * head_size :].astype(jnp.float32)
    return (weight, norm_gain)


def local(hidden_in, cotangent, params):
    width = hidden_in.shape[1]
    head_size = cotangent.shape[1]
    second = lax.all_gather(params, "group", axis=1, tiled=True)
    gathered = lax.all_gather(second, "inner", axis=0, tiled=True)
    row_length = gathered.shape[1]
    weight, norm_gain = unpack(gathered, width, head_size)
    inputs32 = hidden_in.astype(jnp.float32)
    inv_rms = lax.rsqrt(jnp.mean(inputs32 * inputs32, axis=-1, keepdims=True) + 1e-05)
    normed = inputs32 * inv_rms
    normed_rows = (normed * norm_gain).astype(jnp.bfloat16)
    key_rows = jnp.dot(normed_rows, weight, preferred_element_type=jnp.float32).astype(jnp.bfloat16)
    again = lax.all_gather(second, "inner", axis=0, tiled=True)
    back_weight, back_gain = unpack(again, width, head_size)
    back_proj = jnp.dot(cotangent, back_weight.T, preferred_element_type=jnp.float32)
    norm_back = back_proj * back_gain
    input_grad = (
        inv_rms * (norm_back - normed * jnp.mean(norm_back * normed, axis=-1, keepdims=True))
    ).astype(jnp.bfloat16)
    gain_grad = jnp.sum(back_proj * normed, axis=0)
    padded_rows = jnp.pad(normed_rows, ((0, 0), (0, width + 4)))
    gain_flat = jnp.concatenate([jnp.zeros((width * head_size,), jnp.float32), gain_grad])
    length = lax.axis_size("inner") * 1 * row_length
    span = length // head_size + 2
    flat_start = jnp.int32(0) * row_length
    first_row = jnp.minimum(flat_start // head_size, width)
    columns = lax.dynamic_slice_in_dim(padded_rows, first_row, span, 1)
    block = jnp.dot(columns.T, cotangent, preferred_element_type=jnp.float32).reshape(-1)
    weight_part = lax.dynamic_slice_in_dim(block, flat_start - first_row * head_size, length, 0)
    partial_sum = lax.psum_scatter(
        (weight_part + gain_flat).reshape(lax.axis_size("inner") * 1, row_length),
        "inner",
        scatter_dimension=0,
        tiled=True,
    )
    param_grad = lax.psum_scatter(
        partial_sum.astype(jnp.bfloat16), "group", scatter_dimension=1, tiled=True
    ).astype(jnp.float32)
    return (key_rows, input_grad, param_grad)


def solution(mesh):
    in_specs = (P(("group", "inner"), None), P(("group", "inner"), None), P("inner", "group"))
    out_specs = (P(("group", "inner"), None), P(("group", "inner"), None), P("inner", "group"))
    return jax.shard_map(local, mesh=mesh, in_specs=in_specs, out_specs=out_specs, check_vma=False)
```

profile of v0, /device:TPU:1, one launch (start us, length us, event | category | flops | bytes accessed | tf_op | source)
XLA Modules:
  0.0 1103.5 jit_solution(14451184150034008057)
XLA Ops:
  7.2 0.0 copy-start
  7.2 0.0 all-gather.3.cloned.1.call-start
  7.2 0.7 reduce
  8.0 1.3 dynamic-slice
  9.9 0.3 dynamic-update-slice
  10.2 33.3 %all-reduce.2 = bf16[11008]{0:T(1024)(128)(2,1)S(1)} all-reduce(bf16[11008]{0:T(1024)(128)(2,1)S(1)} %dynamic-update-slice), channel_id=1, replica_groups=mesh['group'=8,'inner'=96] {'group'}, use_global_device_ids=true, to_apply=%add.2 | all-reduce | flops 11008 | bytes 44032
  43.5 0.6 reshape.37
  44.1 0.0 all-gather.3.cloned.1.call-update
  44.1 0.0 reduce-scatter.4.cloned.1.call-start
  44.2 3.2 copy.10
  47.4 0.0 copy-start.1
  47.5 1.3 dynamic-slice.1
  48.8 1.1 fusion.11
  49.9 0.0 copy-done.1
  49.9 387.6 %all-gather.3.cloned.1.call-done = bf16[96,1,11008]{2,1,0:T(2,128)(2,1)} async-done(((bf16[1,1,11008]{2,1,0:T(2,128)(2,1)}), bf16[96,1,11008]{2,1,0:T(2,128)(2,1)}) %all-gather.3.cloned.1.call-update) | async-done | bytes 2113552 | tf_op jit(solution)/shard_map/all_gather | solution.py:18
  437.5 12.8 %reduce.1 = bf16[96,11008]{1,0:T(8,128)(2,1)S(1)} reduce(bf16[96,1,11008]{2,1,0:T(2,128)(2,1)} %all-gather.3.cloned.1.call-done, bf16[]{:T(256)} %constant.54), dimensions={1}, to_apply=%all-gather.reduce_sub_computation | reduce | bytes 4227074 | tf_op jit(solution)/shard_map/all_gather | solution.py:18
  450.3 4.7 reshape.32
  455.0 4.2 slice.15
  459.2 0.7 slice_convert_fusion
  459.9 0.0 copy-done
  459.9 0.0 copy-start.2
  459.9 4.4 fusion.10
  464.4 0.0 copy-done.2
  464.4 4.4 fusion.9
  468.8 2.7 fusion
  471.4 5.1 reshape.33
  476.6 423.7 %all-reduce.5 = bf16[96,11008]{1,0:T(8,128)(2,1)} all-reduce(f32[96,11008]{1,0:T(8,128)} %reshape.33), channel_id=2, replica_groups=mesh['group'=8,'inner'=96] {'inner'}, use_global_device_ids=true, to_apply=%region_3.4.clone | all-reduce | flops 1056768 | bytes 6340608
  900.3 1.6 dynamic-slice_convert_fusion
  901.9 2.2 copy.12
  904.1 0.0 reduce-scatter.4.cloned.1.call-update
  904.1 3.0 fusion.15
  907.1 4.1 copy.11
  911.1 183.8 %reduce-scatter.4.cloned.1.call-done = bf16[1376,1]{1,0:T(8,128)(2,1)} async-done(((bf16[11008,1]{1,0:T(8,128)(2,1)}), bf16[1376,1]{1,0:T(8,128)(2,1)}) %reduce-scatter.4.cloned.1.call-update) | async-done | bytes 2768
  1094.9 1.1 copy.13
  1096.1 0.6 convert_element_type.30
  (3 shorter events, 0.0 us)
Async XLA Ops:
  7.2 452.7 %copy-start = (bf16[128,128]{1,0:T(8,128)(2,1)S(1)}, bf16[128,128]{1,0:T(8,128)(2,1)}, u32[]{:S(2)}) copy-start(bf16[128,128]{1,0:T(8,128)(2,1)} %param.4) | copy-start | bytes 98308
  7.2 430.4 %all-gather.3.cloned.1.call-start = ((), (), s32[]{:S(2)}) async-start(), calls=%async_computation.1 | async-start | bytes 4271104 | tf_op jit(solution)/shard_map/all_gather | solution.py:18
  44.1 1050.8 %reduce-scatter.4.cloned.1.call-start = ((), (), s32[]{:S(2)}) async-start(), calls=%async_computation.2 | async-start | bytes 3170304
  47.4 2.4 copy-start.1
  459.9 4.5 copy-start.2
Sparse Core Ops, SparseCore 0:
  44.3 393.2 all-gather.2
  904.2 190.6 reduce-scatter.3
where the time goes:
time: 1110 us; the launch traced here: 1100 us
  waiting for transfers between devices  571 us (51%)
  blocking collectives  457 us (41%)
  local copies, waits for them, and re-layouts  29.8 us (3%)
  other arithmetic  20.4 us (2%)
  between operations  14.8 us (1%)
    unnamed x2, blocking collectives  457 us
    all_gather x1, waiting for transfers between devices, local(): gathered = lax.all_gather(second, 'inner', axis=0, tiled=True)  388 us
    unnamed x3, waiting for transfers between devices  184 us
  transfers between devices with their start and end apart: 2, of which 2 were waited for; matrix products, arithmetic and copies ran while one was open for 1% of the time, Pallas kernels for 0%

commit v1 on v0

v1 whole, which is shorter than its diff:
```python
import jax
import jax.numpy as jnp
from jax import lax
from jax.experimental import pallas as pl
from jax.experimental.pallas import tpu as pltpu
from jax.sharding import Mesh, PartitionSpec as P

AXES = ("yh", "c", "z", "yl", "x")
SIZES = (4, 2, 12, 2, 4)
ZY = ("z", "yh", "yl")
N_ZY = 96

LANES = 128
BLK = 16
USED = 12
GROUP_ROWS = 86
PIECE = 1376
EPS = 1e-05
ROWS_PAD = 8272
STEP = 512


def swap(a):
    return lax.ppermute(a, "c", [(0, 1), (1, 0)])


def shift_x(a, k):
    return lax.ppermute(a, "x", [(i, (i + k) % 4) for i in range(4)])


def sums_kernel(pos_ref, hidden_ref, cot_ref, own_ref, send_ref, inv_ref, u_ref):
    width = hidden_ref.shape[1]
    x, c = pos_ref[0], pos_ref[1]

    def squares(m, acc):
        part = hidden_ref[:, pl.ds(pl.multiple_of(m * STEP, STEP), STEP)].astype(jnp.float32)
        part = part * part
        for k in range(STEP // LANES):
            acc = acc + part[:, k * LANES : (k + 1) * LANES]
        return acc

    acc = lax.fori_loop(0, width // STEP, squares, jnp.zeros((hidden_ref.shape[0], LANES), jnp.float32))
    inv = lax.rsqrt(jnp.sum(acc, axis=1, keepdims=True) / width + EPS)
    inv_ref[...] = jnp.broadcast_to(inv, inv_ref.shape)
    cots = (cot_ref[...].astype(jnp.float32) * inv).astype(jnp.bfloat16)

    def outer(m, _):
        at = pl.multiple_of(m * STEP, STEP)
        u_ref[pl.ds(at, STEP), :] = lax.dot_general(
            hidden_ref[:, pl.ds(at, STEP)], cots, (((0,), (0,)), ((), ())), preferred_element_type=jnp.float32
        )
        return 0

    lax.fori_loop(0, width // STEP, outer, 0)
    u_ref[width:, :] = jnp.zeros((ROWS_PAD - width, LANES), jnp.float32)

    def pack(q, _):
        for k in range(4):
            base = GROUP_ROWS * (q * 4 + lax.rem(x + k, 4))
            for yh in range(4):
                at = (q // 2) * 8 + yh * 2 + lax.rem(q, 2)
                for out, core in ((own_ref, c), (send_ref, 1 - c)):
                    row = base + lax.div(43 * (2 * yh + core), 4)
                    out[k, at] = u_ref[pl.ds(row, BLK), :].astype(jnp.bfloat16)
        return 0

    lax.fori_loop(0, 24, pack, 0)


def rows_kernel(pos_ref, hidden_ref, cot_ref, inv_ref, *refs):
    pieces = (refs[:4], refs[4:8])
    key_ref, grad_ref, gain_ref, s_ref, w_ref = refs[8:]
    width = hidden_ref.shape[1]
    x, c = pos_ref[0], pos_ref[1]

    s_ref[1, 0:BLK, :] = jnp.zeros((BLK, LANES), jnp.float32)
    tail = jnp.zeros((22 - BLK, LANES), jnp.float32)
    one = jnp.zeros((1, LANES), jnp.float32)

    def assemble(q, _):
        for k in range(4):
            base = GROUP_ROWS * (q * 4 + lax.rem(x + 4 - k, 4))
            for core, group in ((c, pieces[0]), (1 - c, pieces[1])):
                s_ref[core, pl.ds(base + 85, 1), :] = one
                for yh in range(4):
                    at = (q // 2) * 8 + yh * 2 + lax.rem(q, 2)
                    row = base + lax.div(43 * (2 * yh + core), 4)
                    s_ref[core, pl.ds(row, BLK), :] = group[k][at].astype(jnp.float32)
                    rest = 6 if yh < 3 else 5
                    s_ref[core, pl.ds(row + BLK, rest), :] = tail[:rest]
        return 0

    lax.fori_loop(0, 24, assemble, 0)
    gain_ref[...] = s_ref[0, width : width + 64, :] + s_ref[1, width : width + 64, :]
    inv = inv_ref[...]

    def forward(m, key):
        at = pl.multiple_of(m * STEP, STEP)
        weight = (s_ref[0, pl.ds(at, STEP), :] + s_ref[1, pl.ds(at, STEP), :]).astype(jnp.bfloat16)
        w_ref[pl.ds(at, STEP), :] = weight
        rows = []
        for k in range(STEP // LANES):
            part = hidden_ref[:, pl.ds(pl.multiple_of(at + k * LANES, LANES), LANES)].astype(jnp.float32)
            gain = gain_ref[pl.ds(m * (STEP // LANES) + k, 1), :]
            rows.append((part * inv * gain).astype(jnp.bfloat16))
        return key + jnp.dot(jnp.concatenate(rows, axis=1), weight, preferred_element_type=jnp.float32)

    key = lax.fori_loop(0, width // STEP, forward, jnp.zeros(key_ref.shape, jnp.float32))
    key_ref[...] = key.astype(jnp.bfloat16)
    cot = cot_ref[...]
    scale = inv * (jnp.sum(cot.astype(jnp.float32) * key, axis=1, keepdims=True) / width)

    def backward(m, _):
        at = pl.multiple_of(m * STEP, STEP)
        back = lax.dot_general(
            cot, w_ref[pl.ds(at, STEP), :], (((1,), (1,)), ((), ())), preferred_element_type=jnp.float32
        )
        for k in range(STEP // LANES):
            lanes = pl.ds(pl.multiple_of(at + k * LANES, LANES), LANES)
            part = hidden_ref[:, lanes].astype(jnp.float32)
            gain = gain_ref[pl.ds(m * (STEP // LANES) + k, 1), :]
            grad = inv * (back[:, k * LANES : (k + 1) * LANES] * gain - part * scale)
            grad_ref[:, lanes] = grad.astype(jnp.bfloat16)
        return 0

    lax.fori_loop(0, width // STEP, backward, 0)


def local(hidden_in, cotangent, params):
    tokens, width = hidden_in.shape
    x, c, z = lax.axis_index("x"), lax.axis_index("c"), lax.axis_index("z")
    yh, yl = lax.axis_index("yh"), lax.axis_index("yl")
    inner, j = (z * 2 + yl) * 4 + x, yh * 2 + c
    first_row, lane = (43 * j) // 4, (96 * j) % LANES
    pos = jnp.stack([x, c]).astype(jnp.int32)
    smem = pl.BlockSpec(memory_space=pltpu.SMEM)
    vmem = pl.BlockSpec(memory_space=pltpu.VMEM)
    bf16, f32 = jnp.bfloat16, jnp.float32

    flat = jnp.pad(params.reshape(-1), (LANES, BLK * LANES - PIECE))
    block = lax.dynamic_slice(flat, (LANES - lane,), (BLK * LANES,)).reshape(1, BLK, LANES)
    mine = lax.all_to_all(jnp.broadcast_to(block, (N_ZY, BLK, LANES)), ZY, 0, 0, tiled=True)

    half = jax.ShapeDtypeStruct((4, N_ZY, BLK, LANES), bf16)
    own, send, inv = pl.pallas_call(
        sums_kernel,
        out_shape=(half, half, jax.ShapeDtypeStruct((tokens, LANES), f32)),
        in_specs=[smem, vmem, vmem],
        out_specs=(vmem, vmem, vmem),
        scratch_shapes=[pltpu.VMEM((ROWS_PAD, LANES), f32)],
        compiler_params=pltpu.CompilerParams(vmem_limit_bytes=24 << 20),
        cost_estimate=pl.CostEstimate(flops=4 * tokens * width * LANES, bytes_accessed=8 << 20, transcendentals=0),
    )(pos, hidden_in, cotangent)
    got = swap(send)
    pair = [own[k].astype(f32) + got[k].astype(f32) for k in range(4)]
    moved = [shift_x(pair[k].astype(bf16), k) for k in range(1, 4)]

    held = [mine] + [shift_x(mine, k) for k in range(1, 4)]
    other = [swap(a) for a in held]

    total = pair[0] + moved[0].astype(f32) + moved[1].astype(f32) + moved[2].astype(f32)
    gain_part = jnp.sum(mine.astype(f32) * total, axis=-1)[:, :USED].reshape(12, 8 * USED)
    pays = [jnp.zeros((512,), f32)]
    for start in (0, 3, 7):
        pays.append(jnp.pad(gain_part[start : start + 5].reshape(-1), (0, 32)))
    pay = jnp.stack(pays).reshape(4, 1, 4, LANES)
    pay = jnp.concatenate([jnp.zeros_like(pay), pay], axis=1).reshape(8, 4, LANES)
    pay = jnp.pad(pay, ((N_ZY - 8, 0), (USED, 0), (0, 0)))
    spare = lax.broadcasted_iota(jnp.int32, (1, BLK, 1), 1) >= USED
    chunk = jnp.where(spare, pay, total).astype(bf16)
    sums = lax.all_to_all(chunk, ZY, 0, 0, tiled=True).astype(f32).sum(axis=0)

    key_rows, input_grad, gains = pl.pallas_call(
        rows_kernel,
        out_shape=(
            jax.ShapeDtypeStruct((tokens, LANES), bf16),
            jax.ShapeDtypeStruct((tokens, width), bf16),
            jax.ShapeDtypeStruct((64, LANES), f32),
        ),
        in_specs=[smem] + [vmem] * 11,
        out_specs=(vmem, vmem, vmem),
        scratch_shapes=[pltpu.VMEM((2, ROWS_PAD, LANES), f32), pltpu.VMEM((width, LANES), bf16)],
        compiler_params=pltpu.CompilerParams(vmem_limit_bytes=36 << 20),
        cost_estimate=pl.CostEstimate(flops=4 * tokens * width * LANES, bytes_accessed=10 << 20, transcendentals=0),
    )(pos, hidden_in, cotangent, inv, *held, *other)

    part = sums[USED:]
    parts = jnp.stack([shift_x(part, 3), shift_x(part, 2), shift_x(part, 1), part])
    theirs = swap(parts)
    both = jnp.stack([jnp.where(c == 0, parts, theirs), jnp.where(c == 0, theirs, parts)])
    both = both.reshape(2, 4, 512)[:, :, :480].reshape(2, 4, 5, 4, 2, USED)
    by_row = 0.0
    for core in range(2):
        for hi in range(4):
            at = (43 * (2 * hi + core)) // 4
            by_row = by_row + jnp.pad(both[core, :, :, hi], ((0, 0), (0, 0), (0, 0), (at, 88 - USED - at)))
    by_row = by_row[..., :GROUP_ROWS].transpose(1, 2, 0, 3).reshape(-1)
    start = jnp.where(yh == 2, 3, jnp.where(yh == 3, 7, 0)) * 688
    gain_grad = lax.dynamic_slice(jnp.pad(by_row, (2816, 0)), (PIECE * j - start,), (PIECE,))

    row_gain = lax.dynamic_slice(jnp.pad(gains.reshape(-1), (0, 80)), (GROUP_ROWS * inner + first_row,), (USED,))
    weight_grad = (sums[:USED] * row_gain[:, None]).reshape(-1)
    weight_grad = lax.dynamic_slice(weight_grad, (lane,), (PIECE,))
    param_grad = weight_grad + jnp.where(inner == 95, gain_grad, 0.0)
    return (key_rows, input_grad, param_grad.reshape(1, PIECE))


def solution(mesh):
    fine = Mesh(mesh.devices.reshape(SIZES), AXES)
    tokens = P(AXES, None)
    params = P(("z", "yl", "x"), ("yh", "c"))
    return jax.shard_map(
        local, mesh=fine, in_specs=(tokens, tokens, params), out_specs=(tokens, tokens, params), check_vma=False
    )
```

time: 1110 us -> 144 us (0.13)
  waiting for transfers between devices: 571 us -> 20.9 us
  blocking collectives: 457 us -> 0 us
  starting transfers between devices: 0.08 us -> 90.3 us
  local copies, waits for them, and re-layouts: 29.8 us -> 4.78 us
  Pallas kernels: 0 us -> 18.4 us
  between operations: 14.8 us -> 1.05 us
  other arithmetic: 20.4 us -> 8.08 us
    unnamed x2 -> x0, blocking collectives: 457 us -> none
    all_gather x1 -> x0, waiting for transfers between devices: 388 us -> none  [local(): gathered = lax.all_gather(second, 'inner', axis=0, tiled=True)]
    unnamed x3 -> x0, waiting for transfers between devices: 184 us -> none
    ppermute x0 -> x15, starting transfers between devices: none -> 62.5 us  [the longest x6 36.1 us: swap(): return lax.ppermute(a, 'c', [(0, 1), (1, 0)])]
    all_to_all x0 -> x2, starting transfers between devices: none -> 27.8 us  [the longest x1 15.1 us: local(): sums = lax.all_to_all(chunk, ZY, 0, 0, tiled=True).astype(f32).sum(axis=0)]
    pallas_call x0 -> x2, Pallas kernels: none -> 18.4 us  [the longest x1 11.4 us: local(): pl.pallas_call(rows_kernel, out_shape=(jax.ShapeDtypeStruct((tokens, LANE...]
    all_gather x1 -> x0, other arithmetic: 12.8 us -> none  [local(): gathered = lax.all_gather(second, 'inner', axis=0, tiled=True)]
    unnamed x15 -> x14, local copies, waits for them, and re-layouts: 14.2 us -> 2.37 us
  transfers between devices with their start and end apart: 2 -> 17, of which waited for: 2 -> 7; matrix products, arithmetic and copies ran while one was open for 1% -> 2% of each run, Pallas kernels for 0% -> 8%
where the time goes in v1:
time: 144 us
  starting transfers between devices  90.3 us (63%)
  waiting for transfers between devices  20.9 us (15%)
  Pallas kernels  18.4 us (13%)
  other arithmetic  8.08 us (6%)
  local copies, waits for them, and re-layouts  4.78 us (3%)
    ppermute x6, starting transfers between devices, swap(): return lax.ppermute(a, 'c', [(0, 1), (1, 0)])  36.1 us
    ppermute x9, starting transfers between devices, shift_x(): return lax.ppermute(a, 'x', [(i, (i + k) % 4) for i in range(4)])  26.5 us
    all_to_all x1, starting transfers between devices, local(): sums = lax.all_to_all(chunk, ZY, 0, 0, tiled=True).astype(f32).sum(axis=0)  15.1 us
    all_to_all x1, starting transfers between devices, local(): lax.all_to_all(jnp.broadcast_to(block, (N_ZY, BLK, LANES)), ZY, 0, 0, til...  12.7 us
    pallas_call x1, Pallas kernels, local(): pl.pallas_call(rows_kernel, out_shape=(jax.ShapeDtypeStruct((tokens, LANE...  11.4 us
    all_to_all x1, waiting for transfers between devices, local(): lax.all_to_all(jnp.broadcast_to(block, (N_ZY, BLK, LANES)), ZY, 0, 0, til...  9.91 us
    ppermute x9, waiting for transfers between devices, shift_x(): return lax.ppermute(a, 'x', [(i, (i + k) % 4) for i in range(4)])  8.7 us
    pallas_call x1, Pallas kernels, local(): pl.pallas_call(sums_kernel, out_shape=(half, half, jax.ShapeDtypeStruct((...  7 us
  transfers between devices with their start and end apart: 17, of which 7 were waited for; matrix products, arithmetic and copies ran while one was open for 2% of the time, Pallas kernels for 8%

profile of v1, /device:TPU:1, one launch (start us, length us, event | category | flops | bytes accessed | tf_op | source)
XLA Modules:
  0.0 143.6 jit_solution(10288632668506887597)
XLA Ops:
  0.6 0.1 pad_add_fusion.6.pos_ref
  0.7 1.6 %copy-done = bf16[128,8192]{1,0:T(8,128)(2,1)S(1)} copy-done((bf16[128,8192]{1,0:T(8,128)(2,1)S(1)}, bf16[128,8192]{1,0:T(8,128)(2,1)}, u32[]{:S(2)}) %copy-start) | copy-done | bytes 2097176
  2.3 0.8 copy-done.3
  3.1 7.0 %shard_map.58 = (bf16[4,96,16,128]{3,2,1,0:T(8,128)(2,1)S(1)}, bf16[4,96,16,128]{3,2,1,0:T(8,128)(2,1)}, f32[128,128]{1,0:T(8,128)S(1)}) custom-call(s32[2]{0:T(128)S(1)} %pad_add_fusion.6.pos_ref, bf16[128,8192]{1,0:T(8,128)(2,1)S(1)} %copy-done, bf16[128,128]{1,0:T(8,128)(2,1)S(1)} %copy-done.3), custom_call_target="tpu_custom_call" | custom-call | flops 536870912 | bytes 8388608 | tf_op jit(solution)/shard_map/pallas_call | solution.py:145
  10.1 12.4 %collective-permute-start.7 = (bf16[4,96,16,128]{3,2,1,0:T(8,128)(2,1)}, bf16[4,96,16,128]{3,2,1,0:T(8,128)(2,1)}, u32[]{:S(2)}, u32[]{:S(2)}) collective-permute-start(bf16[4,96,16,128]{3,2,1,0:T(8,128)(2,1)} %get-tuple-element.13), channel_id=1, source_target_pairs={{0,96},{96,0},{1,97},{97,1},{2,98},{98,2},{3,99},{99,3},{4,100},{1... | collective-permute-start | bytes 4718600 | tf_op jit(solution)/shard_map/ppermute | solution.py:24
  22.6 0.1 fusion.9
  22.7 0.8 broadcast_in_dim.22
  23.5 12.7 %all-to-all-start = ((bf16[96,16,128]{2,1,0:T(8,128)(2,1)}), bf16[96,16,128]{2,1,0:T(8,128)(2,1)S(1)}, u32[]{:S(2)}, u32[]{:S(2)}) async-start(bf16[96,16,128]{2,1,0:T(8,128)(2,1)} %broadcast_in_dim.22), calls=%async_computation | async-start | bytes 786432 | tf_op jit(solution)/shard_map/all_to_all | solution.py:142
  36.2 2.4 %fusion.2 = (bf16[96,16,128]{2,1,0:T(8,128)(2,1)}, bf16[96,16,128]{2,1,0:T(8,128)(2,1)}, bf16[96,16,128]{2,1,0:T(8,128)(2,1)}) fusion(bf16[4,96,16,128]{3,2,1,0:T(8,128)(2,1)} %collective-permute-done.7, bf16[4,96,16,128]{3,2,1,0:T(8,128)(2,1)S(1)} %get-tuple-element.12), kind=kLoop, calls=%fused_computation.9 | loop fusion | flops 2359296 | bytes 3538944 | tf_op jit(solution)/shard_map/convert_element_type | solution.py:156
  38.6 4.4 %collective-permute-start.10 = (bf16[96,16,128]{2,1,0:T(8,128)(2,1)}, bf16[96,16,128]{2,1,0:T(8,128)(2,1)S(1)}, u32[]{:S(2)}, u32[]{:S(2)}) collective-permute-start(bf16[96,16,128]{2,1,0:T(8,128)(2,1)} %get-tuple-element.16), channel_id=1, source_target_pairs={{0,3},{1,0},{2,1},{3,2},{4,7},{5,4},{6,5},{7,6},{8,11},{9,8},{10,9... | collective-permute-start | bytes 1179656 | tf_op jit(solution)/shard_map/ppermute | solution.py:28
  43.0 1.9 %collective-permute-start.8 = (bf16[96,16,128]{2,1,0:T(8,128)(2,1)}, bf16[96,16,128]{2,1,0:T(8,128)(2,1)S(1)}, u32[]{:S(2)}, u32[]{:S(2)}) collective-permute-start(bf16[96,16,128]{2,1,0:T(8,128)(2,1)} %get-tuple-element.15), channel_id=1, source_target_pairs={{0,1},{1,2},{2,3},{3,0},{4,5},{5,6},{6,7},{7,4},{8,9},{9,10},{10,1... | collective-permute-start | bytes 1179656 | tf_op jit(solution)/shard_map/ppermute | solution.py:28
  44.9 3.6 %collective-permute-start.9 = (bf16[96,16,128]{2,1,0:T(8,128)(2,1)}, bf16[96,16,128]{2,1,0:T(8,128)(2,1)S(1)}, u32[]{:S(2)}, u32[]{:S(2)}) collective-permute-start(bf16[96,16,128]{2,1,0:T(8,128)(2,1)} %get-tuple-element.17), channel_id=1, source_target_pairs={{0,2},{1,3},{2,0},{3,1},{4,6},{5,7},{6,4},{7,5},{8,10},{9,11},{10,... | collective-permute-start | bytes 1179656 | tf_op jit(solution)/shard_map/ppermute | solution.py:28
  48.6 9.9 %all-to-all-done.refs_0_ = bf16[96,16,128]{2,1,0:T(8,128)(2,1)S(1)} async-done(((bf16[96,16,128]{2,1,0:T(8,128)(2,1)}), bf16[96,16,128]{2,1,0:T(8,128)(2,1)S(1)}, u32[]{:S(2)}, u32[]{:S(2)}) %all-to-all-start) | async-done | bytes 393248 | tf_op jit(solution)/shard_map/all_to_all | solution.py:142
  58.5 1.3 collective-permute-done.10
  59.8 4.1 %collective-permute-done.9 = bf16[96,16,128]{2,1,0:T(8,128)(2,1)S(1)} collective-permute-done((bf16[96,16,128]{2,1,0:T(8,128)(2,1)}, bf16[96,16,128]{2,1,0:T(8,128)(2,1)S(1)}, u32[]{:S(2)}, u32[]{:S(2)}) %collective-permute-start.9) | collective-permute-done | bytes 393248 | tf_op jit(solution)/shard_map/ppermute | solution.py:28
  63.9 1.6 %multiply_reduce_fusion = bf16[96,16]{1,0:T(8,128)(2,1)S(1)} fusion(bf16[96,16,128]{2,1,0:T(8,128)(2,1)S(1)} %all-to-all-done.refs_0_, bf16[96,16,128]{2,1,0:T(8,128)(2,1)S(1)} %collective-permute-done.10, bf16[96,16,128]{2,1,0:T(8,128)(2,1)S(1)} %collective-permute-done.9, bf16[96,16,128]{2,1,0:T(8,128)(2,1)S(1)} %collective-permute-done.8, ...), kind=kLoop, calls=%fused_computation.5 | loop fusion | flops 2357760 | bytes 2362368 | tf_op jit(solution)/shard_map/reduce_sum | solution.py:162
  65.5 0.1 reshape.81
  65.6 0.1 reshape.82
  65.7 0.1 reshape.80
  65.9 0.1 pad_maximum_fusion.1
  66.0 0.0 copy-start.4
  66.0 2.4 %select_convert_fusion = bf16[96,16,128]{2,1,0:T(8,128)(2,1)} fusion(bf16[8,4,128]{2,1,0:T(4,128)(2,1)S(1)} %bitcast.69, pred[16]{0:T(512)(128)(4,1)S(1)} %iota_compare_fusion, bf16[96,16,128]{2,1,0:T(8,128)(2,1)S(1)} %collective-permute-done.10, bf16[96,16,128]{2,1,0:T(8,128)(2,1)} %copy-done.5, bf16[96,16,128]{2,1,0:T(8,128)(2,1)S(1)} %collective-permute-done.8, ...), kind=kLoop, calls=%fused_computation.4 | loop fusion | flops 1966080 | bytes 2367504 | tf_op jit(solution)/shard_map/convert_element_type | solution.py:170
  68.4 15.1 %all-to-all-start.1 = ((bf16[96,16,128]{2,1,0:T(8,128)(2,1)}), bf16[96,16,128]{2,1,0:T(8,128)(2,1)}, u32[]{:S(2)}, u32[]{:S(2)}) async-start(bf16[96,16,128]{2,1,0:T(8,128)(2,1)} %select_convert_fusion), calls=%async_computation.1 | async-start | bytes 786432 | tf_op jit(solution)/shard_map/all_to_all | solution.py:171
  83.5 1.9 %collective-permute-start = (bf16[96,16,128]{2,1,0:T(8,128)(2,1)S(1)}, bf16[96,16,128]{2,1,0:T(8,128)(2,1)S(1)}, u32[]{:S(2)}, u32[]{:S(2)}) collective-permute-start(bf16[96,16,128]{2,1,0:T(8,128)(2,1)S(1)} %all-to-all-done.refs_0_), channel_id=1, source_target_pairs={{0,1},{1,2},{2,3},{3,0},{4,5},{5,6},{6,7},{7,4},{8,9},{9,10},{10,1... | collective-permute-start | bytes 1179656 | tf_op jit(solution)/shard_map/ppermute | solution.py:28
  85.4 3.4 %collective-permute-start.1 = (bf16[96,16,128]{2,1,0:T(8,128)(2,1)S(1)}, bf16[96,16,128]{2,1,0:T(8,128)(2,1)S(1)}, u32[]{:S(2)}, u32[]{:S(2)}) collective-permute-start(bf16[96,16,128]{2,1,0:T(8,128)(2,1)S(1)} %all-to-all-done.refs_0_), channel_id=1, source_target_pairs={{0,2},{1,3},{2,0},{3,1},{4,6},{5,7},{6,4},{7,5},{8,10},{9,11},{10,... | collective-permute-start | bytes 1179656 | tf_op jit(solution)/shard_map/ppermute | solution.py:28
  88.9 4.0 %collective-permute-start.2 = (bf16[96,16,128]{2,1,0:T(8,128)(2,1)S(1)}, bf16[96,16,128]{2,1,0:T(8,128)(2,1)}, u32[]{:S(2)}, u32[]{:S(2)}) collective-permute-start(bf16[96,16,128]{2,1,0:T(8,128)(2,1)S(1)} %all-to-all-done.refs_0_), channel_id=1, source_target_pairs={{0,3},{1,0},{2,1},{3,2},{4,7},{5,4},{6,5},{7,6},{8,11},{9,8},{10,9... | collective-permute-start | bytes 1179656 | tf_op jit(solution)/shard_map/ppermute | solution.py:28
  92.9 4.5 %collective-permute-start.3 = (bf16[96,16,128]{2,1,0:T(8,128)(2,1)S(1)}, bf16[96,16,128]{2,1,0:T(8,128)(2,1)}, u32[]{:S(2)}, u32[]{:S(2)}) collective-permute-start(bf16[96,16,128]{2,1,0:T(8,128)(2,1)S(1)} %all-to-all-done.refs_0_), channel_id=1, source_target_pairs={{0,96},{96,0},{1,97},{97,1},{2,98},{98,2},{3,99},{99,3},{4,100},{1... | collective-permute-start | bytes 1179656 | tf_op jit(solution)/shard_map/ppermute | solution.py:24
  97.4 11.1 %collective-permute-start.4 = (bf16[96,16,128]{2,1,0:T(8,128)(2,1)S(1)}, bf16[96,16,128]{2,1,0:T(8,128)(2,1)}, u32[]{:S(2)}, u32[]{:S(2)}) collective-permute-start(bf16[96,16,128]{2,1,0:T(8,128)(2,1)S(1)} %collective-permute-done.refs_1_), channel_id=1, source_target_pairs={{0,96},{96,0},{1,97},{97,1},{2,98},{98,2},{3,99},{99,3},{4,100},{1... | collective-permute-start | bytes 1179656 | tf_op jit(solution)/shard_map/ppermute | solution.py:24
  108.5 1.9 %collective-permute-start.5 = (bf16[96,16,128]{2,1,0:T(8,128)(2,1)S(1)}, bf16[96,16,128]{2,1,0:T(8,128)(2,1)}, u32[]{:S(2)}, u32[]{:S(2)}) collective-permute-start(bf16[96,16,128]{2,1,0:T(8,128)(2,1)S(1)} %collective-permute-done.1.refs_2_), channel_id=1, source_target_pairs={{0,96},{96,0},{1,97},{97,1},{2,98},{98,2},{3,99},{99,3},{4,100},{1... | collective-permute-start | bytes 1179656 | tf_op jit(solution)/shard_map/ppermute | solution.py:24
  110.4 2.4 %collective-permute-start.6 = (bf16[96,16,128]{2,1,0:T(8,128)(2,1)}, bf16[96,16,128]{2,1,0:T(8,128)(2,1)}, u32[]{:S(2)}, u32[]{:S(2)}) collective-permute-start(bf16[96,16,128]{2,1,0:T(8,128)(2,1)} %collective-permute-done.2.refs_3_), channel_id=1, source_target_pairs={{0,96},{96,0},{1,97},{97,1},{2,98},{98,2},{3,99},{99,3},{4,100},{1... | collective-permute-start | bytes 1179656 | tf_op jit(solution)/shard_map/ppermute | solution.py:24
  112.9 1.6 %collective-permute-done.6.refs_7_ = bf16[96,16,128]{2,1,0:T(8,128)(2,1)} collective-permute-done((bf16[96,16,128]{2,1,0:T(8,128)(2,1)}, bf16[96,16,128]{2,1,0:T(8,128)(2,1)}, u32[]{:S(2)}, u32[]{:S(2)}) %collective-permute-start.6) | collective-permute-done | bytes 393248 | tf_op jit(solution)/shard_map/ppermute | solution.py:24
  114.5 11.4 %shard_map.59 = (bf16[128,128]{1,0:T(8,128)(2,1)}, bf16[128,8192]{1,0:T(8,128)(2,1)}, f32[64,128]{1,0:T(8,128)S(1)}) custom-call(s32[2]{0:T(128)S(1)} %pad_add_fusion.6.pos_ref, bf16[128,8192]{1,0:T(8,128)(2,1)S(1)} %copy-done.1, bf16[128,128]{1,0:T(8,128)(2,1)S(1)} %copy-done.4, f32[128,128]{1,0:T(8,128)S(1)} %get-tuple-element.9.inv_ref, ...), custom_call_target="tpu_custom_call" | custom-call | flops 536870912 | bytes 10485760 | tf_op jit(solution)/shard_map/pallas_call | solution.py:173
  125.9 1.1 convert_reduce_fusion
  127.0 2.5 %collective-permute-start.11 = (f32[4,128]{1,0:T(4,128)S(1)}, f32[4,128]{1,0:T(4,128)S(1)}, u32[]{:S(2)}, u32[]{:S(2)}) collective-permute-start(f32[4,128]{1,0:T(4,128)S(1)} %get-tuple-element.31), channel_id=1, source_target_pairs={{0,3},{1,0},{2,1},{3,2},{4,7},{5,4},{6,5},{7,6},{8,11},{9,8},{10,9... | collective-permute-start | bytes 6152 | tf_op jit(solution)/shard_map/ppermute | solution.py:28
  129.6 2.2 %collective-permute-start.12 = (f32[4,128]{1,0:T(4,128)S(1)}, f32[4,128]{1,0:T(4,128)S(1)}, u32[]{:S(2)}, u32[]{:S(2)}) collective-permute-start(f32[4,128]{1,0:T(4,128)S(1)} %get-tuple-element.31), channel_id=1, source_target_pairs={{0,2},{1,3},{2,0},{3,1},{4,6},{5,7},{6,4},{7,5},{8,10},{9,11},{10,... | collective-permute-start | bytes 6152 | tf_op jit(solution)/shard_map/ppermute | solution.py:28
  131.8 2.4 %collective-permute-start.13 = (f32[4,128]{1,0:T(4,128)S(1)}, f32[4,128]{1,0:T(4,128)S(1)}, u32[]{:S(2)}, u32[]{:S(2)}) collective-permute-start(f32[4,128]{1,0:T(4,128)S(1)} %get-tuple-element.31), channel_id=1, source_target_pairs={{0,1},{1,2},{2,3},{3,0},{4,5},{5,6},{6,7},{7,4},{8,9},{9,10},{10,1... | collective-permute-start | bytes 6152 | tf_op jit(solution)/shard_map/ppermute | solution.py:28
  134.3 0.1 pad_dynamic-slice_fusion
  134.3 1.1 collective-permute-done.12
  135.4 2.2 %collective-permute-done.13 = f32[4,128]{1,0:T(4,128)S(1)} collective-permute-done((f32[4,128]{1,0:T(4,128)S(1)}, f32[4,128]{1,0:T(4,128)S(1)}, u32[]{:S(2)}, u32[]{:S(2)}) %collective-permute-start.13) | collective-permute-done | bytes 2080 | tf_op jit(solution)/shard_map/ppermute | solution.py:28
  137.6 3.7 %collective-permute-start.14 = (f32[4,4,128]{2,1,0:T(4,128)S(1)}, f32[4,4,128]{2,1,0:T(4,128)S(1)}, u32[]{:S(2)}, u32[]{:S(2)}) collective-permute-start(f32[4,4,128]{2,1,0:T(4,128)S(1)} %pad_maximum_fusion.2), channel_id=1, source_target_pairs={{0,96},{96,0},{1,97},{97,1},{2,98},{98,2},{3,99},{99,3},{4,100},{1... | collective-permute-start | bytes 24584 | tf_op jit(solution)/shard_map/ppermute | solution.py:24
  141.3 0.1 fusion.8
  141.4 0.7 collective-permute-done.14
  142.2 0.2 reshape.86
  142.5 0.1 slice_bitcast_fusion.7
  142.5 0.2 fusion.5
  142.8 0.1 reshape.87
  142.9 0.1 fusion.7
  143.0 0.6 reshape.88
  (35 shorter events, 0.2 us)
Async XLA Ops:
  0.6 21.9 %copy-start.6 = (bf16[1,1376]{1,0:T(2,128)(2,1)S(1)}, bf16[1,1376]{1,0:T(2,128)(2,1)}, u32[]{:S(2)}) copy-start(bf16[1,1376]{1,0:T(2,128)(2,1)} %param.5) | copy-start | bytes 8260
  0.7 1.6 %copy-start = (bf16[128,8192]{1,0:T(8,128)(2,1)S(1)}, bf16[128,8192]{1,0:T(8,128)(2,1)}, u32[]{:S(2)}) copy-start(bf16[128,8192]{1,0:T(8,128)(2,1)} %hidden_ref.3) | copy-start | bytes 6291460
  2.3 0.8 copy-start.3
  10.1 53.9 %copy-start.2 = (bf16[4,96,16,128]{3,2,1,0:T(8,128)(2,1)}, bf16[4,96,16,128]{3,2,1,0:T(8,128)(2,1)S(1)}, u32[]{:S(2)}) copy-start(bf16[4,96,16,128]{3,2,1,0:T(8,128)(2,1)S(1)} %get-tuple-element.12) | copy-start | bytes 4718596
  10.1 26.1 %collective-permute-start.7 = (bf16[4,96,16,128]{3,2,1,0:T(8,128)(2,1)}, bf16[4,96,16,128]{3,2,1,0:T(8,128)(2,1)}, u32[]{:S(2)}, u32[]{:S(2)}) collective-permute-start(bf16[4,96,16,128]{3,2,1,0:T(8,128)(2,1)} %get-tuple-element.13), channel_id=1, source_target_pairs={{0,96},{96,0},{1,97},{97,1},{2,98},{98,2},{3,99},{99,3},{4,100},{1... | collective-permute-start | bytes 4718600 | tf_op jit(solution)/shard_map/ppermute | solution.py:24
  23.5 35.0 %all-to-all-start = ((bf16[96,16,128]{2,1,0:T(8,128)(2,1)}), bf16[96,16,128]{2,1,0:T(8,128)(2,1)S(1)}, u32[]{:S(2)}, u32[]{:S(2)}) async-start(bf16[96,16,128]{2,1,0:T(8,128)(2,1)} %broadcast_in_dim.22), calls=%async_computation | async-start | bytes 786432 | tf_op jit(solution)/shard_map/all_to_all | solution.py:142
  38.6 21.2 %collective-permute-start.10 = (bf16[96,16,128]{2,1,0:T(8,128)(2,1)}, bf16[96,16,128]{2,1,0:T(8,128)(2,1)S(1)}, u32[]{:S(2)}, u32[]{:S(2)}) collective-permute-start(bf16[96,16,128]{2,1,0:T(8,128)(2,1)} %get-tuple-element.16), channel_id=1, source_target_pairs={{0,3},{1,0},{2,1},{3,2},{4,7},{5,4},{6,5},{7,6},{8,11},{9,8},{10,9... | collective-permute-start | bytes 1179656 | tf_op jit(solution)/shard_map/ppermute | solution.py:28
  43.0 16.8 %collective-permute-start.8 = (bf16[96,16,128]{2,1,0:T(8,128)(2,1)}, bf16[96,16,128]{2,1,0:T(8,128)(2,1)S(1)}, u32[]{:S(2)}, u32[]{:S(2)}) collective-permute-start(bf16[96,16,128]{2,1,0:T(8,128)(2,1)} %get-tuple-element.15), channel_id=1, source_target_pairs={{0,1},{1,2},{2,3},{3,0},{4,5},{5,6},{6,7},{7,4},{8,9},{9,10},{10,1... | collective-permute-start | bytes 1179656 | tf_op jit(solution)/shard_map/ppermute | solution.py:28
  44.9 19.0 %collective-permute-start.9 = (bf16[96,16,128]{2,1,0:T(8,128)(2,1)}, bf16[96,16,128]{2,1,0:T(8,128)(2,1)S(1)}, u32[]{:S(2)}, u32[]{:S(2)}) collective-permute-start(bf16[96,16,128]{2,1,0:T(8,128)(2,1)} %get-tuple-element.17), channel_id=1, source_target_pairs={{0,2},{1,3},{2,0},{3,1},{4,6},{5,7},{6,4},{7,5},{8,10},{9,11},{10,... | collective-permute-start | bytes 1179656 | tf_op jit(solution)/shard_map/ppermute | solution.py:28
  63.9 2.0 %copy-start.5 = (bf16[96,16,128]{2,1,0:T(8,128)(2,1)}, bf16[96,16,128]{2,1,0:T(8,128)(2,1)S(1)}, u32[]{:S(2)}) copy-start(bf16[96,16,128]{2,1,0:T(8,128)(2,1)S(1)} %collective-permute-done.9) | copy-start | bytes 1179652
  66.0 48.6 %copy-start.1 = (bf16[128,8192]{1,0:T(8,128)(2,1)S(1)}, bf16[128,8192]{1,0:T(8,128)(2,1)}, u32[]{:S(2)}) copy-start(bf16[128,8192]{1,0:T(8,128)(2,1)} %hidden_ref.3) | copy-start | bytes 6291460
  66.0 48.5 %copy-start.4 = (bf16[128,128]{1,0:T(8,128)(2,1)S(1)}, bf16[128,128]{1,0:T(8,128)(2,1)}, u32[]{:S(2)}) copy-start(bf16[128,128]{1,0:T(8,128)(2,1)} %cot_ref.3) | copy-start | bytes 98308
  68.4 57.5 %all-to-all-start.1 = ((bf16[96,16,128]{2,1,0:T(8,128)(2,1)}), bf16[96,16,128]{2,1,0:T(8,128)(2,1)}, u32[]{:S(2)}, u32[]{:S(2)}) async-start(bf16[96,16,128]{2,1,0:T(8,128)(2,1)} %select_convert_fusion), calls=%async_computation.1 | async-start | bytes 786432 | tf_op jit(solution)/shard_map/all_to_all | solution.py:171
  83.5 13.9 %collective-permute-start = (bf16[96,16,128]{2,1,0:T(8,128)(2,1)S(1)}, bf16[96,16,128]{2,1,0:T(8,128)(2,1)S(1)}, u32[]{:S(2)}, u32[]{:S(2)}) collective-permute-start(bf16[96,16,128]{2,1,0:T(8,128)(2,1)S(1)} %all-to-all-done.refs_0_), channel_id=1, source_target_pairs={{0,1},{1,2},{2,3},{3,0},{4,5},{5,6},{6,7},{7,4},{8,9},{9,10},{10,1... | collective-permute-start | bytes 1179656 | tf_op jit(solution)/shard_map/ppermute | solution.py:28
  85.4 23.0 %collective-permute-start.1 = (bf16[96,16,128]{2,1,0:T(8,128)(2,1)S(1)}, bf16[96,16,128]{2,1,0:T(8,128)(2,1)S(1)}, u32[]{:S(2)}, u32[]{:S(2)}) collective-permute-start(bf16[96,16,128]{2,1,0:T(8,128)(2,1)S(1)} %all-to-all-done.refs_0_), channel_id=1, source_target_pairs={{0,2},{1,3},{2,0},{3,1},{4,6},{5,7},{6,4},{7,5},{8,10},{9,11},{10,... | collective-permute-start | bytes 1179656 | tf_op jit(solution)/shard_map/ppermute | solution.py:28
  88.9 21.5 %collective-permute-start.2 = (bf16[96,16,128]{2,1,0:T(8,128)(2,1)S(1)}, bf16[96,16,128]{2,1,0:T(8,128)(2,1)}, u32[]{:S(2)}, u32[]{:S(2)}) collective-permute-start(bf16[96,16,128]{2,1,0:T(8,128)(2,1)S(1)} %all-to-all-done.refs_0_), channel_id=1, source_target_pairs={{0,3},{1,0},{2,1},{3,2},{4,7},{5,4},{6,5},{7,6},{8,11},{9,8},{10,9... | collective-permute-start | bytes 1179656 | tf_op jit(solution)/shard_map/ppermute | solution.py:28
  92.9 20.1 %collective-permute-start.3 = (bf16[96,16,128]{2,1,0:T(8,128)(2,1)S(1)}, bf16[96,16,128]{2,1,0:T(8,128)(2,1)}, u32[]{:S(2)}, u32[]{:S(2)}) collective-permute-start(bf16[96,16,128]{2,1,0:T(8,128)(2,1)S(1)} %all-to-all-done.refs_0_), channel_id=1, source_target_pairs={{0,96},{96,0},{1,97},{97,1},{2,98},{98,2},{3,99},{99,3},{4,100},{1... | collective-permute-start | bytes 1179656 | tf_op jit(solution)/shard_map/ppermute | solution.py:24
  97.4 15.5 %collective-permute-start.4 = (bf16[96,16,128]{2,1,0:T(8,128)(2,1)S(1)}, bf16[96,16,128]{2,1,0:T(8,128)(2,1)}, u32[]{:S(2)}, u32[]{:S(2)}) collective-permute-start(bf16[96,16,128]{2,1,0:T(8,128)(2,1)S(1)} %collective-permute-done.refs_1_), channel_id=1, source_target_pairs={{0,96},{96,0},{1,97},{97,1},{2,98},{98,2},{3,99},{99,3},{4,100},{1... | collective-permute-start | bytes 1179656 | tf_op jit(solution)/shard_map/ppermute | solution.py:24
  108.5 4.4 %collective-permute-start.5 = (bf16[96,16,128]{2,1,0:T(8,128)(2,1)S(1)}, bf16[96,16,128]{2,1,0:T(8,128)(2,1)}, u32[]{:S(2)}, u32[]{:S(2)}) collective-permute-start(bf16[96,16,128]{2,1,0:T(8,128)(2,1)S(1)} %collective-permute-done.1.refs_2_), channel_id=1, source_target_pairs={{0,96},{96,0},{1,97},{97,1},{2,98},{98,2},{3,99},{99,3},{4,100},{1... | collective-permute-start | bytes 1179656 | tf_op jit(solution)/shard_map/ppermute | solution.py:24
  110.4 4.1 %collective-permute-start.6 = (bf16[96,16,128]{2,1,0:T(8,128)(2,1)}, bf16[96,16,128]{2,1,0:T(8,128)(2,1)}, u32[]{:S(2)}, u32[]{:S(2)}) collective-permute-start(bf16[96,16,128]{2,1,0:T(8,128)(2,1)} %collective-permute-done.2.refs_3_), channel_id=1, source_target_pairs={{0,96},{96,0},{1,97},{97,1},{2,98},{98,2},{3,99},{99,3},{4,100},{1... | collective-permute-start | bytes 1179656 | tf_op jit(solution)/shard_map/ppermute | solution.py:24
  127.0 7.3 %collective-permute-start.11 = (f32[4,128]{1,0:T(4,128)S(1)}, f32[4,128]{1,0:T(4,128)S(1)}, u32[]{:S(2)}, u32[]{:S(2)}) collective-permute-start(f32[4,128]{1,0:T(4,128)S(1)} %get-tuple-element.31), channel_id=1, source_target_pairs={{0,3},{1,0},{2,1},{3,2},{4,7},{5,4},{6,5},{7,6},{8,11},{9,8},{10,9... | collective-permute-start | bytes 6152 | tf_op jit(solution)/shard_map/ppermute | solution.py:28
  129.6 5.8 %collective-permute-start.12 = (f32[4,128]{1,0:T(4,128)S(1)}, f32[4,128]{1,0:T(4,128)S(1)}, u32[]{:S(2)}, u32[]{:S(2)}) collective-permute-start(f32[4,128]{1,0:T(4,128)S(1)} %get-tuple-element.31), channel_id=1, source_target_pairs={{0,2},{1,3},{2,0},{3,1},{4,6},{5,7},{6,4},{7,5},{8,10},{9,11},{10,... | collective-permute-start | bytes 6152 | tf_op jit(solution)/shard_map/ppermute | solution.py:28
  131.8 5.8 %collective-permute-start.13 = (f32[4,128]{1,0:T(4,128)S(1)}, f32[4,128]{1,0:T(4,128)S(1)}, u32[]{:S(2)}, u32[]{:S(2)}) collective-permute-start(f32[4,128]{1,0:T(4,128)S(1)} %get-tuple-element.31), channel_id=1, source_target_pairs={{0,1},{1,2},{2,3},{3,0},{4,5},{5,6},{6,7},{7,4},{8,9},{9,10},{10,1... | collective-permute-start | bytes 6152 | tf_op jit(solution)/shard_map/ppermute | solution.py:28
  137.6 4.5 %collective-permute-start.14 = (f32[4,4,128]{2,1,0:T(4,128)S(1)}, f32[4,4,128]{2,1,0:T(4,128)S(1)}, u32[]{:S(2)}, u32[]{:S(2)}) collective-permute-start(f32[4,4,128]{2,1,0:T(4,128)S(1)} %pad_maximum_fusion.2), channel_id=1, source_target_pairs={{0,96},{96,0},{1,97},{97,1},{2,98},{98,2},{3,99},{99,3},{4,100},{1... | collective-permute-start | bytes 24584 | tf_op jit(solution)/shard_map/ppermute | solution.py:24

commit v2 on v1

--- a/solution.py
+++ b/solution.py
@@ -17,7 +17,7 @@
 PIECE = 1376
 EPS = 1e-05
 ROWS_PAD = 8272
-STEP = 512
+STEP = 1024
 
 
 def swap(a):
@@ -26,6 +26,10 @@
 
 def shift_x(a, k):
     return lax.ppermute(a, "x", [(i, (i + k) % 4) for i in range(4)])
+
+
+def first_row(yh, core):
+    return lax.div(43 * (2 * yh + core), 4)
 
 
 def sums_kernel(pos_ref, hidden_ref, cot_ref, own_ref, send_ref, inv_ref, u_ref):
@@ -51,25 +55,27 @@
         )
         return 0
 
-    lax.fori_loop(0, width // STEP, outer, 0)
+    lax.fori_loop(0, width // STEP, outer, 0, unroll=2)
     u_ref[width:, :] = jnp.zeros((ROWS_PAD - width, LANES), jnp.float32)
 
+    starts = [[GROUP_ROWS * lax.rem(x + k, 4) + first_row(yh, core) for yh in range(4)] for core in (c, 1 - c) for k in range(4)]
+
     def pack(q, _):
-        for k in range(4):
-            base = GROUP_ROWS * (q * 4 + lax.rem(x + k, 4))
-            for yh in range(4):
-                at = (q // 2) * 8 + yh * 2 + lax.rem(q, 2)
-                for out, core in ((own_ref, c), (send_ref, 1 - c)):
-                    row = base + lax.div(43 * (2 * yh + core), 4)
-                    out[k, at] = u_ref[pl.ds(row, BLK), :].astype(jnp.bfloat16)
+        place = (q // 2) * 8 + lax.rem(q, 2)
+        base = 4 * GROUP_ROWS * q
+        for side, out in enumerate((own_ref, send_ref)):
+            for k in range(4):
+                for yh in range(4):
+                    row = base + starts[4 * side + k][yh]
+                    out[k, place + 2 * yh] = u_ref[pl.ds(row, BLK), :].astype(jnp.bfloat16)
         return 0
 
     lax.fori_loop(0, 24, pack, 0)
 
 
 def rows_kernel(pos_ref, hidden_ref, cot_ref, inv_ref, *refs):
-    pieces = (refs[:4], refs[4:8])
-    key_ref, grad_ref, gain_ref, s_ref, w_ref = refs[8:]
+    key_ref, grad_ref, gain_ref, s_ref, w_ref = refs[6:]
+    pieces = (refs[:4], [refs[4]] + [refs[5].at[k] for k in range(3)])
     width = hidden_ref.shape[1]
     x, c = pos_ref[0], pos_ref[1]
 
@@ -77,15 +83,18 @@
     tail = jnp.zeros((22 - BLK, LANES), jnp.float32)
     one = jnp.zeros((1, LANES), jnp.float32)
 
+    offsets = [[first_row(yh, core) for yh in range(4)] for core in (c, 1 - c)]
+    bases = [GROUP_ROWS * lax.rem(x + 4 - k, 4) for k in range(4)]
+
     def assemble(q, _):
+        place = (q // 2) * 8 + lax.rem(q, 2)
         for k in range(4):
-            base = GROUP_ROWS * (q * 4 + lax.rem(x + 4 - k, 4))
-            for core, group in ((c, pieces[0]), (1 - c, pieces[1])):
+            base = 4 * GROUP_ROWS * q + bases[k]
+            for side, core in enumerate((c, 1 - c)):
                 s_ref[core, pl.ds(base + 85, 1), :] = one
                 for yh in range(4):
-                    at = (q // 2) * 8 + yh * 2 + lax.rem(q, 2)
-                    row = base + lax.div(43 * (2 * yh + core), 4)
-                    s_ref[core, pl.ds(row, BLK), :] = group[k][at].astype(jnp.float32)
+                    row = base + offsets[side][yh]
+                    s_ref[core, pl.ds(row, BLK), :] = pieces[side][k][place + 2 * yh].astype(jnp.float32)
                     rest = 6 if yh < 3 else 5
                     s_ref[core, pl.ds(row + BLK, rest), :] = tail[:rest]
         return 0
@@ -105,7 +114,9 @@
             rows.append((part * inv * gain).astype(jnp.bfloat16))
         return key + jnp.dot(jnp.concatenate(rows, axis=1), weight, preferred_element_type=jnp.float32)
 
-    key = lax.fori_loop(0, width // STEP, forward, jnp.zeros(key_ref.shape, jnp.float32))
+    key = lax.fori_loop(
+        0, width // STEP, forward, jnp.zeros(key_ref.shape, jnp.float32), unroll=2
+    )
     key_ref[...] = key.astype(jnp.bfloat16)
     cot = cot_ref[...]
     scale = inv * (jnp.sum(cot.astype(jnp.float32) * key, axis=1, keepdims=True) / width)
@@ -123,7 +134,7 @@
             grad_ref[:, lanes] = grad.astype(jnp.bfloat16)
         return 0
 
-    lax.fori_loop(0, width // STEP, backward, 0)
+    lax.fori_loop(0, width // STEP, backward, 0, unroll=2)
 
 
 def local(hidden_in, cotangent, params):
@@ -131,7 +142,7 @@
     x, c, z = lax.axis_index("x"), lax.axis_index("c"), lax.axis_index("z")
     yh, yl = lax.axis_index("yh"), lax.axis_index("yl")
     inner, j = (z * 2 + yl) * 4 + x, yh * 2 + c
-    first_row, lane = (43 * j) // 4, (96 * j) % LANES
+    row0, lane = first_row(yh, c), (96 * j) % LANES
     pos = jnp.stack([x, c]).astype(jnp.int32)
     smem = pl.BlockSpec(memory_space=pltpu.SMEM)
     vmem = pl.BlockSpec(memory_space=pltpu.VMEM)
@@ -151,12 +162,13 @@
         compiler_params=pltpu.CompilerParams(vmem_limit_bytes=24 << 20),
         cost_estimate=pl.CostEstimate(flops=4 * tokens * width * LANES, bytes_accessed=8 << 20, transcendentals=0),
     )(pos, hidden_in, cotangent)
+    send, mine = lax.optimization_barrier((send, mine))
     got = swap(send)
     pair = [own[k].astype(f32) + got[k].astype(f32) for k in range(4)]
     moved = [shift_x(pair[k].astype(bf16), k) for k in range(1, 4)]
 
     held = [mine] + [shift_x(mine, k) for k in range(1, 4)]
-    other = [swap(a) for a in held]
+    other = [swap(mine), swap(jnp.stack(held[1:]))]
 
     total = pair[0] + moved[0].astype(f32) + moved[1].astype(f32) + moved[2].astype(f32)
     gain_part = jnp.sum(mine.astype(f32) * total, axis=-1)[:, :USED].reshape(12, 8 * USED)
@@ -177,7 +189,7 @@
             jax.ShapeDtypeStruct((tokens, width), bf16),
             jax.ShapeDtypeStruct((64, LANES), f32),
         ),
-        in_specs=[smem] + [vmem] * 11,
+        in_specs=[smem] + [vmem] * 9,
         out_specs=(vmem, vmem, vmem),
         scratch_shapes=[pltpu.VMEM((2, ROWS_PAD, LANES), f32), pltpu.VMEM((width, LANES), bf16)],
         compiler_params=pltpu.CompilerParams(vmem_limit_bytes=36 << 20),
@@ -185,10 +197,8 @@
     )(pos, hidden_in, cotangent, inv, *held, *other)
 
     part = sums[USED:]
-    parts = jnp.stack([shift_x(part, 3), shift_x(part, 2), shift_x(part, 1), part])
-    theirs = swap(parts)
-    both = jnp.stack([jnp.where(c == 0, parts, theirs), jnp.where(c == 0, theirs, parts)])
-    both = both.reshape(2, 4, 512)[:, :, :480].reshape(2, 4, 5, 4, 2, USED)
+    parts = lax.all_to_all(jnp.broadcast_to(part, (8, 4, LANES)), ("c", "x"), 0, 0, tiled=True)
+    both = parts.reshape(2, 4, 512)[:, :, :480].reshape(2, 4, 5, 4, 2, USED)
     by_row = 0.0
     for core in range(2):
         for hi in range(4):
@@ -198,7 +208,7 @@
     start = jnp.where(yh == 2, 3, jnp.where(yh == 3, 7, 0)) * 688
     gain_grad = lax.dynamic_slice(jnp.pad(by_row, (2816, 0)), (PIECE * j - start,), (PIECE,))
 
-    row_gain = lax.dynamic_slice(jnp.pad(gains.reshape(-1), (0, 80)), (GROUP_ROWS * inner + first_row,), (USED,))
+    row_gain = lax.dynamic_slice(jnp.pad(gains.reshape(-1), (0, 80)), (GROUP_ROWS * inner + row0,), (USED,))
     weight_grad = (sums[:USED] * row_gain[:, None]).reshape(-1)
     weight_grad = lax.dynamic_slice(weight_grad, (lane,), (PIECE,))
     param_grad = weight_grad + jnp.where(inner == 95, gain_grad, 0.0)

time: 144 us -> 142 us (0.986)
  waiting for transfers between devices: 20.9 us -> 45.6 us
  starting transfers between devices: 90.3 us -> 68.6 us
  Pallas kernels: 18.4 us -> 11 us
  local copies, waits for them, and re-layouts: 4.78 us -> 7.89 us
    ppermute x6 -> x3, starting transfers between devices: 36.1 us -> 12.1 us  [swap(): return lax.ppermute(a, 'c', [(0, 1), (1, 0)])]
    all_to_all x1, starting transfers between devices: 12.7 us -> 22.5 us  [local(): lax.all_to_all(jnp.broadcast_to(block, (N_ZY, BLK, LANES)), ZY, 0, 0, til...]
    ppermute x9 -> x6, waiting for transfers between devices: 8.7 us -> 17.1 us  [shift_x(): return lax.ppermute(a, 'x', [(i, (i + k) % 4) for i in range(4)])]
    all_to_all x1, starting transfers between devices: 15.1 us -> 6.92 us  [local(): sums = lax.all_to_all(chunk, ZY, 0, 0, tiled=True).astype(f32).sum(axis=0)]
    all_to_all x0 -> x1, starting transfers between devices: none -> 8.1 us  [local(): lax.all_to_all(jnp.broadcast_to(part, (8, 4, LANES)), ('c', 'x'), 0, 0, t...]
    all_to_all x1, waiting for transfers between devices: 0.01 us -> 7.8 us  [local(): sums = lax.all_to_all(chunk, ZY, 0, 0, tiled=True).astype(f32).sum(axis=0)]
    ppermute x9 -> x6, starting transfers between devices: 26.5 us -> 19 us  [shift_x(): return lax.ppermute(a, 'x', [(i, (i + k) % 4) for i in range(4)])]
    all_to_all x0 -> x1, waiting for transfers between devices: none -> 4.83 us  [local(): lax.all_to_all(jnp.broadcast_to(part, (8, 4, LANES)), ('c', 'x'), 0, 0, t...]
  transfers between devices with their start and end apart: 17 -> 12, of which waited for: 7 -> 9; matrix products, arithmetic and copies ran while one was open for 2% -> 4% of each run, Pallas kernels for 8% -> 8%
where the time goes in v2:
time: 142 us; the launch traced here: 141 us
  starting transfers between devices  68.6 us (48%)
  waiting for transfers between devices  45.6 us (32%)
  Pallas kernels  11 us (8%)
  local copies, waits for them, and re-layouts  7.89 us (6%)
  other arithmetic  6.88 us (5%)
    all_to_all x1, starting transfers between devices, local(): lax.all_to_all(jnp.broadcast_to(block, (N_ZY, BLK, LANES)), ZY, 0, 0, til...  22.5 us
    ppermute x6, starting transfers between devices, shift_x(): return lax.ppermute(a, 'x', [(i, (i + k) % 4) for i in range(4)])  19 us
    ppermute x6, waiting for transfers between devices, shift_x(): return lax.ppermute(a, 'x', [(i, (i + k) % 4) for i in range(4)])  17.1 us
    all_to_all x1, waiting for transfers between devices, local(): lax.all_to_all(jnp.broadcast_to(block, (N_ZY, BLK, LANES)), ZY, 0, 0, til...  14.5 us
    ppermute x3, starting transfers between devices, swap(): return lax.ppermute(a, 'c', [(0, 1), (1, 0)])  12.1 us
    all_to_all x1, starting transfers between devices, local(): lax.all_to_all(jnp.broadcast_to(part, (8, 4, LANES)), ('c', 'x'), 0, 0, t...  8.1 us
    all_to_all x1, waiting for transfers between devices, local(): sums = lax.all_to_all(chunk, ZY, 0, 0, tiled=True).astype(f32).sum(axis=0)  7.8 us
    pallas_call x1, Pallas kernels, local(): pl.pallas_call(rows_kernel, out_shape=(jax.ShapeDtypeStruct((tokens, LANE...  7.57 us
  transfers between devices with their start and end apart: 12, of which 9 were waited for; matrix products, arithmetic and copies ran while one was open for 4% of the time, Pallas kernels for 8%

profile of v2, /device:TPU:1, one launch (start us, length us, event | category | flops | bytes accessed | tf_op | source)
XLA Modules:
  0.0 140.9 jit_solution(17936880853900120697)
XLA Ops:
  0.7 0.7 reduce
  1.4 0.1 fusion.9
  1.5 0.8 broadcast_in_dim.25
  2.3 22.5 %all-to-all-start = ((bf16[96,16,128]{2,1,0:T(8,128)(2,1)}), bf16[96,16,128]{2,1,0:T(8,128)(2,1)S(1)}, u32[]{:S(2)}, u32[]{:S(2)}) async-start(bf16[96,16,128]{2,1,0:T(8,128)(2,1)} %broadcast_in_dim.25), calls=%async_computation | async-start | bytes 786432 | tf_op jit(solution)/shard_map/all_to_all | solution.py:153
  24.9 0.1 pad_add_fusion.6.pos_ref
  25.0 1.6 %copy-done = bf16[128,8192]{1,0:T(8,128)(2,1)S(1)} copy-done((bf16[128,8192]{1,0:T(8,128)(2,1)S(1)}, bf16[128,8192]{1,0:T(8,128)(2,1)}, u32[]{:S(2)}) %copy-start) | copy-done | bytes 2097176
  26.5 0.8 copy-done.5
  27.3 3.4 %shard_map.58 = (bf16[4,96,16,128]{3,2,1,0:T(8,128)(2,1)S(1)}, bf16[4,96,16,128]{3,2,1,0:T(8,128)(2,1)S(1)}, f32[128,128]{1,0:T(8,128)S(1)}) custom-call(s32[2]{0:T(128)S(1)} %pad_add_fusion.6.pos_ref, bf16[128,8192]{1,0:T(8,128)(2,1)S(1)} %copy-done, bf16[128,128]{1,0:T(8,128)(2,1)S(1)} %copy-done.5), custom_call_target="tpu_custom_call" | custom-call | flops 536870912 | bytes 8388608 | tf_op jit(solution)/shard_map/pallas_call | solution.py:156
  30.7 1.1 copy-done.7
  31.8 14.5 %all-to-all-done.refs_0_ = bf16[96,16,128]{2,1,0:T(8,128)(2,1)S(1)} async-done(((bf16[96,16,128]{2,1,0:T(8,128)(2,1)}), bf16[96,16,128]{2,1,0:T(8,128)(2,1)S(1)}, u32[]{:S(2)}, u32[]{:S(2)}) %all-to-all-start) | async-done | bytes 393248 | tf_op jit(solution)/shard_map/all_to_all | solution.py:153
  46.3 5.3 %collective-permute-start.5 = (bf16[4,96,16,128]{3,2,1,0:T(8,128)(2,1)}, bf16[4,96,16,128]{3,2,1,0:T(8,128)(2,1)S(1)}, u32[]{:S(2)}, u32[]{:S(2)}) collective-permute-start(bf16[4,96,16,128]{3,2,1,0:T(8,128)(2,1)} %copy-done.7), channel_id=1, source_target_pairs={{0,96},{96,0},{1,97},{97,1},{2,98},{98,2},{3,99},{99,3},{4,100},{1... | collective-permute-start | bytes 4718600 | tf_op jit(solution)/shard_map/ppermute | solution.py:24
  51.6 3.1 %collective-permute-start = (bf16[96,16,128]{2,1,0:T(8,128)(2,1)S(1)}, bf16[96,16,128]{2,1,0:T(8,128)(2,1)S(1)}, u32[]{:S(2)}, u32[]{:S(2)}) collective-permute-start(bf16[96,16,128]{2,1,0:T(8,128)(2,1)S(1)} %all-to-all-done.refs_0_), channel_id=1, source_target_pairs={{0,1},{1,2},{2,3},{3,0},{4,5},{5,6},{6,7},{7,4},{8,9},{9,10},{10,1... | collective-permute-start | bytes 1179656 | tf_op jit(solution)/shard_map/ppermute | solution.py:28
  54.8 4.4 %collective-permute-start.1 = (bf16[96,16,128]{2,1,0:T(8,128)(2,1)S(1)}, bf16[96,16,128]{2,1,0:T(8,128)(2,1)S(1)}, u32[]{:S(2)}, u32[]{:S(2)}) collective-permute-start(bf16[96,16,128]{2,1,0:T(8,128)(2,1)S(1)} %all-to-all-done.refs_0_), channel_id=1, source_target_pairs={{0,2},{1,3},{2,0},{3,1},{4,6},{5,7},{6,4},{7,5},{8,10},{9,11},{10,... | collective-permute-start | bytes 1179656 | tf_op jit(solution)/shard_map/ppermute | solution.py:28
  59.1 3.1 %collective-permute-start.2 = (bf16[96,16,128]{2,1,0:T(8,128)(2,1)S(1)}, bf16[96,16,128]{2,1,0:T(8,128)(2,1)S(1)}, u32[]{:S(2)}, u32[]{:S(2)}) collective-permute-start(bf16[96,16,128]{2,1,0:T(8,128)(2,1)S(1)} %all-to-all-done.refs_0_), channel_id=1, source_target_pairs={{0,3},{1,0},{2,1},{3,2},{4,7},{5,4},{6,5},{7,6},{8,11},{9,8},{10,9... | collective-permute-start | bytes 1179656 | tf_op jit(solution)/shard_map/ppermute | solution.py:28
  62.2 0.3 fusion.2
  62.5 2.2 %collective-permute-start.6 = (bf16[96,16,128]{2,1,0:T(8,128)(2,1)S(1)}, bf16[96,16,128]{2,1,0:T(8,128)(2,1)S(1)}, u32[]{:S(2)}, u32[]{:S(2)}) collective-permute-start(bf16[96,16,128]{2,1,0:T(8,128)(2,1)S(1)} %get-tuple-element.19), channel_id=1, source_target_pairs={{0,1},{1,2},{2,3},{3,0},{4,5},{5,6},{6,7},{7,4},{8,9},{9,10},{10,1... | collective-permute-start | bytes 1179656 | tf_op jit(solution)/shard_map/ppermute | solution.py:28
  64.8 2.8 %collective-permute-start.7 = (bf16[96,16,128]{2,1,0:T(8,128)(2,1)S(1)}, bf16[96,16,128]{2,1,0:T(8,128)(2,1)S(1)}, u32[]{:S(2)}, u32[]{:S(2)}) collective-permute-start(bf16[96,16,128]{2,1,0:T(8,128)(2,1)S(1)} %get-tuple-element.21), channel_id=1, source_target_pairs={{0,2},{1,3},{2,0},{3,1},{4,6},{5,7},{6,4},{7,5},{8,10},{9,11},{10,... | collective-permute-start | bytes 1179656 | tf_op jit(solution)/shard_map/ppermute | solution.py:28
  67.6 3.4 %collective-permute-start.8 = (bf16[96,16,128]{2,1,0:T(8,128)(2,1)S(1)}, bf16[96,16,128]{2,1,0:T(8,128)(2,1)S(1)}, u32[]{:S(2)}, u32[]{:S(2)}) collective-permute-start(bf16[96,16,128]{2,1,0:T(8,128)(2,1)S(1)} %get-tuple-element.20), channel_id=1, source_target_pairs={{0,3},{1,0},{2,1},{3,2},{4,7},{5,4},{6,5},{7,6},{8,11},{9,8},{10,9... | collective-permute-start | bytes 1179656 | tf_op jit(solution)/shard_map/ppermute | solution.py:28
  71.0 3.9 %collective-permute-done.1.refs_2_ = bf16[96,16,128]{2,1,0:T(8,128)(2,1)S(1)} collective-permute-done((bf16[96,16,128]{2,1,0:T(8,128)(2,1)S(1)}, bf16[96,16,128]{2,1,0:T(8,128)(2,1)S(1)}, u32[]{:S(2)}, u32[]{:S(2)}) %collective-permute-start.1) | collective-permute-done | bytes 393248 | tf_op jit(solution)/shard_map/ppermute | solution.py:28
  74.9 1.2 collective-permute-done.2.refs_3_
  76.1 1.2 pad_maximum_fusion
  77.3 3.7 %collective-permute-start.4 = (bf16[3,96,16,128]{3,2,1,0:T(8,128)(2,1)}, bf16[3,96,16,128]{3,2,1,0:T(8,128)(2,1)}, u32[]{:S(2)}, u32[]{:S(2)}) collective-permute-start(bf16[3,96,16,128]{3,2,1,0:T(8,128)(2,1)} %pad_maximum_fusion), channel_id=1, source_target_pairs={{0,96},{96,0},{1,97},{97,1},{2,98},{98,2},{3,99},{99,3},{4,100},{1... | collective-permute-start | bytes 3538952 | tf_op jit(solution)/shard_map/ppermute | solution.py:24
  81.0 2.9 %collective-permute-done.6 = bf16[96,16,128]{2,1,0:T(8,128)(2,1)S(1)} collective-permute-done((bf16[96,16,128]{2,1,0:T(8,128)(2,1)S(1)}, bf16[96,16,128]{2,1,0:T(8,128)(2,1)S(1)}, u32[]{:S(2)}, u32[]{:S(2)}) %collective-permute-start.6) | collective-permute-done | bytes 393248 | tf_op jit(solution)/shard_map/ppermute | solution.py:28
  83.9 7.9 %collective-permute-done.7 = bf16[96,16,128]{2,1,0:T(8,128)(2,1)S(1)} collective-permute-done((bf16[96,16,128]{2,1,0:T(8,128)(2,1)S(1)}, bf16[96,16,128]{2,1,0:T(8,128)(2,1)S(1)}, u32[]{:S(2)}, u32[]{:S(2)}) %collective-permute-start.7) | collective-permute-done | bytes 393248 | tf_op jit(solution)/shard_map/ppermute | solution.py:28
  91.8 1.2 collective-permute-done.8
  93.0 0.4 multiply_reduce_fusion
  93.4 0.3 copy-done.11
  93.8 0.1 reshape.79
  93.9 0.1 reshape.80
  94.0 0.1 reshape.78
  94.2 0.1 pad_maximum_fusion.1
  94.3 2.7 %select_convert_fusion = bf16[96,16,128]{2,1,0:T(8,128)(2,1)} fusion(bf16[8,4,128]{2,1,0:T(4,128)(2,1)S(1)} %bitcast.72, pred[16]{0:T(512)(128)(4,1)S(1)} %iota_compare_fusion, bf16[96,16,128]{2,1,0:T(8,128)(2,1)} %copy-done.11, bf16[96,16,128]{2,1,0:T(8,128)(2,1)} %copy-done.10, bf16[96,16,128]{2,1,0:T(8,128)(2,1)} %copy-done.9, ...), kind=kLoop, calls=%fused_computation.5 | loop fusion | flops 1966080 | bytes 2367504 | tf_op jit(solution)/shard_map/convert_element_type | solution.py:182
  96.9 6.9 %all-to-all-start.1 = ((bf16[96,16,128]{2,1,0:T(8,128)(2,1)}), bf16[96,16,128]{2,1,0:T(8,128)(2,1)}, u32[]{:S(2)}, u32[]{:S(2)}) async-start(bf16[96,16,128]{2,1,0:T(8,128)(2,1)} %select_convert_fusion), calls=%async_computation.1 | async-start | bytes 786432 | tf_op jit(solution)/shard_map/all_to_all | solution.py:183
  103.9 3.0 %collective-permute-start.3 = (bf16[96,16,128]{2,1,0:T(8,128)(2,1)S(1)}, bf16[96,16,128]{2,1,0:T(8,128)(2,1)}, u32[]{:S(2)}, u32[]{:S(2)}) collective-permute-start(bf16[96,16,128]{2,1,0:T(8,128)(2,1)S(1)} %all-to-all-done.refs_0_), channel_id=1, source_target_pairs={{0,96},{96,0},{1,97},{97,1},{2,98},{98,2},{3,99},{99,3},{4,100},{1... | collective-permute-start | bytes 1179656 | tf_op jit(solution)/shard_map/ppermute | solution.py:24
  106.9 1.4 collective-permute-done.3.refs_4_
  108.4 1.0 copy-done.4
  109.4 7.6 %shard_map.59 = (bf16[128,128]{1,0:T(8,128)(2,1)}, bf16[128,8192]{1,0:T(8,128)(2,1)}, f32[64,128]{1,0:T(8,128)S(1)}) custom-call(s32[2]{0:T(128)S(1)} %pad_add_fusion.6.pos_ref, bf16[128,8192]{1,0:T(8,128)(2,1)S(1)} %copy-done.1, bf16[128,128]{1,0:T(8,128)(2,1)S(1)} %copy-done.6, f32[128,128]{1,0:T(8,128)S(1)} %get-tuple-element.11.inv_ref, ...), custom_call_target="tpu_custom_call" | custom-call | flops 536870912 | bytes 10485760 | tf_op jit(solution)/shard_map/pallas_call | solution.py:185
  116.9 0.1 pad_dynamic-slice_fusion
  117.0 7.8 %all-to-all-done.1 = bf16[96,16,128]{2,1,0:T(8,128)(2,1)} async-done(((bf16[96,16,128]{2,1,0:T(8,128)(2,1)}), bf16[96,16,128]{2,1,0:T(8,128)(2,1)}, u32[]{:S(2)}, u32[]{:S(2)}) %all-to-all-start.1) | async-done | bytes 393248 | tf_op jit(solution)/shard_map/all_to_all | solution.py:183
  124.8 1.1 convert_reduce_fusion
  125.9 0.6 broadcast_in_dim.27
  126.5 8.1 %all-to-all-start.2 = ((f32[8,4,128]{2,1,0:T(4,128)}), f32[8,4,128]{2,1,0:T(4,128)S(1)}, u32[]{:S(2)}, u32[]{:S(2)}) async-start(f32[8,4,128]{2,1,0:T(4,128)} %broadcast_in_dim.27), calls=%async_computation.2 | async-start | bytes 32768 | tf_op jit(solution)/shard_map/all_to_all | solution.py:200
  134.7 4.8 %all-to-all-done.2 = f32[8,4,128]{2,1,0:T(4,128)S(1)} async-done(((f32[8,4,128]{2,1,0:T(4,128)}), f32[8,4,128]{2,1,0:T(4,128)S(1)}, u32[]{:S(2)}, u32[]{:S(2)}) %all-to-all-start.2) | async-done | bytes 16416 | tf_op jit(solution)/shard_map/all_to_all | solution.py:200
  139.5 0.2 reshape.85
  139.9 0.2 fusion.5
  140.1 0.1 reshape.86
  140.2 0.1 fusion.7
  140.3 0.6 reshape.87
  (33 shorter events, 0.3 us)
Async XLA Ops:
  2.3 44.0 %all-to-all-start = ((bf16[96,16,128]{2,1,0:T(8,128)(2,1)}), bf16[96,16,128]{2,1,0:T(8,128)(2,1)S(1)}, u32[]{:S(2)}, u32[]{:S(2)}) async-start(bf16[96,16,128]{2,1,0:T(8,128)(2,1)} %broadcast_in_dim.25), calls=%async_computation | async-start | bytes 786432 | tf_op jit(solution)/shard_map/all_to_all | solution.py:153
  25.0 1.6 %copy-start = (bf16[128,8192]{1,0:T(8,128)(2,1)S(1)}, bf16[128,8192]{1,0:T(8,128)(2,1)}, u32[]{:S(2)}) copy-start(bf16[128,8192]{1,0:T(8,128)(2,1)} %hidden_ref.3) | copy-start | bytes 6291460
  26.5 0.8 copy-start.5
  30.7 1.1 copy-start.7
  31.8 61.2 %copy-start.2 = (bf16[4,96,16,128]{3,2,1,0:T(8,128)(2,1)}, bf16[4,96,16,128]{3,2,1,0:T(8,128)(2,1)S(1)}, u32[]{:S(2)}) copy-start(bf16[4,96,16,128]{3,2,1,0:T(8,128)(2,1)S(1)} %get-tuple-element.16) | copy-start | bytes 4718596
  46.3 15.9 %collective-permute-start.5 = (bf16[4,96,16,128]{3,2,1,0:T(8,128)(2,1)}, bf16[4,96,16,128]{3,2,1,0:T(8,128)(2,1)S(1)}, u32[]{:S(2)}, u32[]{:S(2)}) collective-permute-start(bf16[4,96,16,128]{3,2,1,0:T(8,128)(2,1)} %copy-done.7), channel_id=1, source_target_pairs={{0,96},{96,0},{1,97},{97,1},{2,98},{98,2},{3,99},{99,3},{4,100},{1... | collective-permute-start | bytes 4718600 | tf_op jit(solution)/shard_map/ppermute | solution.py:24
  51.6 15.9 %collective-permute-start = (bf16[96,16,128]{2,1,0:T(8,128)(2,1)S(1)}, bf16[96,16,128]{2,1,0:T(8,128)(2,1)S(1)}, u32[]{:S(2)}, u32[]{:S(2)}) collective-permute-start(bf16[96,16,128]{2,1,0:T(8,128)(2,1)S(1)} %all-to-all-done.refs_0_), channel_id=1, source_target_pairs={{0,1},{1,2},{2,3},{3,0},{4,5},{5,6},{6,7},{7,4},{8,9},{9,10},{10,1... | collective-permute-start | bytes 1179656 | tf_op jit(solution)/shard_map/ppermute | solution.py:28
  54.8 20.2 %collective-permute-start.1 = (bf16[96,16,128]{2,1,0:T(8,128)(2,1)S(1)}, bf16[96,16,128]{2,1,0:T(8,128)(2,1)S(1)}, u32[]{:S(2)}, u32[]{:S(2)}) collective-permute-start(bf16[96,16,128]{2,1,0:T(8,128)(2,1)S(1)} %all-to-all-done.refs_0_), channel_id=1, source_target_pairs={{0,2},{1,3},{2,0},{3,1},{4,6},{5,7},{6,4},{7,5},{8,10},{9,11},{10,... | collective-permute-start | bytes 1179656 | tf_op jit(solution)/shard_map/ppermute | solution.py:28
  59.1 17.0 %collective-permute-start.2 = (bf16[96,16,128]{2,1,0:T(8,128)(2,1)S(1)}, bf16[96,16,128]{2,1,0:T(8,128)(2,1)S(1)}, u32[]{:S(2)}, u32[]{:S(2)}) collective-permute-start(bf16[96,16,128]{2,1,0:T(8,128)(2,1)S(1)} %all-to-all-done.refs_0_), channel_id=1, source_target_pairs={{0,3},{1,0},{2,1},{3,2},{4,7},{5,4},{6,5},{7,6},{8,11},{9,8},{10,9... | collective-permute-start | bytes 1179656 | tf_op jit(solution)/shard_map/ppermute | solution.py:28
  62.2 30.8 %copy-start.8 = (bf16[4,96,16,128]{3,2,1,0:T(8,128)(2,1)}, bf16[4,96,16,128]{3,2,1,0:T(8,128)(2,1)S(1)}, u32[]{:S(2)}) copy-start(bf16[4,96,16,128]{3,2,1,0:T(8,128)(2,1)S(1)} %collective-permute-done.5) | copy-start | bytes 4718596
  62.5 21.3 %collective-permute-start.6 = (bf16[96,16,128]{2,1,0:T(8,128)(2,1)S(1)}, bf16[96,16,128]{2,1,0:T(8,128)(2,1)S(1)}, u32[]{:S(2)}, u32[]{:S(2)}) collective-permute-start(bf16[96,16,128]{2,1,0:T(8,128)(2,1)S(1)} %get-tuple-element.19), channel_id=1, source_target_pairs={{0,1},{1,2},{2,3},{3,0},{4,5},{5,6},{6,7},{7,4},{8,9},{9,10},{10,1... | collective-permute-start | bytes 1179656 | tf_op jit(solution)/shard_map/ppermute | solution.py:28
  64.8 27.0 %collective-permute-start.7 = (bf16[96,16,128]{2,1,0:T(8,128)(2,1)S(1)}, bf16[96,16,128]{2,1,0:T(8,128)(2,1)S(1)}, u32[]{:S(2)}, u32[]{:S(2)}) collective-permute-start(bf16[96,16,128]{2,1,0:T(8,128)(2,1)S(1)} %get-tuple-element.21), channel_id=1, source_target_pairs={{0,2},{1,3},{2,0},{3,1},{4,6},{5,7},{6,4},{7,5},{8,10},{9,11},{10,... | collective-permute-start | bytes 1179656 | tf_op jit(solution)/shard_map/ppermute | solution.py:28
  67.6 25.4 %collective-permute-start.8 = (bf16[96,16,128]{2,1,0:T(8,128)(2,1)S(1)}, bf16[96,16,128]{2,1,0:T(8,128)(2,1)S(1)}, u32[]{:S(2)}, u32[]{:S(2)}) collective-permute-start(bf16[96,16,128]{2,1,0:T(8,128)(2,1)S(1)} %get-tuple-element.20), channel_id=1, source_target_pairs={{0,3},{1,0},{2,1},{3,2},{4,7},{5,4},{6,5},{7,6},{8,11},{9,8},{10,9... | collective-permute-start | bytes 1179656 | tf_op jit(solution)/shard_map/ppermute | solution.py:28
  76.1 17.3 %copy-start.3 = (bf16[96,16,128]{2,1,0:T(8,128)(2,1)}, bf16[96,16,128]{2,1,0:T(8,128)(2,1)S(1)}, u32[]{:S(2)}) copy-start(bf16[96,16,128]{2,1,0:T(8,128)(2,1)S(1)} %collective-permute-done.2.refs_3_) | copy-start | bytes 1179652
  77.3 31.1 %collective-permute-start.4 = (bf16[3,96,16,128]{3,2,1,0:T(8,128)(2,1)}, bf16[3,96,16,128]{3,2,1,0:T(8,128)(2,1)}, u32[]{:S(2)}, u32[]{:S(2)}) collective-permute-start(bf16[3,96,16,128]{3,2,1,0:T(8,128)(2,1)} %pad_maximum_fusion), channel_id=1, source_target_pairs={{0,96},{96,0},{1,97},{97,1},{2,98},{98,2},{3,99},{99,3},{4,100},{1... | collective-permute-start | bytes 3538952 | tf_op jit(solution)/shard_map/ppermute | solution.py:24
  83.9 9.6 %copy-start.9 = (bf16[96,16,128]{2,1,0:T(8,128)(2,1)}, bf16[96,16,128]{2,1,0:T(8,128)(2,1)S(1)}, u32[]{:S(2)}) copy-start(bf16[96,16,128]{2,1,0:T(8,128)(2,1)S(1)} %collective-permute-done.6) | copy-start | bytes 1179652
  91.8 1.7 %copy-start.10 = (bf16[96,16,128]{2,1,0:T(8,128)(2,1)}, bf16[96,16,128]{2,1,0:T(8,128)(2,1)S(1)}, u32[]{:S(2)}) copy-start(bf16[96,16,128]{2,1,0:T(8,128)(2,1)S(1)} %collective-permute-done.7) | copy-start | bytes 1179652
  93.0 0.8 copy-start.11
  94.2 14.1 %copy-start.1 = (bf16[128,8192]{1,0:T(8,128)(2,1)S(1)}, bf16[128,8192]{1,0:T(8,128)(2,1)}, u32[]{:S(2)}) copy-start(bf16[128,8192]{1,0:T(8,128)(2,1)} %hidden_ref.3) | copy-start | bytes 6291460
  94.3 14.1 %copy-start.6 = (bf16[128,128]{1,0:T(8,128)(2,1)S(1)}, bf16[128,128]{1,0:T(8,128)(2,1)}, u32[]{:S(2)}) copy-start(bf16[128,128]{1,0:T(8,128)(2,1)} %cot_ref.3) | copy-start | bytes 98308
  96.9 27.9 %all-to-all-start.1 = ((bf16[96,16,128]{2,1,0:T(8,128)(2,1)}), bf16[96,16,128]{2,1,0:T(8,128)(2,1)}, u32[]{:S(2)}, u32[]{:S(2)}) async-start(bf16[96,16,128]{2,1,0:T(8,128)(2,1)} %select_convert_fusion), calls=%async_computation.1 | async-start | bytes 786432 | tf_op jit(solution)/shard_map/all_to_all | solution.py:183
  103.9 4.5 %collective-permute-start.3 = (bf16[96,16,128]{2,1,0:T(8,128)(2,1)S(1)}, bf16[96,16,128]{2,1,0:T(8,128)(2,1)}, u32[]{:S(2)}, u32[]{:S(2)}) collective-permute-start(bf16[96,16,128]{2,1,0:T(8,128)(2,1)S(1)} %all-to-all-done.refs_0_), channel_id=1, source_target_pairs={{0,96},{96,0},{1,97},{97,1},{2,98},{98,2},{3,99},{99,3},{4,100},{1... | collective-permute-start | bytes 1179656 | tf_op jit(solution)/shard_map/ppermute | solution.py:24
  108.4 1.0 copy-start.4
  126.5 13.0 %all-to-all-start.2 = ((f32[8,4,128]{2,1,0:T(4,128)}), f32[8,4,128]{2,1,0:T(4,128)S(1)}, u32[]{:S(2)}, u32[]{:S(2)}) async-start(f32[8,4,128]{2,1,0:T(4,128)} %broadcast_in_dim.27), calls=%async_computation.2 | async-start | bytes 32768 | tf_op jit(solution)/shard_map/all_to_all | solution.py:200

commit v3 on v2

--- a/solution.py
+++ b/solution.py
@@ -162,10 +162,10 @@
         compiler_params=pltpu.CompilerParams(vmem_limit_bytes=24 << 20),
         cost_estimate=pl.CostEstimate(flops=4 * tokens * width * LANES, bytes_accessed=8 << 20, transcendentals=0),
     )(pos, hidden_in, cotangent)
-    send, mine = lax.optimization_barrier((send, mine))
     got = swap(send)
     pair = [own[k].astype(f32) + got[k].astype(f32) for k in range(4)]
     moved = [shift_x(pair[k].astype(bf16), k) for k in range(1, 4)]
+    moved, mine = lax.optimization_barrier((moved, mine))
 
     held = [mine] + [shift_x(mine, k) for k in range(1, 4)]
     other = [swap(mine), swap(jnp.stack(held[1:]))]
@@ -196,7 +196,7 @@
         cost_estimate=pl.CostEstimate(flops=4 * tokens * width * LANES, bytes_accessed=10 << 20, transcendentals=0),
     )(pos, hidden_in, cotangent, inv, *held, *other)
 
-    part = sums[USED:]
+    part, gains = lax.optimization_barrier((sums[USED:], gains))
     parts = lax.all_to_all(jnp.broadcast_to(part, (8, 4, LANES)), ("c", "x"), 0, 0, tiled=True)
     both = parts.reshape(2, 4, 512)[:, :, :480].reshape(2, 4, 5, 4, 2, USED)
     by_row = 0.0

time: 142 us -> 138 us (0.972)
  waiting for transfers between devices: 45.6 us -> 34.7 us
  other arithmetic: 6.88 us -> 10.3 us
  starting transfers between devices: 68.6 us -> 71.7 us
    ppermute x6, waiting for transfers between devices: 17.1 us -> 6.84 us  [shift_x(): return lax.ppermute(a, 'x', [(i, (i + k) % 4) for i in range(4)])]
    all_to_all x1, starting transfers between devices: 22.5 us -> 12.7 us  [local(): lax.all_to_all(jnp.broadcast_to(block, (N_ZY, BLK, LANES)), ZY, 0, 0, til...]
    all_to_all x1, starting transfers between devices: 6.92 us -> 15.4 us  [local(): sums = lax.all_to_all(chunk, ZY, 0, 0, tiled=True).astype(f32).sum(axis=0)]
    ppermute x3, starting transfers between devices: 12.1 us -> 17.7 us  [swap(): return lax.ppermute(a, 'c', [(0, 1), (1, 0)])]
    all_to_all x1, waiting for transfers between devices: 7.8 us -> 12.6 us  [local(): sums = lax.all_to_all(chunk, ZY, 0, 0, tiled=True).astype(f32).sum(axis=0)]
    all_to_all x1, waiting for transfers between devices: 14.5 us -> 10.5 us  [local(): lax.all_to_all(jnp.broadcast_to(block, (N_ZY, BLK, LANES)), ZY, 0, 0, til...]
    ppermute x6, starting transfers between devices: 19 us -> 16.5 us  [shift_x(): return lax.ppermute(a, 'x', [(i, (i + k) % 4) for i in range(4)])]
    convert_element_type x1, other arithmetic: 0.31 us -> 2.43 us  [local(): moved = [shift_x(pair[k].astype(bf16), k) for k in range(1, 4)]]
  transfers between devices with their start and end apart: 12 -> 12, of which waited for: 9 -> 5; matrix products, arithmetic and copies ran while one was open for 4% -> 8% of each run, Pallas kernels for 8% -> 0%
where the time goes in v3:
time: 138 us; the launch traced here: 137 us
  starting transfers between devices  71.7 us (52%)
  waiting for transfers between devices  34.7 us (25%)
  Pallas kernels  12.2 us (9%)
  other arithmetic  10.3 us (7%)
  local copies, waits for them, and re-layouts  6.88 us (5%)
    ppermute x3, starting transfers between devices, swap(): return lax.ppermute(a, 'c', [(0, 1), (1, 0)])  17.7 us
    ppermute x6, starting transfers between devices, shift_x(): return lax.ppermute(a, 'x', [(i, (i + k) % 4) for i in range(4)])  16.5 us
    all_to_all x1, starting transfers between devices, local(): sums = lax.all_to_all(chunk, ZY, 0, 0, tiled=True).astype(f32).sum(axis=0)  15.4 us
    all_to_all x1, starting transfers between devices, local(): lax.all_to_all(jnp.broadcast_to(block, (N_ZY, BLK, LANES)), ZY, 0, 0, til...  12.7 us
    all_to_all x1, waiting for transfers between devices, local(): sums = lax.all_to_all(chunk, ZY, 0, 0, tiled=True).astype(f32).sum(axis=0)  12.6 us
    all_to_all x1, waiting for transfers between devices, local(): lax.all_to_all(jnp.broadcast_to(block, (N_ZY, BLK, LANES)), ZY, 0, 0, til...  10.5 us
    all_to_all x1, starting transfers between devices, local(): lax.all_to_all(jnp.broadcast_to(part, (8, 4, LANES)), ('c', 'x'), 0, 0, t...  9.3 us
    pallas_call x1, Pallas kernels, local(): pl.pallas_call(rows_kernel, out_shape=(jax.ShapeDtypeStruct((tokens, LANE...  7.67 us
  transfers between devices with their start and end apart: 12, of which 5 were waited for; matrix products, arithmetic and copies ran while one was open for 8% of the time, Pallas kernels for 0%

profile of v3, /device:TPU:1, one launch (start us, length us, event | category | flops | bytes accessed | tf_op | source)
XLA Modules:
  0.0 136.8 jit_solution(1947017636678194997)
XLA Ops:
  0.6 0.1 pad_add_fusion.6.pos_ref
  0.7 1.6 %copy-done = bf16[128,8192]{1,0:T(8,128)(2,1)S(1)} copy-done((bf16[128,8192]{1,0:T(8,128)(2,1)S(1)}, bf16[128,8192]{1,0:T(8,128)(2,1)}, u32[]{:S(2)}) %copy-start) | copy-done | bytes 2097176
  2.3 0.8 copy-done.2
  3.1 4.5 %shard_map.58 = (bf16[4,96,16,128]{3,2,1,0:T(8,128)(2,1)S(1)}, bf16[4,96,16,128]{3,2,1,0:T(8,128)(2,1)}, f32[128,128]{1,0:T(8,128)S(1)}) custom-call(s32[2]{0:T(128)S(1)} %pad_add_fusion.6.pos_ref, bf16[128,8192]{1,0:T(8,128)(2,1)S(1)} %copy-done, bf16[128,128]{1,0:T(8,128)(2,1)S(1)} %copy-done.2), custom_call_target="tpu_custom_call" | custom-call | flops 536870912 | bytes 8388608 | tf_op jit(solution)/shard_map/pallas_call | solution.py:156
  7.6 12.4 %collective-permute-start = (bf16[4,96,16,128]{3,2,1,0:T(8,128)(2,1)}, bf16[4,96,16,128]{3,2,1,0:T(8,128)(2,1)}, u32[]{:S(2)}, u32[]{:S(2)}) collective-permute-start(bf16[4,96,16,128]{3,2,1,0:T(8,128)(2,1)} %get-tuple-element.17), channel_id=1, source_target_pairs={{0,96},{96,0},{1,97},{97,1},{2,98},{98,2},{3,99},{99,3},{4,100},{1... | collective-permute-start | bytes 4718600 | tf_op jit(solution)/shard_map/ppermute | solution.py:24
  20.1 0.1 fusion.9
  20.2 0.8 broadcast_in_dim.25
  21.0 12.7 %all-to-all-start = ((bf16[96,16,128]{2,1,0:T(8,128)(2,1)}), bf16[96,16,128]{2,1,0:T(8,128)(2,1)S(1)}, u32[]{:S(2)}, u32[]{:S(2)}) async-start(bf16[96,16,128]{2,1,0:T(8,128)(2,1)} %broadcast_in_dim.25), calls=%async_computation | async-start | bytes 786432 | tf_op jit(solution)/shard_map/all_to_all | solution.py:153
  33.7 2.4 %fusion.4 = (bf16[96,16,128]{2,1,0:T(8,128)(2,1)}, bf16[96,16,128]{2,1,0:T(8,128)(2,1)}, bf16[96,16,128]{2,1,0:T(8,128)(2,1)}) fusion(bf16[4,96,16,128]{3,2,1,0:T(8,128)(2,1)} %collective-permute-done, bf16[4,96,16,128]{3,2,1,0:T(8,128)(2,1)S(1)} %get-tuple-element.16), kind=kLoop, calls=%fused_computation.12 | loop fusion | flops 2359296 | bytes 3538944 | tf_op jit(solution)/shard_map/convert_element_type | solution.py:167
  36.2 4.4 %collective-permute-start.3 = (bf16[96,16,128]{2,1,0:T(8,128)(2,1)}, bf16[96,16,128]{2,1,0:T(8,128)(2,1)S(1)}, u32[]{:S(2)}, u32[]{:S(2)}) collective-permute-start(bf16[96,16,128]{2,1,0:T(8,128)(2,1)} %get-tuple-element.27), channel_id=1, source_target_pairs={{0,3},{1,0},{2,1},{3,2},{4,7},{5,4},{6,5},{7,6},{8,11},{9,8},{10,9... | collective-permute-start | bytes 1179656 | tf_op jit(solution)/shard_map/ppermute | solution.py:28
  40.5 2.4 %collective-permute-start.2 = (bf16[96,16,128]{2,1,0:T(8,128)(2,1)}, bf16[96,16,128]{2,1,0:T(8,128)(2,1)S(1)}, u32[]{:S(2)}, u32[]{:S(2)}) collective-permute-start(bf16[96,16,128]{2,1,0:T(8,128)(2,1)} %get-tuple-element.28), channel_id=1, source_target_pairs={{0,2},{1,3},{2,0},{3,1},{4,6},{5,7},{6,4},{7,5},{8,10},{9,11},{10,... | collective-permute-start | bytes 1179656 | tf_op jit(solution)/shard_map/ppermute | solution.py:28
  43.0 2.5 %collective-permute-start.1 = (bf16[96,16,128]{2,1,0:T(8,128)(2,1)}, bf16[96,16,128]{2,1,0:T(8,128)(2,1)S(1)}, u32[]{:S(2)}, u32[]{:S(2)}) collective-permute-start(bf16[96,16,128]{2,1,0:T(8,128)(2,1)} %get-tuple-element.29), channel_id=1, source_target_pairs={{0,1},{1,2},{2,3},{3,0},{4,5},{5,6},{6,7},{7,4},{8,9},{9,10},{10,1... | collective-permute-start | bytes 1179656 | tf_op jit(solution)/shard_map/ppermute | solution.py:28
  45.5 10.5 %all-to-all-done.refs_0_ = bf16[96,16,128]{2,1,0:T(8,128)(2,1)S(1)} async-done(((bf16[96,16,128]{2,1,0:T(8,128)(2,1)}), bf16[96,16,128]{2,1,0:T(8,128)(2,1)S(1)}, u32[]{:S(2)}, u32[]{:S(2)}) %all-to-all-start) | async-done | bytes 393248 | tf_op jit(solution)/shard_map/all_to_all | solution.py:153
  56.0 1.3 collective-permute-done.3
  57.3 0.0 collective-permute-done.2
  57.3 0.7 copy-done.4
  58.1 5.5 %collective-permute-done.1 = bf16[96,16,128]{2,1,0:T(8,128)(2,1)S(1)} collective-permute-done((bf16[96,16,128]{2,1,0:T(8,128)(2,1)}, bf16[96,16,128]{2,1,0:T(8,128)(2,1)S(1)}, u32[]{:S(2)}, u32[]{:S(2)}) %collective-permute-start.1) | collective-permute-done | bytes 393248 | tf_op jit(solution)/shard_map/ppermute | solution.py:28
  63.6 0.8 copy-done.5
  64.4 1.9 %collective-permute-start.6 = (bf16[96,16,128]{2,1,0:T(8,128)(2,1)S(1)}, bf16[96,16,128]{2,1,0:T(8,128)(2,1)S(1)}, u32[]{:S(2)}, u32[]{:S(2)}) collective-permute-start(bf16[96,16,128]{2,1,0:T(8,128)(2,1)S(1)} %all-to-all-done.refs_0_), channel_id=1, source_target_pairs={{0,3},{1,0},{2,1},{3,2},{4,7},{5,4},{6,5},{7,6},{8,11},{9,8},{10,9... | collective-permute-start | bytes 1179656 | tf_op jit(solution)/shard_map/ppermute | solution.py:28
  66.3 2.4 %collective-permute-start.5 = (bf16[96,16,128]{2,1,0:T(8,128)(2,1)S(1)}, bf16[96,16,128]{2,1,0:T(8,128)(2,1)S(1)}, u32[]{:S(2)}, u32[]{:S(2)}) collective-permute-start(bf16[96,16,128]{2,1,0:T(8,128)(2,1)S(1)} %all-to-all-done.refs_0_), channel_id=1, source_target_pairs={{0,2},{1,3},{2,0},{3,1},{4,6},{5,7},{6,4},{7,5},{8,10},{9,11},{10,... | collective-permute-start | bytes 1179656 | tf_op jit(solution)/shard_map/ppermute | solution.py:28
  68.7 2.9 %collective-permute-start.4 = (bf16[96,16,128]{2,1,0:T(8,128)(2,1)S(1)}, bf16[96,16,128]{2,1,0:T(8,128)(2,1)}, u32[]{:S(2)}, u32[]{:S(2)}) collective-permute-start(bf16[96,16,128]{2,1,0:T(8,128)(2,1)S(1)} %all-to-all-done.refs_0_), channel_id=1, source_target_pairs={{0,1},{1,2},{2,3},{3,0},{4,5},{5,6},{6,7},{7,4},{8,9},{9,10},{10,1... | collective-permute-start | bytes 1179656 | tf_op jit(solution)/shard_map/ppermute | solution.py:28
  71.6 1.7 %multiply_reduce_fusion = bf16[96,16]{1,0:T(8,128)(2,1)S(1)} fusion(bf16[96,16,128]{2,1,0:T(8,128)(2,1)S(1)} %all-to-all-done.refs_0_, bf16[96,16,128]{2,1,0:T(8,128)(2,1)S(1)} %collective-permute-done.3, bf16[96,16,128]{2,1,0:T(8,128)(2,1)} %copy-done.4, bf16[96,16,128]{2,1,0:T(8,128)(2,1)} %copy-done.5, bf16[4,96,16,128]{3,2,1,0:T(8,128)(2,1)} %collective-permute-done, ...), kind=kLoop, calls=%fused_computation.6 | loop fusion | flops 2357760 | bytes 2362368 | tf_op jit(solution)/shard_map/reduce_sum | solution.py:174
  73.3 0.1 reshape.78
  73.4 0.1 reshape.80
  73.5 0.1 reshape.79
  73.6 0.1 pad_maximum_fusion.1
  73.7 2.3 %select_convert_fusion = bf16[96,16,128]{2,1,0:T(8,128)(2,1)} fusion(bf16[8,4,128]{2,1,0:T(4,128)(2,1)S(1)} %bitcast.71, pred[16]{0:T(512)(128)(4,1)S(1)} %iota_compare_fusion, bf16[96,16,128]{2,1,0:T(8,128)(2,1)S(1)} %collective-permute-done.3, bf16[96,16,128]{2,1,0:T(8,128)(2,1)} %copy-done.4, bf16[96,16,128]{2,1,0:T(8,128)(2,1)} %copy-done.5, ...), kind=kLoop, calls=%fused_computation.5 | loop fusion | flops 1966080 | bytes 2367504 | tf_op jit(solution)/shard_map/convert_element_type | solution.py:182
  76.0 15.4 %all-to-all-start.1 = ((bf16[96,16,128]{2,1,0:T(8,128)(2,1)}), bf16[96,16,128]{2,1,0:T(8,128)(2,1)}, u32[]{:S(2)}, u32[]{:S(2)}) async-start(bf16[96,16,128]{2,1,0:T(8,128)(2,1)} %select_convert_fusion), calls=%async_computation.1 | async-start | bytes 786432 | tf_op jit(solution)/shard_map/all_to_all | solution.py:183
  91.4 0.0 copy-start.1
  91.4 0.0 copy-start.3
  91.5 0.0 collective-permute-done.6.refs_3_
  91.5 2.3 %pad_maximum_fusion = bf16[3,96,16,128]{3,2,1,0:T(8,128)(2,1)} fusion(bf16[1,96,16,128]{3,2,1,0:T(8,128)(2,1)S(1)} %bitcast.67, bf16[1,96,16,128]{3,2,1,0:T(8,128)(2,1)S(1)} %bitcast.68, bf16[1,96,16,128]{3,2,1,0:T(8,128)(2,1)} %bitcast.6), kind=kLoop, calls=%fused_computation | loop fusion | flops 1179648 | bytes 2359296 | tf_op jit(solution)/shard_map/stack | solution.py:171
  93.8 3.4 %collective-permute-start.8 = (bf16[3,96,16,128]{3,2,1,0:T(8,128)(2,1)}, bf16[3,96,16,128]{3,2,1,0:T(8,128)(2,1)}, u32[]{:S(2)}, u32[]{:S(2)}) collective-permute-start(bf16[3,96,16,128]{3,2,1,0:T(8,128)(2,1)} %pad_maximum_fusion), channel_id=1, source_target_pairs={{0,96},{96,0},{1,97},{97,1},{2,98},{98,2},{3,99},{99,3},{4,100},{1... | collective-permute-start | bytes 3538952 | tf_op jit(solution)/shard_map/ppermute | solution.py:24
  97.2 1.9 %collective-permute-start.7 = (bf16[96,16,128]{2,1,0:T(8,128)(2,1)S(1)}, bf16[96,16,128]{2,1,0:T(8,128)(2,1)}, u32[]{:S(2)}, u32[]{:S(2)}) collective-permute-start(bf16[96,16,128]{2,1,0:T(8,128)(2,1)S(1)} %all-to-all-done.refs_0_), channel_id=1, source_target_pairs={{0,96},{96,0},{1,97},{97,1},{2,98},{98,2},{3,99},{99,3},{4,100},{1... | collective-permute-start | bytes 1179656 | tf_op jit(solution)/shard_map/ppermute | solution.py:24
  99.2 12.6 %all-to-all-done.1 = bf16[96,16,128]{2,1,0:T(8,128)(2,1)} async-done(((bf16[96,16,128]{2,1,0:T(8,128)(2,1)}), bf16[96,16,128]{2,1,0:T(8,128)(2,1)}, u32[]{:S(2)}, u32[]{:S(2)}) %all-to-all-start.1) | async-done | bytes 393248 | tf_op jit(solution)/shard_map/all_to_all | solution.py:183
  111.8 1.1 convert_reduce_fusion
  113.0 7.7 %shard_map.59 = (bf16[128,128]{1,0:T(8,128)(2,1)}, bf16[128,8192]{1,0:T(8,128)(2,1)}, f32[64,128]{1,0:T(8,128)S(1)}) custom-call(s32[2]{0:T(128)S(1)} %pad_add_fusion.6.pos_ref, bf16[128,8192]{1,0:T(8,128)(2,1)S(1)} %copy-done.1, bf16[128,128]{1,0:T(8,128)(2,1)S(1)} %copy-done.3, f32[128,128]{1,0:T(8,128)S(1)} %get-tuple-element.15.inv_ref, ...), custom_call_target="tpu_custom_call" | custom-call | flops 536870912 | bytes 10485760 | tf_op jit(solution)/shard_map/pallas_call | solution.py:185
  120.6 0.6 broadcast_in_dim.27
  121.2 9.3 %all-to-all-start.2 = ((f32[8,4,128]{2,1,0:T(4,128)}), f32[8,4,128]{2,1,0:T(4,128)S(1)}, u32[]{:S(2)}, u32[]{:S(2)}) async-start(f32[8,4,128]{2,1,0:T(4,128)} %broadcast_in_dim.27), calls=%async_computation.2 | async-start | bytes 32768 | tf_op jit(solution)/shard_map/all_to_all | solution.py:200
  130.5 0.1 pad_dynamic-slice_fusion
  130.6 0.1 fusion.8
  130.7 4.7 %all-to-all-done.2 = f32[8,4,128]{2,1,0:T(4,128)S(1)} async-done(((f32[8,4,128]{2,1,0:T(4,128)}), f32[8,4,128]{2,1,0:T(4,128)S(1)}, u32[]{:S(2)}, u32[]{:S(2)}) %all-to-all-start.2) | async-done | bytes 16416 | tf_op jit(solution)/shard_map/all_to_all | solution.py:200
  135.4 0.2 reshape.85
  135.7 0.1 slice_bitcast_fusion.7
  135.8 0.2 fusion.5
  136.0 0.1 reshape.86
  136.1 0.1 fusion.7
  136.2 0.6 reshape.87
  (23 shorter events, 0.1 us)
Async XLA Ops:
  0.6 19.4 %copy-start.6 = (bf16[1,1376]{1,0:T(2,128)(2,1)S(1)}, bf16[1,1376]{1,0:T(2,128)(2,1)}, u32[]{:S(2)}) copy-start(bf16[1,1376]{1,0:T(2,128)(2,1)} %param.5) | copy-start | bytes 8260
  0.7 1.6 %copy-start = (bf16[128,8192]{1,0:T(8,128)(2,1)S(1)}, bf16[128,8192]{1,0:T(8,128)(2,1)}, u32[]{:S(2)}) copy-start(bf16[128,8192]{1,0:T(8,128)(2,1)} %hidden_ref.3) | copy-start | bytes 6291460
  2.3 0.8 copy-start.2
  7.6 26.1 %collective-permute-start = (bf16[4,96,16,128]{3,2,1,0:T(8,128)(2,1)}, bf16[4,96,16,128]{3,2,1,0:T(8,128)(2,1)}, u32[]{:S(2)}, u32[]{:S(2)}) collective-permute-start(bf16[4,96,16,128]{3,2,1,0:T(8,128)(2,1)} %get-tuple-element.17), channel_id=1, source_target_pairs={{0,96},{96,0},{1,97},{97,1},{2,98},{98,2},{3,99},{99,3},{4,100},{1... | collective-permute-start | bytes 4718600 | tf_op jit(solution)/shard_map/ppermute | solution.py:24
  21.0 35.0 %all-to-all-start = ((bf16[96,16,128]{2,1,0:T(8,128)(2,1)}), bf16[96,16,128]{2,1,0:T(8,128)(2,1)S(1)}, u32[]{:S(2)}, u32[]{:S(2)}) async-start(bf16[96,16,128]{2,1,0:T(8,128)(2,1)} %broadcast_in_dim.25), calls=%async_computation | async-start | bytes 786432 | tf_op jit(solution)/shard_map/all_to_all | solution.py:153
  36.2 21.2 %collective-permute-start.3 = (bf16[96,16,128]{2,1,0:T(8,128)(2,1)}, bf16[96,16,128]{2,1,0:T(8,128)(2,1)S(1)}, u32[]{:S(2)}, u32[]{:S(2)}) collective-permute-start(bf16[96,16,128]{2,1,0:T(8,128)(2,1)} %get-tuple-element.27), channel_id=1, source_target_pairs={{0,3},{1,0},{2,1},{3,2},{4,7},{5,4},{6,5},{7,6},{8,11},{9,8},{10,9... | collective-permute-start | bytes 1179656 | tf_op jit(solution)/shard_map/ppermute | solution.py:28
  40.5 16.8 %collective-permute-start.2 = (bf16[96,16,128]{2,1,0:T(8,128)(2,1)}, bf16[96,16,128]{2,1,0:T(8,128)(2,1)S(1)}, u32[]{:S(2)}, u32[]{:S(2)}) collective-permute-start(bf16[96,16,128]{2,1,0:T(8,128)(2,1)} %get-tuple-element.28), channel_id=1, source_target_pairs={{0,2},{1,3},{2,0},{3,1},{4,6},{5,7},{6,4},{7,5},{8,10},{9,11},{10,... | collective-permute-start | bytes 1179656 | tf_op jit(solution)/shard_map/ppermute | solution.py:28
  43.0 20.6 %collective-permute-start.1 = (bf16[96,16,128]{2,1,0:T(8,128)(2,1)}, bf16[96,16,128]{2,1,0:T(8,128)(2,1)S(1)}, u32[]{:S(2)}, u32[]{:S(2)}) collective-permute-start(bf16[96,16,128]{2,1,0:T(8,128)(2,1)} %get-tuple-element.29), channel_id=1, source_target_pairs={{0,1},{1,2},{2,3},{3,0},{4,5},{5,6},{6,7},{7,4},{8,9},{9,10},{10,1... | collective-permute-start | bytes 1179656 | tf_op jit(solution)/shard_map/ppermute | solution.py:28
  57.3 0.7 copy-start.4
  63.6 0.8 copy-start.5
  64.4 27.1 %collective-permute-start.6 = (bf16[96,16,128]{2,1,0:T(8,128)(2,1)S(1)}, bf16[96,16,128]{2,1,0:T(8,128)(2,1)S(1)}, u32[]{:S(2)}, u32[]{:S(2)}) collective-permute-start(bf16[96,16,128]{2,1,0:T(8,128)(2,1)S(1)} %all-to-all-done.refs_0_), channel_id=1, source_target_pairs={{0,3},{1,0},{2,1},{3,2},{4,7},{5,4},{6,5},{7,6},{8,11},{9,8},{10,9... | collective-permute-start | bytes 1179656 | tf_op jit(solution)/shard_map/ppermute | solution.py:28
  66.3 25.2 %collective-permute-start.5 = (bf16[96,16,128]{2,1,0:T(8,128)(2,1)S(1)}, bf16[96,16,128]{2,1,0:T(8,128)(2,1)S(1)}, u32[]{:S(2)}, u32[]{:S(2)}) collective-permute-start(bf16[96,16,128]{2,1,0:T(8,128)(2,1)S(1)} %all-to-all-done.refs_0_), channel_id=1, source_target_pairs={{0,2},{1,3},{2,0},{3,1},{4,6},{5,7},{6,4},{7,5},{8,10},{9,11},{10,... | collective-permute-start | bytes 1179656 | tf_op jit(solution)/shard_map/ppermute | solution.py:28
  68.7 22.7 %collective-permute-start.4 = (bf16[96,16,128]{2,1,0:T(8,128)(2,1)S(1)}, bf16[96,16,128]{2,1,0:T(8,128)(2,1)}, u32[]{:S(2)}, u32[]{:S(2)}) collective-permute-start(bf16[96,16,128]{2,1,0:T(8,128)(2,1)S(1)} %all-to-all-done.refs_0_), channel_id=1, source_target_pairs={{0,1},{1,2},{2,3},{3,0},{4,5},{5,6},{6,7},{7,4},{8,9},{9,10},{10,1... | collective-permute-start | bytes 1179656 | tf_op jit(solution)/shard_map/ppermute | solution.py:28
  76.0 35.8 %all-to-all-start.1 = ((bf16[96,16,128]{2,1,0:T(8,128)(2,1)}), bf16[96,16,128]{2,1,0:T(8,128)(2,1)}, u32[]{:S(2)}, u32[]{:S(2)}) async-start(bf16[96,16,128]{2,1,0:T(8,128)(2,1)} %select_convert_fusion), calls=%async_computation.1 | async-start | bytes 786432 | tf_op jit(solution)/shard_map/all_to_all | solution.py:183
  91.4 21.5 %copy-start.1 = (bf16[128,8192]{1,0:T(8,128)(2,1)S(1)}, bf16[128,8192]{1,0:T(8,128)(2,1)}, u32[]{:S(2)}) copy-start(bf16[128,8192]{1,0:T(8,128)(2,1)} %hidden_ref.3) | copy-start | bytes 6291460
  91.4 21.5 %copy-start.3 = (bf16[128,128]{1,0:T(8,128)(2,1)S(1)}, bf16[128,128]{1,0:T(8,128)(2,1)}, u32[]{:S(2)}) copy-start(bf16[128,128]{1,0:T(8,128)(2,1)} %cot_ref.3) | copy-start | bytes 98308
  93.8 19.2 %collective-permute-start.8 = (bf16[3,96,16,128]{3,2,1,0:T(8,128)(2,1)}, bf16[3,96,16,128]{3,2,1,0:T(8,128)(2,1)}, u32[]{:S(2)}, u32[]{:S(2)}) collective-permute-start(bf16[3,96,16,128]{3,2,1,0:T(8,128)(2,1)} %pad_maximum_fusion), channel_id=1, source_target_pairs={{0,96},{96,0},{1,97},{97,1},{2,98},{98,2},{3,99},{99,3},{4,100},{1... | collective-permute-start | bytes 3538952 | tf_op jit(solution)/shard_map/ppermute | solution.py:24
  97.2 15.7 %collective-permute-start.7 = (bf16[96,16,128]{2,1,0:T(8,128)(2,1)S(1)}, bf16[96,16,128]{2,1,0:T(8,128)(2,1)}, u32[]{:S(2)}, u32[]{:S(2)}) collective-permute-start(bf16[96,16,128]{2,1,0:T(8,128)(2,1)S(1)} %all-to-all-done.refs_0_), channel_id=1, source_target_pairs={{0,96},{96,0},{1,97},{97,1},{2,98},{98,2},{3,99},{99,3},{4,100},{1... | collective-permute-start | bytes 1179656 | tf_op jit(solution)/shard_map/ppermute | solution.py:24
  121.2 14.2 %all-to-all-start.2 = ((f32[8,4,128]{2,1,0:T(4,128)}), f32[8,4,128]{2,1,0:T(4,128)S(1)}, u32[]{:S(2)}, u32[]{:S(2)}) async-start(f32[8,4,128]{2,1,0:T(4,128)} %broadcast_in_dim.27), calls=%async_computation.2 | async-start | bytes 32768 | tf_op jit(solution)/shard_map/all_to_all | solution.py:200

commit v4 on v2

--- a/solution.py
+++ b/solution.py
@@ -162,13 +162,9 @@
         compiler_params=pltpu.CompilerParams(vmem_limit_bytes=24 << 20),
         cost_estimate=pl.CostEstimate(flops=4 * tokens * width * LANES, bytes_accessed=8 << 20, transcendentals=0),
     )(pos, hidden_in, cotangent)
-    send, mine = lax.optimization_barrier((send, mine))
     got = swap(send)
     pair = [own[k].astype(f32) + got[k].astype(f32) for k in range(4)]
     moved = [shift_x(pair[k].astype(bf16), k) for k in range(1, 4)]
-
-    held = [mine] + [shift_x(mine, k) for k in range(1, 4)]
-    other = [swap(mine), swap(jnp.stack(held[1:]))]
 
     total = pair[0] + moved[0].astype(f32) + moved[1].astype(f32) + moved[2].astype(f32)
     gain_part = jnp.sum(mine.astype(f32) * total, axis=-1)[:, :USED].reshape(12, 8 * USED)
@@ -179,8 +175,11 @@
     pay = jnp.concatenate([jnp.zeros_like(pay), pay], axis=1).reshape(8, 4, LANES)
     pay = jnp.pad(pay, ((N_ZY - 8, 0), (USED, 0), (0, 0)))
     spare = lax.broadcasted_iota(jnp.int32, (1, BLK, 1), 1) >= USED
-    chunk = jnp.where(spare, pay, total).astype(bf16)
-    sums = lax.all_to_all(chunk, ZY, 0, 0, tiled=True).astype(f32).sum(axis=0)
+    chunk, mine = lax.optimization_barrier((jnp.where(spare, pay, total).astype(bf16), mine))
+
+    held = [mine] + [shift_x(mine, k) for k in range(1, 4)]
+    other = [swap(mine), swap(jnp.stack(held[1:]))]
+    received = lax.all_to_all(chunk, ZY, 0, 0, tiled=True)
 
     key_rows, input_grad, gains = pl.pallas_call(
         rows_kernel,
@@ -196,6 +195,8 @@
         cost_estimate=pl.CostEstimate(flops=4 * tokens * width * LANES, bytes_accessed=10 << 20, transcendentals=0),
     )(pos, hidden_in, cotangent, inv, *held, *other)
 
+    received, gains = lax.optimization_barrier((received, gains))
+    sums = received.astype(f32).sum(axis=0)
     part = sums[USED:]
     parts = lax.all_to_all(jnp.broadcast_to(part, (8, 4, LANES)), ("c", "x"), 0, 0, tiled=True)
     both = parts.reshape(2, 4, 512)[:, :, :480].reshape(2, 4, 5, 4, 2, USED)

time: 142 us -> 147 us (1.035)
  starting transfers between devices: 68.6 us -> 70.5 us
  other arithmetic: 6.88 us -> 8.71 us
    all_to_all x1, starting transfers between devices: 22.5 us -> 12.7 us  [local(): lax.all_to_all(jnp.broadcast_to(block, (N_ZY, BLK, LANES)), ZY, 0, 0, til...]
    all_to_all x1, starting transfers between devices: 6.92 us -> 15.1 us  [local(): received = lax.all_to_all(chunk, ZY, 0, 0, tiled=True)]
    ppermute x3, starting transfers between devices: 12.1 us -> 17 us  [swap(): return lax.ppermute(a, 'c', [(0, 1), (1, 0)])]
    all_to_all x1, waiting for transfers between devices: 14.5 us -> 9.9 us  [local(): lax.all_to_all(jnp.broadcast_to(block, (N_ZY, BLK, LANES)), ZY, 0, 0, til...]
    ppermute x6, waiting for transfers between devices: 17.1 us -> 21.1 us  [shift_x(): return lax.ppermute(a, 'x', [(i, (i + k) % 4) for i in range(4)])]
    all_to_all x1, starting transfers between devices: 8.1 us -> 5.72 us  [local(): lax.all_to_all(jnp.broadcast_to(part, (8, 4, LANES)), ('c', 'x'), 0, 0, t...]
    convert_element_type x1, other arithmetic: 0.31 us -> 2.43 us  [local(): moved = [shift_x(pair[k].astype(bf16), k) for k in range(1, 4)]]
    all_to_all x1, waiting for transfers between devices: 7.8 us -> 9.68 us  [local(): received = lax.all_to_all(chunk, ZY, 0, 0, tiled=True)]
  transfers between devices with their start and end apart: 12 -> 12, of which waited for: 9 -> 8; matrix products, arithmetic and copies ran while one was open for 4% -> 2% of each run, Pallas kernels for 8% -> 5%
where the time goes in v4:
time: 147 us; the launch traced here: 146 us
  starting transfers between devices  70.5 us (48%)
  waiting for transfers between devices  46.9 us (32%)
  Pallas kernels  12.1 us (8%)
  other arithmetic  8.71 us (6%)
  local copies, waits for them, and re-layouts  7.11 us (5%)
    ppermute x6, waiting for transfers between devices, shift_x(): return lax.ppermute(a, 'x', [(i, (i + k) % 4) for i in range(4)])  21.1 us
    ppermute x6, starting transfers between devices, shift_x(): return lax.ppermute(a, 'x', [(i, (i + k) % 4) for i in range(4)])  19.9 us
    ppermute x3, starting transfers between devices, swap(): return lax.ppermute(a, 'c', [(0, 1), (1, 0)])  17 us
    all_to_all x1, starting transfers between devices, local(): received = lax.all_to_all(chunk, ZY, 0, 0, tiled=True)  15.1 us
    all_to_all x1, starting transfers between devices, local(): lax.all_to_all(jnp.broadcast_to(block, (N_ZY, BLK, LANES)), ZY, 0, 0, til...  12.7 us
    all_to_all x1, waiting for transfers between devices, local(): lax.all_to_all(jnp.broadcast_to(block, (N_ZY, BLK, LANES)), ZY, 0, 0, til...  9.9 us
    all_to_all x1, waiting for transfers between devices, local(): received = lax.all_to_all(chunk, ZY, 0, 0, tiled=True)  9.68 us
    pallas_call x1, Pallas kernels, local(): pl.pallas_call(rows_kernel, out_shape=(jax.ShapeDtypeStruct((tokens, LANE...  7.58 us
  transfers between devices with their start and end apart: 12, of which 8 were waited for; matrix products, arithmetic and copies ran while one was open for 2% of the time, Pallas kernels for 5%

profile of v4, /device:TPU:1, one launch (start us, length us, event | category | flops | bytes accessed | tf_op | source)
XLA Modules:
  0.0 146.2 jit_solution(11157164624487136632)
XLA Ops:
  0.6 0.1 pad_add_fusion.6.pos_ref
  0.7 1.6 %copy-done = bf16[128,8192]{1,0:T(8,128)(2,1)S(1)} copy-done((bf16[128,8192]{1,0:T(8,128)(2,1)S(1)}, bf16[128,8192]{1,0:T(8,128)(2,1)}, u32[]{:S(2)}) %copy-start) | copy-done | bytes 2097176
  2.3 0.8 copy-done.4
  3.1 4.5 %shard_map.58 = (bf16[4,96,16,128]{3,2,1,0:T(8,128)(2,1)S(1)}, bf16[4,96,16,128]{3,2,1,0:T(8,128)(2,1)}, f32[128,128]{1,0:T(8,128)S(1)}) custom-call(s32[2]{0:T(128)S(1)} %pad_add_fusion.6.pos_ref, bf16[128,8192]{1,0:T(8,128)(2,1)S(1)} %copy-done, bf16[128,128]{1,0:T(8,128)(2,1)S(1)} %copy-done.4), custom_call_target="tpu_custom_call" | custom-call | flops 536870912 | bytes 8388608 | tf_op jit(solution)/shard_map/pallas_call | solution.py:156
  7.6 12.4 %collective-permute-start = (bf16[4,96,16,128]{3,2,1,0:T(8,128)(2,1)}, bf16[4,96,16,128]{3,2,1,0:T(8,128)(2,1)}, u32[]{:S(2)}, u32[]{:S(2)}) collective-permute-start(bf16[4,96,16,128]{3,2,1,0:T(8,128)(2,1)} %get-tuple-element.15), channel_id=1, source_target_pairs={{0,96},{96,0},{1,97},{97,1},{2,98},{98,2},{3,99},{99,3},{4,100},{1... | collective-permute-start | bytes 4718600 | tf_op jit(solution)/shard_map/ppermute | solution.py:24
  20.1 0.1 fusion.9
  20.2 0.8 broadcast_in_dim.26
  21.0 12.7 %all-to-all-start = ((bf16[96,16,128]{2,1,0:T(8,128)(2,1)}), bf16[96,16,128]{2,1,0:T(8,128)(2,1)S(1)}, u32[]{:S(2)}, u32[]{:S(2)}) async-start(bf16[96,16,128]{2,1,0:T(8,128)(2,1)} %broadcast_in_dim.26), calls=%async_computation | async-start | bytes 786432 | tf_op jit(solution)/shard_map/all_to_all | solution.py:153
  33.7 2.4 %fusion.2 = (bf16[96,16,128]{2,1,0:T(8,128)(2,1)}, bf16[96,16,128]{2,1,0:T(8,128)(2,1)}, bf16[96,16,128]{2,1,0:T(8,128)(2,1)}) fusion(bf16[4,96,16,128]{3,2,1,0:T(8,128)(2,1)} %collective-permute-done, bf16[4,96,16,128]{3,2,1,0:T(8,128)(2,1)S(1)} %get-tuple-element.14), kind=kLoop, calls=%fused_computation.10 | loop fusion | flops 2359296 | bytes 3538944 | tf_op jit(solution)/shard_map/convert_element_type | solution.py:167
  36.2 3.1 %collective-permute-start.1 = (bf16[96,16,128]{2,1,0:T(8,128)(2,1)}, bf16[96,16,128]{2,1,0:T(8,128)(2,1)S(1)}, u32[]{:S(2)}, u32[]{:S(2)}) collective-permute-start(bf16[96,16,128]{2,1,0:T(8,128)(2,1)} %get-tuple-element.23), channel_id=1, source_target_pairs={{0,1},{1,2},{2,3},{3,0},{4,5},{5,6},{6,7},{7,4},{8,9},{9,10},{10,1... | collective-permute-start | bytes 1179656 | tf_op jit(solution)/shard_map/ppermute | solution.py:28
  39.3 3.4 %collective-permute-start.3 = (bf16[96,16,128]{2,1,0:T(8,128)(2,1)}, bf16[96,16,128]{2,1,0:T(8,128)(2,1)S(1)}, u32[]{:S(2)}, u32[]{:S(2)}) collective-permute-start(bf16[96,16,128]{2,1,0:T(8,128)(2,1)} %get-tuple-element.24), channel_id=1, source_target_pairs={{0,3},{1,0},{2,1},{3,2},{4,7},{5,4},{6,5},{7,6},{8,11},{9,8},{10,9... | collective-permute-start | bytes 1179656 | tf_op jit(solution)/shard_map/ppermute | solution.py:28
  42.7 3.4 %collective-permute-start.2 = (bf16[96,16,128]{2,1,0:T(8,128)(2,1)}, bf16[96,16,128]{2,1,0:T(8,128)(2,1)S(1)}, u32[]{:S(2)}, u32[]{:S(2)}) collective-permute-start(bf16[96,16,128]{2,1,0:T(8,128)(2,1)} %get-tuple-element.25), channel_id=1, source_target_pairs={{0,2},{1,3},{2,0},{3,1},{4,6},{5,7},{6,4},{7,5},{8,10},{9,11},{10,... | collective-permute-start | bytes 1179656 | tf_op jit(solution)/shard_map/ppermute | solution.py:28
  46.1 9.9 %all-to-all-done.refs_0_ = bf16[96,16,128]{2,1,0:T(8,128)(2,1)S(1)} async-done(((bf16[96,16,128]{2,1,0:T(8,128)(2,1)}), bf16[96,16,128]{2,1,0:T(8,128)(2,1)S(1)}, u32[]{:S(2)}, u32[]{:S(2)}) %all-to-all-start) | async-done | bytes 393248 | tf_op jit(solution)/shard_map/all_to_all | solution.py:153
  56.0 0.0 collective-permute-done.3
  56.0 3.3 %collective-permute-done.2 = bf16[96,16,128]{2,1,0:T(8,128)(2,1)S(1)} collective-permute-done((bf16[96,16,128]{2,1,0:T(8,128)(2,1)}, bf16[96,16,128]{2,1,0:T(8,128)(2,1)S(1)}, u32[]{:S(2)}, u32[]{:S(2)}) %collective-permute-start.2) | collective-permute-done | bytes 393248 | tf_op jit(solution)/shard_map/ppermute | solution.py:28
  59.3 1.4 multiply_reduce_fusion
  60.7 0.1 reshape.78
  60.8 0.1 reshape.80
  61.0 0.1 reshape.79
  61.1 0.1 pad_maximum_fusion.1
  61.2 2.0 %select_convert_fusion = bf16[96,16,128]{2,1,0:T(8,128)(2,1)} fusion(bf16[8,4,128]{2,1,0:T(4,128)(2,1)S(1)} %bitcast.72, pred[16]{0:T(512)(128)(4,1)S(1)} %iota_compare_fusion, bf16[96,16,128]{2,1,0:T(8,128)(2,1)S(1)} %collective-permute-done.3, bf16[96,16,128]{2,1,0:T(8,128)(2,1)S(1)} %collective-permute-done.2, ...), kind=kLoop, calls=%fused_computation.5 | loop fusion | flops 1966080 | bytes 2367504 | tf_op jit(solution)/shard_map/convert_element_type | solution.py:178
  63.2 5.0 %collective-permute-start.6 = (bf16[96,16,128]{2,1,0:T(8,128)(2,1)S(1)}, bf16[96,16,128]{2,1,0:T(8,128)(2,1)S(1)}, u32[]{:S(2)}, u32[]{:S(2)}) collective-permute-start(bf16[96,16,128]{2,1,0:T(8,128)(2,1)S(1)} %all-to-all-done.refs_0_), channel_id=1, source_target_pairs={{0,3},{1,0},{2,1},{3,2},{4,7},{5,4},{6,5},{7,6},{8,11},{9,8},{10,9... | collective-permute-start | bytes 1179656 | tf_op jit(solution)/shard_map/ppermute | solution.py:28
  68.2 3.1 %collective-permute-start.5 = (bf16[96,16,128]{2,1,0:T(8,128)(2,1)S(1)}, bf16[96,16,128]{2,1,0:T(8,128)(2,1)S(1)}, u32[]{:S(2)}, u32[]{:S(2)}) collective-permute-start(bf16[96,16,128]{2,1,0:T(8,128)(2,1)S(1)} %all-to-all-done.refs_0_), channel_id=1, source_target_pairs={{0,2},{1,3},{2,0},{3,1},{4,6},{5,7},{6,4},{7,5},{8,10},{9,11},{10,... | collective-permute-start | bytes 1179656 | tf_op jit(solution)/shard_map/ppermute | solution.py:28
  71.3 1.9 %collective-permute-start.4 = (bf16[96,16,128]{2,1,0:T(8,128)(2,1)S(1)}, bf16[96,16,128]{2,1,0:T(8,128)(2,1)S(1)}, u32[]{:S(2)}, u32[]{:S(2)}) collective-permute-start(bf16[96,16,128]{2,1,0:T(8,128)(2,1)S(1)} %all-to-all-done.refs_0_), channel_id=1, source_target_pairs={{0,1},{1,2},{2,3},{3,0},{4,5},{5,6},{6,7},{7,4},{8,9},{9,10},{10,1... | collective-permute-start | bytes 1179656 | tf_op jit(solution)/shard_map/ppermute | solution.py:28
  73.2 2.3 %collective-permute-done.6.refs_3_ = bf16[96,16,128]{2,1,0:T(8,128)(2,1)S(1)} collective-permute-done((bf16[96,16,128]{2,1,0:T(8,128)(2,1)S(1)}, bf16[96,16,128]{2,1,0:T(8,128)(2,1)S(1)}, u32[]{:S(2)}, u32[]{:S(2)}) %collective-permute-start.6) | collective-permute-done | bytes 393248 | tf_op jit(solution)/shard_map/ppermute | solution.py:28
  75.6 4.7 %collective-permute-done.5.refs_2_ = bf16[96,16,128]{2,1,0:T(8,128)(2,1)S(1)} collective-permute-done((bf16[96,16,128]{2,1,0:T(8,128)(2,1)S(1)}, bf16[96,16,128]{2,1,0:T(8,128)(2,1)S(1)}, u32[]{:S(2)}, u32[]{:S(2)}) %collective-permute-start.5) | collective-permute-done | bytes 393248 | tf_op jit(solution)/shard_map/ppermute | solution.py:28
  80.3 10.8 %collective-permute-done.4.refs_1_ = bf16[96,16,128]{2,1,0:T(8,128)(2,1)S(1)} collective-permute-done((bf16[96,16,128]{2,1,0:T(8,128)(2,1)S(1)}, bf16[96,16,128]{2,1,0:T(8,128)(2,1)S(1)}, u32[]{:S(2)}, u32[]{:S(2)}) %collective-permute-start.4) | collective-permute-done | bytes 393248 | tf_op jit(solution)/shard_map/ppermute | solution.py:28
  91.0 1.1 pad_maximum_fusion
  92.2 0.7 copy-done.2
  92.9 2.4 %collective-permute-start.8 = (bf16[3,96,16,128]{3,2,1,0:T(8,128)(2,1)}, bf16[3,96,16,128]{3,2,1,0:T(8,128)(2,1)}, u32[]{:S(2)}, u32[]{:S(2)}) collective-permute-start(bf16[3,96,16,128]{3,2,1,0:T(8,128)(2,1)} %pad_maximum_fusion), channel_id=1, source_target_pairs={{0,96},{96,0},{1,97},{97,1},{2,98},{98,2},{3,99},{99,3},{4,100},{1... | collective-permute-start | bytes 3538952 | tf_op jit(solution)/shard_map/ppermute | solution.py:24
  95.3 15.1 %all-to-all-start.1 = ((bf16[96,16,128]{2,1,0:T(8,128)(2,1)}), bf16[96,16,128]{2,1,0:T(8,128)(2,1)}, u32[]{:S(2)}, u32[]{:S(2)}) async-start(bf16[96,16,128]{2,1,0:T(8,128)(2,1)} %select_convert_fusion), calls=%async_computation.1 | async-start | bytes 786432 | tf_op jit(solution)/shard_map/all_to_all | solution.py:182
  110.5 2.2 %collective-permute-start.7 = (bf16[96,16,128]{2,1,0:T(8,128)(2,1)S(1)}, bf16[96,16,128]{2,1,0:T(8,128)(2,1)}, u32[]{:S(2)}, u32[]{:S(2)}) collective-permute-start(bf16[96,16,128]{2,1,0:T(8,128)(2,1)S(1)} %all-to-all-done.refs_0_), channel_id=1, source_target_pairs={{0,96},{96,0},{1,97},{97,1},{2,98},{98,2},{3,99},{99,3},{4,100},{1... | collective-permute-start | bytes 1179656 | tf_op jit(solution)/shard_map/ppermute | solution.py:24
  112.7 1.5 %collective-permute-done.7.refs_4_ = bf16[96,16,128]{2,1,0:T(8,128)(2,1)} collective-permute-done((bf16[96,16,128]{2,1,0:T(8,128)(2,1)S(1)}, bf16[96,16,128]{2,1,0:T(8,128)(2,1)}, u32[]{:S(2)}, u32[]{:S(2)}) %collective-permute-start.7) | collective-permute-done | bytes 393248 | tf_op jit(solution)/shard_map/ppermute | solution.py:24
  114.2 1.0 copy-done.3
  115.2 7.6 %shard_map.59 = (bf16[128,128]{1,0:T(8,128)(2,1)}, bf16[128,8192]{1,0:T(8,128)(2,1)}, f32[64,128]{1,0:T(8,128)S(1)}) custom-call(s32[2]{0:T(128)S(1)} %pad_add_fusion.6.pos_ref, bf16[128,8192]{1,0:T(8,128)(2,1)S(1)} %copy-done.1, bf16[128,128]{1,0:T(8,128)(2,1)S(1)} %copy-done.5, f32[128,128]{1,0:T(8,128)S(1)} %get-tuple-element.13.inv_ref, ...), custom_call_target="tpu_custom_call" | custom-call | flops 536870912 | bytes 10485760 | tf_op jit(solution)/shard_map/pallas_call | solution.py:184
  122.8 9.7 %all-to-all-done.1 = bf16[96,16,128]{2,1,0:T(8,128)(2,1)} async-done(((bf16[96,16,128]{2,1,0:T(8,128)(2,1)}), bf16[96,16,128]{2,1,0:T(8,128)(2,1)}, u32[]{:S(2)}, u32[]{:S(2)}) %all-to-all-start.1) | async-done | bytes 393248 | tf_op jit(solution)/shard_map/all_to_all | solution.py:182
  132.5 1.1 convert_reduce_fusion
  133.6 0.6 broadcast_in_dim.27
  134.2 5.7 %all-to-all-start.2 = ((f32[8,4,128]{2,1,0:T(4,128)}), f32[8,4,128]{2,1,0:T(4,128)S(1)}, u32[]{:S(2)}, u32[]{:S(2)}) async-start(f32[8,4,128]{2,1,0:T(4,128)} %broadcast_in_dim.27), calls=%async_computation.2 | async-start | bytes 32768 | tf_op jit(solution)/shard_map/all_to_all | solution.py:201
  139.9 0.1 pad_dynamic-slice_fusion
  140.0 0.1 fusion.8
  140.1 4.7 %all-to-all-done.2 = f32[8,4,128]{2,1,0:T(4,128)S(1)} async-done(((f32[8,4,128]{2,1,0:T(4,128)}), f32[8,4,128]{2,1,0:T(4,128)S(1)}, u32[]{:S(2)}, u32[]{:S(2)}) %all-to-all-start.2) | async-done | bytes 16416 | tf_op jit(solution)/shard_map/all_to_all | solution.py:201
  144.8 0.2 reshape.85
  145.1 0.1 slice_bitcast_fusion.7
  145.2 0.2 fusion.5
  145.4 0.1 reshape.86
  145.5 0.1 fusion.7
  145.6 0.6 reshape.87
  (23 shorter events, 0.1 us)
Async XLA Ops:
  0.6 19.4 %copy-start.6 = (bf16[1,1376]{1,0:T(2,128)(2,1)S(1)}, bf16[1,1376]{1,0:T(2,128)(2,1)}, u32[]{:S(2)}) copy-start(bf16[1,1376]{1,0:T(2,128)(2,1)} %param.5) | copy-start | bytes 8260
  0.7 1.6 %copy-start = (bf16[128,8192]{1,0:T(8,128)(2,1)S(1)}, bf16[128,8192]{1,0:T(8,128)(2,1)}, u32[]{:S(2)}) copy-start(bf16[128,8192]{1,0:T(8,128)(2,1)} %hidden_ref.3) | copy-start | bytes 6291460
  2.3 0.8 copy-start.4
  7.6 26.1 %collective-permute-start = (bf16[4,96,16,128]{3,2,1,0:T(8,128)(2,1)}, bf16[4,96,16,128]{3,2,1,0:T(8,128)(2,1)}, u32[]{:S(2)}, u32[]{:S(2)}) collective-permute-start(bf16[4,96,16,128]{3,2,1,0:T(8,128)(2,1)} %get-tuple-element.15), channel_id=1, source_target_pairs={{0,96},{96,0},{1,97},{97,1},{2,98},{98,2},{3,99},{99,3},{4,100},{1... | collective-permute-start | bytes 4718600 | tf_op jit(solution)/shard_map/ppermute | solution.py:24
  21.0 35.0 %all-to-all-start = ((bf16[96,16,128]{2,1,0:T(8,128)(2,1)}), bf16[96,16,128]{2,1,0:T(8,128)(2,1)S(1)}, u32[]{:S(2)}, u32[]{:S(2)}) async-start(bf16[96,16,128]{2,1,0:T(8,128)(2,1)} %broadcast_in_dim.26), calls=%async_computation | async-start | bytes 786432 | tf_op jit(solution)/shard_map/all_to_all | solution.py:153
  36.2 19.9 %collective-permute-start.1 = (bf16[96,16,128]{2,1,0:T(8,128)(2,1)}, bf16[96,16,128]{2,1,0:T(8,128)(2,1)S(1)}, u32[]{:S(2)}, u32[]{:S(2)}) collective-permute-start(bf16[96,16,128]{2,1,0:T(8,128)(2,1)} %get-tuple-element.23), channel_id=1, source_target_pairs={{0,1},{1,2},{2,3},{3,0},{4,5},{5,6},{6,7},{7,4},{8,9},{9,10},{10,1... | collective-permute-start | bytes 1179656 | tf_op jit(solution)/shard_map/ppermute | solution.py:28
  39.3 16.8 %collective-permute-start.3 = (bf16[96,16,128]{2,1,0:T(8,128)(2,1)}, bf16[96,16,128]{2,1,0:T(8,128)(2,1)S(1)}, u32[]{:S(2)}, u32[]{:S(2)}) collective-permute-start(bf16[96,16,128]{2,1,0:T(8,128)(2,1)} %get-tuple-element.24), channel_id=1, source_target_pairs={{0,3},{1,0},{2,1},{3,2},{4,7},{5,4},{6,5},{7,6},{8,11},{9,8},{10,9... | collective-permute-start | bytes 1179656 | tf_op jit(solution)/shard_map/ppermute | solution.py:28
  42.7 16.6 %collective-permute-start.2 = (bf16[96,16,128]{2,1,0:T(8,128)(2,1)}, bf16[96,16,128]{2,1,0:T(8,128)(2,1)S(1)}, u32[]{:S(2)}, u32[]{:S(2)}) collective-permute-start(bf16[96,16,128]{2,1,0:T(8,128)(2,1)} %get-tuple-element.25), channel_id=1, source_target_pairs={{0,2},{1,3},{2,0},{3,1},{4,6},{5,7},{6,4},{7,5},{8,10},{9,11},{10,... | collective-permute-start | bytes 1179656 | tf_op jit(solution)/shard_map/ppermute | solution.py:28
  63.2 12.3 %collective-permute-start.6 = (bf16[96,16,128]{2,1,0:T(8,128)(2,1)S(1)}, bf16[96,16,128]{2,1,0:T(8,128)(2,1)S(1)}, u32[]{:S(2)}, u32[]{:S(2)}) collective-permute-start(bf16[96,16,128]{2,1,0:T(8,128)(2,1)S(1)} %all-to-all-done.refs_0_), channel_id=1, source_target_pairs={{0,3},{1,0},{2,1},{3,2},{4,7},{5,4},{6,5},{7,6},{8,11},{9,8},{10,9... | collective-permute-start | bytes 1179656 | tf_op jit(solution)/shard_map/ppermute | solution.py:28
  68.2 12.1 %collective-permute-start.5 = (bf16[96,16,128]{2,1,0:T(8,128)(2,1)S(1)}, bf16[96,16,128]{2,1,0:T(8,128)(2,1)S(1)}, u32[]{:S(2)}, u32[]{:S(2)}) collective-permute-start(bf16[96,16,128]{2,1,0:T(8,128)(2,1)S(1)} %all-to-all-done.refs_0_), channel_id=1, source_target_pairs={{0,2},{1,3},{2,0},{3,1},{4,6},{5,7},{6,4},{7,5},{8,10},{9,11},{10,... | collective-permute-start | bytes 1179656 | tf_op jit(solution)/shard_map/ppermute | solution.py:28
  71.3 19.8 %collective-permute-start.4 = (bf16[96,16,128]{2,1,0:T(8,128)(2,1)S(1)}, bf16[96,16,128]{2,1,0:T(8,128)(2,1)S(1)}, u32[]{:S(2)}, u32[]{:S(2)}) collective-permute-start(bf16[96,16,128]{2,1,0:T(8,128)(2,1)S(1)} %all-to-all-done.refs_0_), channel_id=1, source_target_pairs={{0,1},{1,2},{2,3},{3,0},{4,5},{5,6},{6,7},{7,4},{8,9},{9,10},{10,1... | collective-permute-start | bytes 1179656 | tf_op jit(solution)/shard_map/ppermute | solution.py:28
  91.0 23.2 %copy-start.1 = (bf16[128,8192]{1,0:T(8,128)(2,1)S(1)}, bf16[128,8192]{1,0:T(8,128)(2,1)}, u32[]{:S(2)}) copy-start(bf16[128,8192]{1,0:T(8,128)(2,1)} %hidden_ref.3) | copy-start | bytes 6291460
  91.0 23.2 %copy-start.5 = (bf16[128,128]{1,0:T(8,128)(2,1)S(1)}, bf16[128,128]{1,0:T(8,128)(2,1)}, u32[]{:S(2)}) copy-start(bf16[128,128]{1,0:T(8,128)(2,1)} %cot_ref.3) | copy-start | bytes 98308
  92.2 0.8 copy-start.2
  92.9 21.3 %collective-permute-start.8 = (bf16[3,96,16,128]{3,2,1,0:T(8,128)(2,1)}, bf16[3,96,16,128]{3,2,1,0:T(8,128)(2,1)}, u32[]{:S(2)}, u32[]{:S(2)}) collective-permute-start(bf16[3,96,16,128]{3,2,1,0:T(8,128)(2,1)} %pad_maximum_fusion), channel_id=1, source_target_pairs={{0,96},{96,0},{1,97},{97,1},{2,98},{98,2},{3,99},{99,3},{4,100},{1... | collective-permute-start | bytes 3538952 | tf_op jit(solution)/shard_map/ppermute | solution.py:24
  95.3 37.1 %all-to-all-start.1 = ((bf16[96,16,128]{2,1,0:T(8,128)(2,1)}), bf16[96,16,128]{2,1,0:T(8,128)(2,1)}, u32[]{:S(2)}, u32[]{:S(2)}) async-start(bf16[96,16,128]{2,1,0:T(8,128)(2,1)} %select_convert_fusion), calls=%async_computation.1 | async-start | bytes 786432 | tf_op jit(solution)/shard_map/all_to_all | solution.py:182
  110.5 3.7 %collective-permute-start.7 = (bf16[96,16,128]{2,1,0:T(8,128)(2,1)S(1)}, bf16[96,16,128]{2,1,0:T(8,128)(2,1)}, u32[]{:S(2)}, u32[]{:S(2)}) collective-permute-start(bf16[96,16,128]{2,1,0:T(8,128)(2,1)S(1)} %all-to-all-done.refs_0_), channel_id=1, source_target_pairs={{0,96},{96,0},{1,97},{97,1},{2,98},{98,2},{3,99},{99,3},{4,100},{1... | collective-permute-start | bytes 1179656 | tf_op jit(solution)/shard_map/ppermute | solution.py:24
  114.2 1.0 copy-start.3
  134.2 10.6 %all-to-all-start.2 = ((f32[8,4,128]{2,1,0:T(4,128)}), f32[8,4,128]{2,1,0:T(4,128)S(1)}, u32[]{:S(2)}, u32[]{:S(2)}) async-start(f32[8,4,128]{2,1,0:T(4,128)} %broadcast_in_dim.27), calls=%async_computation.2 | async-start | bytes 32768 | tf_op jit(solution)/shard_map/all_to_all | solution.py:201

commit v5 on v2

--- a/solution.py
+++ b/solution.py
@@ -162,13 +162,13 @@
         compiler_params=pltpu.CompilerParams(vmem_limit_bytes=24 << 20),
         cost_estimate=pl.CostEstimate(flops=4 * tokens * width * LANES, bytes_accessed=8 << 20, transcendentals=0),
     )(pos, hidden_in, cotangent)
-    send, mine = lax.optimization_barrier((send, mine))
     got = swap(send)
     pair = [own[k].astype(f32) + got[k].astype(f32) for k in range(4)]
     moved = [shift_x(pair[k].astype(bf16), k) for k in range(1, 4)]
-
+    moved[0], mine = lax.optimization_barrier((moved[0], mine))
     held = [mine] + [shift_x(mine, k) for k in range(1, 4)]
     other = [swap(mine), swap(jnp.stack(held[1:]))]
+
 
     total = pair[0] + moved[0].astype(f32) + moved[1].astype(f32) + moved[2].astype(f32)
     gain_part = jnp.sum(mine.astype(f32) * total, axis=-1)[:, :USED].reshape(12, 8 * USED)
@@ -180,7 +180,7 @@
     pay = jnp.pad(pay, ((N_ZY - 8, 0), (USED, 0), (0, 0)))
     spare = lax.broadcasted_iota(jnp.int32, (1, BLK, 1), 1) >= USED
     chunk = jnp.where(spare, pay, total).astype(bf16)
-    sums = lax.all_to_all(chunk, ZY, 0, 0, tiled=True).astype(f32).sum(axis=0)
+    received = lax.all_to_all(chunk, ZY, 0, 0, tiled=True)
 
     key_rows, input_grad, gains = pl.pallas_call(
         rows_kernel,
@@ -196,8 +196,10 @@
         cost_estimate=pl.CostEstimate(flops=4 * tokens * width * LANES, bytes_accessed=10 << 20, transcendentals=0),
     )(pos, hidden_in, cotangent, inv, *held, *other)
 
+    sums = received.astype(f32).sum(axis=0)
     part = sums[USED:]
     parts = lax.all_to_all(jnp.broadcast_to(part, (8, 4, LANES)), ("c", "x"), 0, 0, tiled=True)
+    parts, gains = lax.optimization_barrier((parts, gains))
     both = parts.reshape(2, 4, 512)[:, :, :480].reshape(2, 4, 5, 4, 2, USED)
     by_row = 0.0
     for core in range(2):

time: 142 us -> 122 us (0.86)
  waiting for transfers between devices: 45.6 us -> 21.7 us
  other arithmetic: 6.88 us -> 10.2 us
  local copies, waits for them, and re-layouts: 7.89 us -> 5.37 us
  starting transfers between devices: 68.6 us -> 70.4 us
    ppermute x6, waiting for transfers between devices: 17.1 us -> 2.8 us  [shift_x(): return lax.ppermute(a, 'x', [(i, (i + k) % 4) for i in range(4)])]
    all_to_all x1, starting transfers between devices: 22.5 us -> 12.7 us  [local(): lax.all_to_all(jnp.broadcast_to(block, (N_ZY, BLK, LANES)), ZY, 0, 0, til...]
    all_to_all x1, waiting for transfers between devices: 14.5 us -> 9.28 us  [local(): lax.all_to_all(jnp.broadcast_to(block, (N_ZY, BLK, LANES)), ZY, 0, 0, til...]
    ppermute x3, starting transfers between devices: 12.1 us -> 17 us  [swap(): return lax.ppermute(a, 'c', [(0, 1), (1, 0)])]
    all_to_all x1, waiting for transfers between devices: 4.83 us -> 0.01 us  [local(): lax.all_to_all(jnp.broadcast_to(part, (8, 4, LANES)), ('c', 'x'), 0, 0, t...]
    all_to_all x1, starting transfers between devices: 6.92 us -> 10.5 us  [local(): received = lax.all_to_all(chunk, ZY, 0, 0, tiled=True)]
    unnamed x24 -> x10, local copies, waits for them, and re-layouts: 4.85 us -> 2.37 us
    all_to_all x1, starting transfers between devices: 8.1 us -> 10.2 us  [local(): lax.all_to_all(jnp.broadcast_to(part, (8, 4, LANES)), ('c', 'x'), 0, 0, t...]
  transfers between devices with their start and end apart: 12 -> 12, of which waited for: 9 -> 3; matrix products, arithmetic and copies ran while one was open for 4% -> 10% of each run, Pallas kernels for 8% -> 6%
where the time goes in v5:
time: 122 us; the launch traced here: 121 us
  starting transfers between devices  70.4 us (58%)
  waiting for transfers between devices  21.7 us (18%)
  Pallas kernels  12.2 us (10%)
  other arithmetic  10.2 us (8%)
  local copies, waits for them, and re-layouts  5.37 us (4%)
    ppermute x6, starting transfers between devices, shift_x(): return lax.ppermute(a, 'x', [(i, (i + k) % 4) for i in range(4)])  19.9 us
    ppermute x3, starting transfers between devices, swap(): return lax.ppermute(a, 'c', [(0, 1), (1, 0)])  17 us
    all_to_all x1, starting transfers between devices, local(): lax.all_to_all(jnp.broadcast_to(block, (N_ZY, BLK, LANES)), ZY, 0, 0, til...  12.7 us
    all_to_all x1, starting transfers between devices, local(): received = lax.all_to_all(chunk, ZY, 0, 0, tiled=True)  10.5 us
    all_to_all x1, starting transfers between devices, local(): lax.all_to_all(jnp.broadcast_to(part, (8, 4, LANES)), ('c', 'x'), 0, 0, t...  10.2 us
    all_to_all x1, waiting for transfers between devices, local(): received = lax.all_to_all(chunk, ZY, 0, 0, tiled=True)  9.58 us
    all_to_all x1, waiting for transfers between devices, local(): lax.all_to_all(jnp.broadcast_to(block, (N_ZY, BLK, LANES)), ZY, 0, 0, til...  9.28 us
    pallas_call x1, Pallas kernels, local(): pl.pallas_call(rows_kernel, out_shape=(jax.ShapeDtypeStruct((tokens, LANE...  7.67 us
  transfers between devices with their start and end apart: 12, of which 3 were waited for; matrix products, arithmetic and copies ran while one was open for 10% of the time, Pallas kernels for 6%

profile of v5, /device:TPU:1, one launch (start us, length us, event | category | flops | bytes accessed | tf_op | source)
XLA Modules:
  0.0 120.8 jit_solution(2038529174257089514)
XLA Ops:
  0.6 0.1 pad_add_fusion.6.pos_ref
  0.7 1.6 %copy-done = bf16[128,8192]{1,0:T(8,128)(2,1)S(1)} copy-done((bf16[128,8192]{1,0:T(8,128)(2,1)S(1)}, bf16[128,8192]{1,0:T(8,128)(2,1)}, u32[]{:S(2)}) %copy-start) | copy-done | bytes 2097176
  2.3 0.8 copy-done.2
  3.1 4.5 %shard_map.58 = (bf16[4,96,16,128]{3,2,1,0:T(8,128)(2,1)S(1)}, bf16[4,96,16,128]{3,2,1,0:T(8,128)(2,1)}, f32[128,128]{1,0:T(8,128)S(1)}) custom-call(s32[2]{0:T(128)S(1)} %pad_add_fusion.6.pos_ref, bf16[128,8192]{1,0:T(8,128)(2,1)S(1)} %copy-done, bf16[128,128]{1,0:T(8,128)(2,1)S(1)} %copy-done.2), custom_call_target="tpu_custom_call" | custom-call | flops 536870912 | bytes 8388608 | tf_op jit(solution)/shard_map/pallas_call | solution.py:156
  7.6 12.4 %collective-permute-start = (bf16[4,96,16,128]{3,2,1,0:T(8,128)(2,1)}, bf16[4,96,16,128]{3,2,1,0:T(8,128)(2,1)}, u32[]{:S(2)}, u32[]{:S(2)}) collective-permute-start(bf16[4,96,16,128]{3,2,1,0:T(8,128)(2,1)} %get-tuple-element.15), channel_id=1, source_target_pairs={{0,96},{96,0},{1,97},{97,1},{2,98},{98,2},{3,99},{99,3},{4,100},{1... | collective-permute-start | bytes 4718600 | tf_op jit(solution)/shard_map/ppermute | solution.py:24
  20.1 0.1 fusion.9
  20.2 0.8 broadcast_in_dim.25
  21.0 12.7 %all-to-all-start = ((bf16[96,16,128]{2,1,0:T(8,128)(2,1)}), bf16[96,16,128]{2,1,0:T(8,128)(2,1)S(1)}, u32[]{:S(2)}, u32[]{:S(2)}) async-start(bf16[96,16,128]{2,1,0:T(8,128)(2,1)} %broadcast_in_dim.25), calls=%async_computation | async-start | bytes 786432 | tf_op jit(solution)/shard_map/all_to_all | solution.py:153
  33.7 2.4 %fusion.3 = (bf16[96,16,128]{2,1,0:T(8,128)(2,1)}, bf16[96,16,128]{2,1,0:T(8,128)(2,1)}, bf16[96,16,128]{2,1,0:T(8,128)(2,1)S(1)}) fusion(bf16[4,96,16,128]{3,2,1,0:T(8,128)(2,1)} %collective-permute-done, bf16[4,96,16,128]{3,2,1,0:T(8,128)(2,1)S(1)} %get-tuple-element.14), kind=kLoop, calls=%fused_computation.11 | loop fusion | flops 2359296 | bytes 3538944 | tf_op jit(solution)/shard_map/convert_element_type | solution.py:167
  36.2 3.1 %collective-permute-start.1 = (bf16[96,16,128]{2,1,0:T(8,128)(2,1)S(1)}, bf16[96,16,128]{2,1,0:T(8,128)(2,1)S(1)}, u32[]{:S(2)}, u32[]{:S(2)}) collective-permute-start(bf16[96,16,128]{2,1,0:T(8,128)(2,1)S(1)} %get-tuple-element.25), channel_id=1, source_target_pairs={{0,1},{1,2},{2,3},{3,0},{4,5},{5,6},{6,7},{7,4},{8,9},{9,10},{10,1... | collective-permute-start | bytes 1179656 | tf_op jit(solution)/shard_map/ppermute | solution.py:28
  39.3 4.4 %collective-permute-start.7 = (bf16[96,16,128]{2,1,0:T(8,128)(2,1)}, bf16[96,16,128]{2,1,0:T(8,128)(2,1)}, u32[]{:S(2)}, u32[]{:S(2)}) collective-permute-start(bf16[96,16,128]{2,1,0:T(8,128)(2,1)} %get-tuple-element.23), channel_id=1, source_target_pairs={{0,2},{1,3},{2,0},{3,1},{4,6},{5,7},{6,4},{7,5},{8,10},{9,11},{10,... | collective-permute-start | bytes 1179656 | tf_op jit(solution)/shard_map/ppermute | solution.py:28
  43.6 3.1 %collective-permute-start.8 = (bf16[96,16,128]{2,1,0:T(8,128)(2,1)}, bf16[96,16,128]{2,1,0:T(8,128)(2,1)}, u32[]{:S(2)}, u32[]{:S(2)}) collective-permute-start(bf16[96,16,128]{2,1,0:T(8,128)(2,1)} %get-tuple-element.24), channel_id=1, source_target_pairs={{0,3},{1,0},{2,1},{3,2},{4,7},{5,4},{6,5},{7,6},{8,11},{9,8},{10,9... | collective-permute-start | bytes 1179656 | tf_op jit(solution)/shard_map/ppermute | solution.py:28
  46.7 9.3 %all-to-all-done.refs_0_ = bf16[96,16,128]{2,1,0:T(8,128)(2,1)S(1)} async-done(((bf16[96,16,128]{2,1,0:T(8,128)(2,1)}), bf16[96,16,128]{2,1,0:T(8,128)(2,1)S(1)}, u32[]{:S(2)}, u32[]{:S(2)}) %all-to-all-start) | async-done | bytes 393248 | tf_op jit(solution)/shard_map/all_to_all | solution.py:153
  56.0 4.4 %collective-permute-start.4 = (bf16[96,16,128]{2,1,0:T(8,128)(2,1)S(1)}, bf16[96,16,128]{2,1,0:T(8,128)(2,1)S(1)}, u32[]{:S(2)}, u32[]{:S(2)}) collective-permute-start(bf16[96,16,128]{2,1,0:T(8,128)(2,1)S(1)} %all-to-all-done.refs_0_), channel_id=1, source_target_pairs={{0,3},{1,0},{2,1},{3,2},{4,7},{5,4},{6,5},{7,6},{8,11},{9,8},{10,9... | collective-permute-start | bytes 1179656 | tf_op jit(solution)/shard_map/ppermute | solution.py:28
  60.4 2.4 %collective-permute-start.3 = (bf16[96,16,128]{2,1,0:T(8,128)(2,1)S(1)}, bf16[96,16,128]{2,1,0:T(8,128)(2,1)S(1)}, u32[]{:S(2)}, u32[]{:S(2)}) collective-permute-start(bf16[96,16,128]{2,1,0:T(8,128)(2,1)S(1)} %all-to-all-done.refs_0_), channel_id=1, source_target_pairs={{0,2},{1,3},{2,0},{3,1},{4,6},{5,7},{6,4},{7,5},{8,10},{9,11},{10,... | collective-permute-start | bytes 1179656 | tf_op jit(solution)/shard_map/ppermute | solution.py:28
  62.8 2.5 %collective-permute-start.2 = (bf16[96,16,128]{2,1,0:T(8,128)(2,1)S(1)}, bf16[96,16,128]{2,1,0:T(8,128)(2,1)}, u32[]{:S(2)}, u32[]{:S(2)}) collective-permute-start(bf16[96,16,128]{2,1,0:T(8,128)(2,1)S(1)} %all-to-all-done.refs_0_), channel_id=1, source_target_pairs={{0,1},{1,2},{2,3},{3,0},{4,5},{5,6},{6,7},{7,4},{8,9},{9,10},{10,1... | collective-permute-start | bytes 1179656 | tf_op jit(solution)/shard_map/ppermute | solution.py:28
  65.4 0.0 collective-permute-done.8
  65.4 1.7 %multiply_reduce_fusion = bf16[96,16]{1,0:T(8,128)(2,1)S(1)} fusion(bf16[96,16,128]{2,1,0:T(8,128)(2,1)S(1)} %all-to-all-done.refs_0_, bf16[96,16,128]{2,1,0:T(8,128)(2,1)} %collective-permute-done.8, bf16[96,16,128]{2,1,0:T(8,128)(2,1)} %collective-permute-done.7, bf16[96,16,128]{2,1,0:T(8,128)(2,1)S(1)} %collective-permute-done.1, ...), kind=kLoop, calls=%fused_computation.6 | loop fusion | flops 2357760 | bytes 2362368 | tf_op jit(solution)/shard_map/reduce_sum | solution.py:174
  67.1 0.1 reshape.78
  67.2 0.1 reshape.80
  67.3 0.1 reshape.79
  67.4 0.1 pad_maximum_fusion.1
  67.5 2.3 %select_convert_fusion = bf16[96,16,128]{2,1,0:T(8,128)(2,1)} fusion(bf16[8,4,128]{2,1,0:T(4,128)(2,1)S(1)} %bitcast.71, pred[16]{0:T(512)(128)(4,1)S(1)} %iota_compare_fusion, bf16[96,16,128]{2,1,0:T(8,128)(2,1)} %collective-permute-done.8, bf16[96,16,128]{2,1,0:T(8,128)(2,1)} %collective-permute-done.7, bf16[96,16,128]{2,1,0:T(8,128)(2,1)S(1)} %collective-permute-done.1, ...), kind=kLoop, calls=%fused_computation.5 | loop fusion | flops 1966080 | bytes 2367504 | tf_op jit(solution)/shard_map/convert_element_type | solution.py:182
  69.8 10.5 %all-to-all-start.1 = ((bf16[96,16,128]{2,1,0:T(8,128)(2,1)}), bf16[96,16,128]{2,1,0:T(8,128)(2,1)}, u32[]{:S(2)}, u32[]{:S(2)}) async-start(bf16[96,16,128]{2,1,0:T(8,128)(2,1)} %select_convert_fusion), calls=%async_computation.1 | async-start | bytes 786432 | tf_op jit(solution)/shard_map/all_to_all | solution.py:183
  80.4 0.0 copy-start.1
  80.4 0.0 copy-start.3
  80.4 0.0 collective-permute-done.4.refs_3_
  80.4 0.0 collective-permute-done.3.refs_2_
  80.4 2.8 %collective-permute-done.2.refs_1_ = bf16[96,16,128]{2,1,0:T(8,128)(2,1)} collective-permute-done((bf16[96,16,128]{2,1,0:T(8,128)(2,1)S(1)}, bf16[96,16,128]{2,1,0:T(8,128)(2,1)}, u32[]{:S(2)}, u32[]{:S(2)}) %collective-permute-start.2) | collective-permute-done | bytes 393248 | tf_op jit(solution)/shard_map/ppermute | solution.py:28
  83.2 2.1 %pad_maximum_fusion = bf16[3,96,16,128]{3,2,1,0:T(8,128)(2,1)} fusion(bf16[1,96,16,128]{3,2,1,0:T(8,128)(2,1)S(1)} %bitcast.67, bf16[1,96,16,128]{3,2,1,0:T(8,128)(2,1)S(1)} %bitcast.68, bf16[1,96,16,128]{3,2,1,0:T(8,128)(2,1)} %bitcast.4), kind=kLoop, calls=%fused_computation | loop fusion | flops 1179648 | bytes 2359296 | tf_op jit(solution)/shard_map/stack | solution.py:170
  85.3 2.7 %collective-permute-start.6 = (bf16[3,96,16,128]{3,2,1,0:T(8,128)(2,1)}, bf16[3,96,16,128]{3,2,1,0:T(8,128)(2,1)}, u32[]{:S(2)}, u32[]{:S(2)}) collective-permute-start(bf16[3,96,16,128]{3,2,1,0:T(8,128)(2,1)} %pad_maximum_fusion), channel_id=1, source_target_pairs={{0,96},{96,0},{1,97},{97,1},{2,98},{98,2},{3,99},{99,3},{4,100},{1... | collective-permute-start | bytes 3538952 | tf_op jit(solution)/shard_map/ppermute | solution.py:24
  88.1 1.9 %collective-permute-start.5 = (bf16[96,16,128]{2,1,0:T(8,128)(2,1)S(1)}, bf16[96,16,128]{2,1,0:T(8,128)(2,1)}, u32[]{:S(2)}, u32[]{:S(2)}) collective-permute-start(bf16[96,16,128]{2,1,0:T(8,128)(2,1)S(1)} %all-to-all-done.refs_0_), channel_id=1, source_target_pairs={{0,96},{96,0},{1,97},{97,1},{2,98},{98,2},{3,99},{99,3},{4,100},{1... | collective-permute-start | bytes 1179656 | tf_op jit(solution)/shard_map/ppermute | solution.py:24
  90.0 9.6 %all-to-all-done.1 = bf16[96,16,128]{2,1,0:T(8,128)(2,1)} async-done(((bf16[96,16,128]{2,1,0:T(8,128)(2,1)}), bf16[96,16,128]{2,1,0:T(8,128)(2,1)}, u32[]{:S(2)}, u32[]{:S(2)}) %all-to-all-start.1) | async-done | bytes 393248 | tf_op jit(solution)/shard_map/all_to_all | solution.py:183
  99.6 1.1 convert_reduce_fusion
  100.7 0.6 broadcast_in_dim.27
  101.3 10.2 %all-to-all-start.2 = ((f32[8,4,128]{2,1,0:T(4,128)}), f32[8,4,128]{2,1,0:T(4,128)S(1)}, u32[]{:S(2)}, u32[]{:S(2)}) async-start(f32[8,4,128]{2,1,0:T(4,128)} %broadcast_in_dim.27), calls=%async_computation.2 | async-start | bytes 32768 | tf_op jit(solution)/shard_map/all_to_all | solution.py:201
  111.6 0.0 collective-permute-done.5.refs_4_
  111.6 0.0 collective-permute-done.6.refs_5_
  111.6 7.7 %shard_map.59 = (bf16[128,128]{1,0:T(8,128)(2,1)}, bf16[128,8192]{1,0:T(8,128)(2,1)}, f32[64,128]{1,0:T(8,128)S(1)}) custom-call(s32[2]{0:T(128)S(1)} %pad_add_fusion.6.pos_ref, bf16[128,8192]{1,0:T(8,128)(2,1)S(1)} %copy-done.1, bf16[128,128]{1,0:T(8,128)(2,1)S(1)} %copy-done.3, f32[128,128]{1,0:T(8,128)S(1)} %get-tuple-element.13.inv_ref, ...), custom_call_target="tpu_custom_call" | custom-call | flops 536870912 | bytes 10485760 | tf_op jit(solution)/shard_map/pallas_call | solution.py:185
  119.3 0.0 all-to-all-done.2
  119.3 0.1 pad_dynamic-slice_fusion
  119.4 0.1 fusion.8
  119.4 0.3 reshape.85
  119.7 0.1 slice_bitcast_fusion.7
  119.8 0.2 fusion.5
  120.0 0.1 reshape.86
  120.1 0.1 fusion.7
  120.2 0.6 reshape.87
  (19 shorter events, 0.1 us)
Async XLA Ops:
  0.6 19.4 %copy-start.4 = (bf16[1,1376]{1,0:T(2,128)(2,1)S(1)}, bf16[1,1376]{1,0:T(2,128)(2,1)}, u32[]{:S(2)}) copy-start(bf16[1,1376]{1,0:T(2,128)(2,1)} %param.5) | copy-start | bytes 8260
  0.7 1.6 %copy-start = (bf16[128,8192]{1,0:T(8,128)(2,1)S(1)}, bf16[128,8192]{1,0:T(8,128)(2,1)}, u32[]{:S(2)}) copy-start(bf16[128,8192]{1,0:T(8,128)(2,1)} %hidden_ref.3) | copy-start | bytes 6291460
  2.3 0.8 copy-start.2
  7.6 26.1 %collective-permute-start = (bf16[4,96,16,128]{3,2,1,0:T(8,128)(2,1)}, bf16[4,96,16,128]{3,2,1,0:T(8,128)(2,1)}, u32[]{:S(2)}, u32[]{:S(2)}) collective-permute-start(bf16[4,96,16,128]{3,2,1,0:T(8,128)(2,1)} %get-tuple-element.15), channel_id=1, source_target_pairs={{0,96},{96,0},{1,97},{97,1},{2,98},{98,2},{3,99},{99,3},{4,100},{1... | collective-permute-start | bytes 4718600 | tf_op jit(solution)/shard_map/ppermute | solution.py:24
  21.0 35.0 %all-to-all-start = ((bf16[96,16,128]{2,1,0:T(8,128)(2,1)}), bf16[96,16,128]{2,1,0:T(8,128)(2,1)S(1)}, u32[]{:S(2)}, u32[]{:S(2)}) async-start(bf16[96,16,128]{2,1,0:T(8,128)(2,1)} %broadcast_in_dim.25), calls=%async_computation | async-start | bytes 786432 | tf_op jit(solution)/shard_map/all_to_all | solution.py:153
  36.2 19.9 %collective-permute-start.1 = (bf16[96,16,128]{2,1,0:T(8,128)(2,1)S(1)}, bf16[96,16,128]{2,1,0:T(8,128)(2,1)S(1)}, u32[]{:S(2)}, u32[]{:S(2)}) collective-permute-start(bf16[96,16,128]{2,1,0:T(8,128)(2,1)S(1)} %get-tuple-element.25), channel_id=1, source_target_pairs={{0,1},{1,2},{2,3},{3,0},{4,5},{5,6},{6,7},{7,4},{8,9},{9,10},{10,1... | collective-permute-start | bytes 1179656 | tf_op jit(solution)/shard_map/ppermute | solution.py:28
  39.3 26.1 %collective-permute-start.7 = (bf16[96,16,128]{2,1,0:T(8,128)(2,1)}, bf16[96,16,128]{2,1,0:T(8,128)(2,1)}, u32[]{:S(2)}, u32[]{:S(2)}) collective-permute-start(bf16[96,16,128]{2,1,0:T(8,128)(2,1)} %get-tuple-element.23), channel_id=1, source_target_pairs={{0,2},{1,3},{2,0},{3,1},{4,6},{5,7},{6,4},{7,5},{8,10},{9,11},{10,... | collective-permute-start | bytes 1179656 | tf_op jit(solution)/shard_map/ppermute | solution.py:28
  43.6 21.7 %collective-permute-start.8 = (bf16[96,16,128]{2,1,0:T(8,128)(2,1)}, bf16[96,16,128]{2,1,0:T(8,128)(2,1)}, u32[]{:S(2)}, u32[]{:S(2)}) collective-permute-start(bf16[96,16,128]{2,1,0:T(8,128)(2,1)} %get-tuple-element.24), channel_id=1, source_target_pairs={{0,3},{1,0},{2,1},{3,2},{4,7},{5,4},{6,5},{7,6},{8,11},{9,8},{10,9... | collective-permute-start | bytes 1179656 | tf_op jit(solution)/shard_map/ppermute | solution.py:28
  56.0 24.4 %collective-permute-start.4 = (bf16[96,16,128]{2,1,0:T(8,128)(2,1)S(1)}, bf16[96,16,128]{2,1,0:T(8,128)(2,1)S(1)}, u32[]{:S(2)}, u32[]{:S(2)}) collective-permute-start(bf16[96,16,128]{2,1,0:T(8,128)(2,1)S(1)} %all-to-all-done.refs_0_), channel_id=1, source_target_pairs={{0,3},{1,0},{2,1},{3,2},{4,7},{5,4},{6,5},{7,6},{8,11},{9,8},{10,9... | collective-permute-start | bytes 1179656 | tf_op jit(solution)/shard_map/ppermute | solution.py:28
  60.4 20.0 %collective-permute-start.3 = (bf16[96,16,128]{2,1,0:T(8,128)(2,1)S(1)}, bf16[96,16,128]{2,1,0:T(8,128)(2,1)S(1)}, u32[]{:S(2)}, u32[]{:S(2)}) collective-permute-start(bf16[96,16,128]{2,1,0:T(8,128)(2,1)S(1)} %all-to-all-done.refs_0_), channel_id=1, source_target_pairs={{0,2},{1,3},{2,0},{3,1},{4,6},{5,7},{6,4},{7,5},{8,10},{9,11},{10,... | collective-permute-start | bytes 1179656 | tf_op jit(solution)/shard_map/ppermute | solution.py:28
  62.8 20.4 %collective-permute-start.2 = (bf16[96,16,128]{2,1,0:T(8,128)(2,1)S(1)}, bf16[96,16,128]{2,1,0:T(8,128)(2,1)}, u32[]{:S(2)}, u32[]{:S(2)}) collective-permute-start(bf16[96,16,128]{2,1,0:T(8,128)(2,1)S(1)} %all-to-all-done.refs_0_), channel_id=1, source_target_pairs={{0,1},{1,2},{2,3},{3,0},{4,5},{5,6},{6,7},{7,4},{8,9},{9,10},{10,1... | collective-permute-start | bytes 1179656 | tf_op jit(solution)/shard_map/ppermute | solution.py:28
  69.8 29.8 %all-to-all-start.1 = ((bf16[96,16,128]{2,1,0:T(8,128)(2,1)}), bf16[96,16,128]{2,1,0:T(8,128)(2,1)}, u32[]{:S(2)}, u32[]{:S(2)}) async-start(bf16[96,16,128]{2,1,0:T(8,128)(2,1)} %select_convert_fusion), calls=%async_computation.1 | async-start | bytes 786432 | tf_op jit(solution)/shard_map/all_to_all | solution.py:183
  80.4 31.2 %copy-start.1 = (bf16[128,8192]{1,0:T(8,128)(2,1)S(1)}, bf16[128,8192]{1,0:T(8,128)(2,1)}, u32[]{:S(2)}) copy-start(bf16[128,8192]{1,0:T(8,128)(2,1)} %hidden_ref.3) | copy-start | bytes 6291460
  80.4 31.2 %copy-start.3 = (bf16[128,128]{1,0:T(8,128)(2,1)S(1)}, bf16[128,128]{1,0:T(8,128)(2,1)}, u32[]{:S(2)}) copy-start(bf16[128,128]{1,0:T(8,128)(2,1)} %cot_ref.3) | copy-start | bytes 98308
  85.3 26.2 %collective-permute-start.6 = (bf16[3,96,16,128]{3,2,1,0:T(8,128)(2,1)}, bf16[3,96,16,128]{3,2,1,0:T(8,128)(2,1)}, u32[]{:S(2)}, u32[]{:S(2)}) collective-permute-start(bf16[3,96,16,128]{3,2,1,0:T(8,128)(2,1)} %pad_maximum_fusion), channel_id=1, source_target_pairs={{0,96},{96,0},{1,97},{97,1},{2,98},{98,2},{3,99},{99,3},{4,100},{1... | collective-permute-start | bytes 3538952 | tf_op jit(solution)/shard_map/ppermute | solution.py:24
  88.1 23.5 %collective-permute-start.5 = (bf16[96,16,128]{2,1,0:T(8,128)(2,1)S(1)}, bf16[96,16,128]{2,1,0:T(8,128)(2,1)}, u32[]{:S(2)}, u32[]{:S(2)}) collective-permute-start(bf16[96,16,128]{2,1,0:T(8,128)(2,1)S(1)} %all-to-all-done.refs_0_), channel_id=1, source_target_pairs={{0,96},{96,0},{1,97},{97,1},{2,98},{98,2},{3,99},{99,3},{4,100},{1... | collective-permute-start | bytes 1179656 | tf_op jit(solution)/shard_map/ppermute | solution.py:24
  101.3 17.9 %all-to-all-start.2 = ((f32[8,4,128]{2,1,0:T(4,128)}), f32[8,4,128]{2,1,0:T(4,128)S(1)}, u32[]{:S(2)}, u32[]{:S(2)}) async-start(f32[8,4,128]{2,1,0:T(4,128)} %broadcast_in_dim.27), calls=%async_computation.2 | async-start | bytes 32768 | tf_op jit(solution)/shard_map/all_to_all | solution.py:201

commit v6 on v5

--- a/solution.py
+++ b/solution.py
@@ -163,14 +163,17 @@
         cost_estimate=pl.CostEstimate(flops=4 * tokens * width * LANES, bytes_accessed=8 << 20, transcendentals=0),
     )(pos, hidden_in, cotangent)
     got = swap(send)
-    pair = [own[k].astype(f32) + got[k].astype(f32) for k in range(4)]
-    moved = [shift_x(pair[k].astype(bf16), k) for k in range(1, 4)]
-    moved[0], mine = lax.optimization_barrier((moved[0], mine))
+    moved = {}
+    for k in (2, 1, 3):
+        sent, got = lax.optimization_barrier(((own[k].astype(f32) + got[k].astype(f32)).astype(bf16), got))
+        moved[k] = shift_x(sent, k)
+    moved[2], mine = lax.optimization_barrier((moved[2], mine))
     held = [mine] + [shift_x(mine, k) for k in range(1, 4)]
     other = [swap(mine), swap(jnp.stack(held[1:]))]
 
 
-    total = pair[0] + moved[0].astype(f32) + moved[1].astype(f32) + moved[2].astype(f32)
+    total = own[0].astype(f32) + got[0].astype(f32)
+    total = total + moved[1].astype(f32) + moved[2].astype(f32) + moved[3].astype(f32)
     gain_part = jnp.sum(mine.astype(f32) * total, axis=-1)[:, :USED].reshape(12, 8 * USED)
     pays = [jnp.zeros((512,), f32)]
     for start in (0, 3, 7):

time: 122 us -> 121 us (level)
  other arithmetic: 10.2 us -> 12.6 us
  waiting for transfers between devices: 21.7 us -> 19.5 us
  starting transfers between devices: 70.4 us -> 69.1 us
    convert_element_type x1 -> x3, other arithmetic: 2.44 us -> 4.82 us  [local(): (own[k].astype(f32) + got[k].astype(f32)).astype(bf16)]
    all_to_all x1, waiting for transfers between devices: 9.28 us -> 7.51 us  [local(): lax.all_to_all(jnp.broadcast_to(block, (N_ZY, BLK, LANES)), ZY, 0, 0, til...]
    all_to_all x1, waiting for transfers between devices: 9.58 us -> 8.2 us  [local(): received = lax.all_to_all(chunk, ZY, 0, 0, tiled=True)]
  transfers between devices with their start and end apart: 12 -> 12, of which waited for: 3 -> 3; matrix products, arithmetic and copies ran while one was open for 10% -> 12% of each run, Pallas kernels for 6% -> 6%
where the time goes in v6:
time: 121 us; the launch traced here: 120 us
  starting transfers between devices  69.1 us (57%)
  waiting for transfers between devices  19.5 us (16%)
  other arithmetic  12.6 us (10%)
  Pallas kernels  12.2 us (10%)
  local copies, waits for them, and re-layouts  5.37 us (4%)
    ppermute x6, starting transfers between devices, shift_x(): return lax.ppermute(a, 'x', [(i, (i + k) % 4) for i in range(4)])  19.2 us
    ppermute x3, starting transfers between devices, swap(): return lax.ppermute(a, 'c', [(0, 1), (1, 0)])  16.9 us
    all_to_all x1, starting transfers between devices, local(): lax.all_to_all(jnp.broadcast_to(block, (N_ZY, BLK, LANES)), ZY, 0, 0, til...  12.7 us
    all_to_all x1, starting transfers between devices, local(): lax.all_to_all(jnp.broadcast_to(part, (8, 4, LANES)), ('c', 'x'), 0, 0, t...  10.7 us
    all_to_all x1, starting transfers between devices, local(): received = lax.all_to_all(chunk, ZY, 0, 0, tiled=True)  9.6 us
    all_to_all x1, waiting for transfers between devices, local(): received = lax.all_to_all(chunk, ZY, 0, 0, tiled=True)  8.2 us
    pallas_call x1, Pallas kernels, local(): pl.pallas_call(rows_kernel, out_shape=(jax.ShapeDtypeStruct((tokens, LANE...  7.67 us
    all_to_all x1, waiting for transfers between devices, local(): lax.all_to_all(jnp.broadcast_to(block, (N_ZY, BLK, LANES)), ZY, 0, 0, til...  7.51 us
  transfers between devices with their start and end apart: 12, of which 3 were waited for; matrix products, arithmetic and copies ran while one was open for 12% of the time, Pallas kernels for 6%

profile of v6, /device:TPU:1, one launch (start us, length us, event | category | flops | bytes accessed | tf_op | source)
XLA Modules:
  0.0 119.7 jit_solution(14312315708436030109)
XLA Ops:
  0.6 0.1 pad_add_fusion.6.pos_ref
  0.7 1.6 %copy-done = bf16[128,8192]{1,0:T(8,128)(2,1)S(1)} copy-done((bf16[128,8192]{1,0:T(8,128)(2,1)S(1)}, bf16[128,8192]{1,0:T(8,128)(2,1)}, u32[]{:S(2)}) %copy-start) | copy-done | bytes 2097176
  2.3 0.8 copy-done.2
  3.1 4.5 %shard_map.58 = (bf16[4,96,16,128]{3,2,1,0:T(8,128)(2,1)S(1)}, bf16[4,96,16,128]{3,2,1,0:T(8,128)(2,1)}, f32[128,128]{1,0:T(8,128)S(1)}) custom-call(s32[2]{0:T(128)S(1)} %pad_add_fusion.6.pos_ref, bf16[128,8192]{1,0:T(8,128)(2,1)S(1)} %copy-done, bf16[128,128]{1,0:T(8,128)(2,1)S(1)} %copy-done.2), custom_call_target="tpu_custom_call" | custom-call | flops 536870912 | bytes 8388608 | tf_op jit(solution)/shard_map/pallas_call | solution.py:156
  7.6 12.4 %collective-permute-start = (bf16[4,96,16,128]{3,2,1,0:T(8,128)(2,1)}, bf16[4,96,16,128]{3,2,1,0:T(8,128)(2,1)}, u32[]{:S(2)}, u32[]{:S(2)}) collective-permute-start(bf16[4,96,16,128]{3,2,1,0:T(8,128)(2,1)} %get-tuple-element.21), channel_id=1, source_target_pairs={{0,96},{96,0},{1,97},{97,1},{2,98},{98,2},{3,99},{99,3},{4,100},{1... | collective-permute-start | bytes 4718600 | tf_op jit(solution)/shard_map/ppermute | solution.py:24
  20.1 0.1 fusion.9
  20.2 0.8 broadcast_in_dim.25
  21.0 12.7 %all-to-all-start = ((bf16[96,16,128]{2,1,0:T(8,128)(2,1)}), bf16[96,16,128]{2,1,0:T(8,128)(2,1)S(1)}, u32[]{:S(2)}, u32[]{:S(2)}) async-start(bf16[96,16,128]{2,1,0:T(8,128)(2,1)} %broadcast_in_dim.25), calls=%async_computation | async-start | bytes 786432 | tf_op jit(solution)/shard_map/all_to_all | solution.py:153
  33.7 0.0 collective-permute-done
  33.7 1.1 fusion.2
  34.8 1.9 %fusion.3 = bf16[96,16,128]{2,1,0:T(8,128)(2,1)} fusion(bf16[4,96,16,128]{3,2,1,0:T(8,128)(2,1)} %collective-permute-done, bf16[4,96,16,128]{3,2,1,0:T(8,128)(2,1)S(1)} %get-tuple-element.20), kind=kLoop, calls=%fused_computation.11 | loop fusion | flops 786432 | bytes 1179648 | tf_op jit(solution)/shard_map/convert_element_type | solution.py:168
  36.7 4.6 %collective-permute-start.1 = (bf16[96,16,128]{2,1,0:T(8,128)(2,1)S(1)}, bf16[96,16,128]{2,1,0:T(8,128)(2,1)S(1)}, u32[]{:S(2)}, u32[]{:S(2)}) collective-permute-start(bf16[96,16,128]{2,1,0:T(8,128)(2,1)S(1)} %fusion.2), channel_id=1, source_target_pairs={{0,2},{1,3},{2,0},{3,1},{4,6},{5,7},{6,4},{7,5},{8,10},{9,11},{10,... | collective-permute-start | bytes 1179656 | tf_op jit(solution)/shard_map/ppermute | solution.py:28
  41.4 1.8 %fusion.4 = bf16[96,16,128]{2,1,0:T(8,128)(2,1)} fusion(bf16[4,96,16,128]{3,2,1,0:T(8,128)(2,1)} %collective-permute-done, bf16[4,96,16,128]{3,2,1,0:T(8,128)(2,1)S(1)} %get-tuple-element.20), kind=kLoop, calls=%fused_computation.12 | loop fusion | flops 786432 | bytes 1179648 | tf_op jit(solution)/shard_map/convert_element_type | solution.py:168
  43.2 2.8 %collective-permute-start.8 = (bf16[96,16,128]{2,1,0:T(8,128)(2,1)}, bf16[96,16,128]{2,1,0:T(8,128)(2,1)}, u32[]{:S(2)}, u32[]{:S(2)}) collective-permute-start(bf16[96,16,128]{2,1,0:T(8,128)(2,1)} %fusion.4), channel_id=1, source_target_pairs={{0,3},{1,0},{2,1},{3,2},{4,7},{5,4},{6,5},{7,6},{8,11},{9,8},{10,9... | collective-permute-start | bytes 1179656 | tf_op jit(solution)/shard_map/ppermute | solution.py:28
  46.0 2.5 %collective-permute-start.7 = (bf16[96,16,128]{2,1,0:T(8,128)(2,1)}, bf16[96,16,128]{2,1,0:T(8,128)(2,1)}, u32[]{:S(2)}, u32[]{:S(2)}) collective-permute-start(bf16[96,16,128]{2,1,0:T(8,128)(2,1)} %fusion.3), channel_id=1, source_target_pairs={{0,1},{1,2},{2,3},{3,0},{4,5},{5,6},{6,7},{7,4},{8,9},{9,10},{10,1... | collective-permute-start | bytes 1179656 | tf_op jit(solution)/shard_map/ppermute | solution.py:28
  48.5 7.5 %all-to-all-done.refs_0_ = bf16[96,16,128]{2,1,0:T(8,128)(2,1)S(1)} async-done(((bf16[96,16,128]{2,1,0:T(8,128)(2,1)}), bf16[96,16,128]{2,1,0:T(8,128)(2,1)S(1)}, u32[]{:S(2)}, u32[]{:S(2)}) %all-to-all-start) | async-done | bytes 393248 | tf_op jit(solution)/shard_map/all_to_all | solution.py:153
  56.0 0.0 collective-permute-done.1
  56.0 4.4 %collective-permute-start.4 = (bf16[96,16,128]{2,1,0:T(8,128)(2,1)S(1)}, bf16[96,16,128]{2,1,0:T(8,128)(2,1)S(1)}, u32[]{:S(2)}, u32[]{:S(2)}) collective-permute-start(bf16[96,16,128]{2,1,0:T(8,128)(2,1)S(1)} %all-to-all-done.refs_0_), channel_id=1, source_target_pairs={{0,3},{1,0},{2,1},{3,2},{4,7},{5,4},{6,5},{7,6},{8,11},{9,8},{10,9... | collective-permute-start | bytes 1179656 | tf_op jit(solution)/shard_map/ppermute | solution.py:28
  60.4 2.4 %collective-permute-start.3 = (bf16[96,16,128]{2,1,0:T(8,128)(2,1)S(1)}, bf16[96,16,128]{2,1,0:T(8,128)(2,1)S(1)}, u32[]{:S(2)}, u32[]{:S(2)}) collective-permute-start(bf16[96,16,128]{2,1,0:T(8,128)(2,1)S(1)} %all-to-all-done.refs_0_), channel_id=1, source_target_pairs={{0,2},{1,3},{2,0},{3,1},{4,6},{5,7},{6,4},{7,5},{8,10},{9,11},{10,... | collective-permute-start | bytes 1179656 | tf_op jit(solution)/shard_map/ppermute | solution.py:28
  62.8 2.5 %collective-permute-start.2 = (bf16[96,16,128]{2,1,0:T(8,128)(2,1)S(1)}, bf16[96,16,128]{2,1,0:T(8,128)(2,1)}, u32[]{:S(2)}, u32[]{:S(2)}) collective-permute-start(bf16[96,16,128]{2,1,0:T(8,128)(2,1)S(1)} %all-to-all-done.refs_0_), channel_id=1, source_target_pairs={{0,1},{1,2},{2,3},{3,0},{4,5},{5,6},{6,7},{7,4},{8,9},{9,10},{10,1... | collective-permute-start | bytes 1179656 | tf_op jit(solution)/shard_map/ppermute | solution.py:28
  65.4 0.0 collective-permute-done.8
  65.4 0.0 collective-permute-done.7
  65.4 1.6 %multiply_reduce_fusion = bf16[96,16]{1,0:T(8,128)(2,1)S(1)} fusion(bf16[96,16,128]{2,1,0:T(8,128)(2,1)S(1)} %all-to-all-done.refs_0_, bf16[96,16,128]{2,1,0:T(8,128)(2,1)} %collective-permute-done.8, bf16[96,16,128]{2,1,0:T(8,128)(2,1)S(1)} %collective-permute-done.1, bf16[96,16,128]{2,1,0:T(8,128)(2,1)} %collective-permute-done.7, ...), kind=kLoop, calls=%fused_computation.6 | loop fusion | flops 2357760 | bytes 2362368 | tf_op jit(solution)/shard_map/reduce_sum | solution.py:177
  67.0 0.1 reshape.78
  67.2 0.1 reshape.80
  67.3 0.1 reshape.79
  67.4 0.1 pad_maximum_fusion.1
  67.5 2.3 %select_convert_fusion = bf16[96,16,128]{2,1,0:T(8,128)(2,1)} fusion(bf16[8,4,128]{2,1,0:T(4,128)(2,1)S(1)} %bitcast.71, pred[16]{0:T(512)(128)(4,1)S(1)} %iota_compare_fusion, bf16[96,16,128]{2,1,0:T(8,128)(2,1)} %collective-permute-done.8, bf16[96,16,128]{2,1,0:T(8,128)(2,1)S(1)} %collective-permute-done.1, bf16[96,16,128]{2,1,0:T(8,128)(2,1)} %collective-permute-done.7, ...), kind=kLoop, calls=%fused_computation.5 | loop fusion | flops 1966080 | bytes 2367504 | tf_op jit(solution)/shard_map/convert_element_type | solution.py:185
  69.8 9.6 %all-to-all-start.1 = ((bf16[96,16,128]{2,1,0:T(8,128)(2,1)}), bf16[96,16,128]{2,1,0:T(8,128)(2,1)}, u32[]{:S(2)}, u32[]{:S(2)}) async-start(bf16[96,16,128]{2,1,0:T(8,128)(2,1)} %select_convert_fusion), calls=%async_computation.1 | async-start | bytes 786432 | tf_op jit(solution)/shard_map/all_to_all | solution.py:186
  79.4 0.0 copy-start.1
  79.4 0.0 copy-start.3
  79.4 3.8 %collective-permute-done.2.refs_1_ = bf16[96,16,128]{2,1,0:T(8,128)(2,1)} collective-permute-done((bf16[96,16,128]{2,1,0:T(8,128)(2,1)S(1)}, bf16[96,16,128]{2,1,0:T(8,128)(2,1)}, u32[]{:S(2)}, u32[]{:S(2)}) %collective-permute-start.2) | collective-permute-done | bytes 393248 | tf_op jit(solution)/shard_map/ppermute | solution.py:28
  83.2 2.1 %pad_maximum_fusion = bf16[3,96,16,128]{3,2,1,0:T(8,128)(2,1)} fusion(bf16[1,96,16,128]{3,2,1,0:T(8,128)(2,1)S(1)} %bitcast.67, bf16[1,96,16,128]{3,2,1,0:T(8,128)(2,1)S(1)} %bitcast.68, bf16[1,96,16,128]{3,2,1,0:T(8,128)(2,1)} %bitcast.4), kind=kLoop, calls=%fused_computation | loop fusion | flops 1179648 | bytes 2359296 | tf_op jit(solution)/shard_map/stack | solution.py:172
  85.3 2.6 %collective-permute-start.6 = (bf16[3,96,16,128]{3,2,1,0:T(8,128)(2,1)}, bf16[3,96,16,128]{3,2,1,0:T(8,128)(2,1)}, u32[]{:S(2)}, u32[]{:S(2)}) collective-permute-start(bf16[3,96,16,128]{3,2,1,0:T(8,128)(2,1)} %pad_maximum_fusion), channel_id=1, source_target_pairs={{0,96},{96,0},{1,97},{97,1},{2,98},{98,2},{3,99},{99,3},{4,100},{1... | collective-permute-start | bytes 3538952 | tf_op jit(solution)/shard_map/ppermute | solution.py:24
  87.9 1.9 %collective-permute-start.5 = (bf16[96,16,128]{2,1,0:T(8,128)(2,1)S(1)}, bf16[96,16,128]{2,1,0:T(8,128)(2,1)}, u32[]{:S(2)}, u32[]{:S(2)}) collective-permute-start(bf16[96,16,128]{2,1,0:T(8,128)(2,1)S(1)} %all-to-all-done.refs_0_), channel_id=1, source_target_pairs={{0,96},{96,0},{1,97},{97,1},{2,98},{98,2},{3,99},{99,3},{4,100},{1... | collective-permute-start | bytes 1179656 | tf_op jit(solution)/shard_map/ppermute | solution.py:24
  89.9 8.2 %all-to-all-done.1 = bf16[96,16,128]{2,1,0:T(8,128)(2,1)} async-done(((bf16[96,16,128]{2,1,0:T(8,128)(2,1)}), bf16[96,16,128]{2,1,0:T(8,128)(2,1)}, u32[]{:S(2)}, u32[]{:S(2)}) %all-to-all-start.1) | async-done | bytes 393248 | tf_op jit(solution)/shard_map/all_to_all | solution.py:186
  98.1 1.1 convert_reduce_fusion
  99.2 0.6 broadcast_in_dim.27
  99.8 10.7 %all-to-all-start.2 = ((f32[8,4,128]{2,1,0:T(4,128)}), f32[8,4,128]{2,1,0:T(4,128)S(1)}, u32[]{:S(2)}, u32[]{:S(2)}) async-start(f32[8,4,128]{2,1,0:T(4,128)} %broadcast_in_dim.27), calls=%async_computation.2 | async-start | bytes 32768 | tf_op jit(solution)/shard_map/all_to_all | solution.py:204
  110.5 7.7 %shard_map.59 = (bf16[128,128]{1,0:T(8,128)(2,1)}, bf16[128,8192]{1,0:T(8,128)(2,1)}, f32[64,128]{1,0:T(8,128)S(1)}) custom-call(s32[2]{0:T(128)S(1)} %pad_add_fusion.6.pos_ref, bf16[128,8192]{1,0:T(8,128)(2,1)S(1)} %copy-done.1, bf16[128,128]{1,0:T(8,128)(2,1)S(1)} %copy-done.3, f32[128,128]{1,0:T(8,128)S(1)} %get-tuple-element.19.inv_ref, ...), custom_call_target="tpu_custom_call" | custom-call | flops 536870912 | bytes 10485760 | tf_op jit(solution)/shard_map/pallas_call | solution.py:188
  118.2 0.1 pad_dynamic-slice_fusion
  118.3 0.1 fusion.8
  118.4 0.3 reshape.85
  118.6 0.1 slice_bitcast_fusion.7
  118.7 0.2 fusion.5
  118.9 0.1 reshape.86
  119.0 0.1 fusion.7
  119.1 0.6 reshape.87
  (21 shorter events, 0.1 us)
Async XLA Ops:
  0.6 19.4 %copy-start.4 = (bf16[1,1376]{1,0:T(2,128)(2,1)S(1)}, bf16[1,1376]{1,0:T(2,128)(2,1)}, u32[]{:S(2)}) copy-start(bf16[1,1376]{1,0:T(2,128)(2,1)} %param.5) | copy-start | bytes 8260
  0.7 1.6 %copy-start = (bf16[128,8192]{1,0:T(8,128)(2,1)S(1)}, bf16[128,8192]{1,0:T(8,128)(2,1)}, u32[]{:S(2)}) copy-start(bf16[128,8192]{1,0:T(8,128)(2,1)} %hidden_ref.3) | copy-start | bytes 6291460
  2.3 0.8 copy-start.2
  7.6 26.1 %collective-permute-start = (bf16[4,96,16,128]{3,2,1,0:T(8,128)(2,1)}, bf16[4,96,16,128]{3,2,1,0:T(8,128)(2,1)}, u32[]{:S(2)}, u32[]{:S(2)}) collective-permute-start(bf16[4,96,16,128]{3,2,1,0:T(8,128)(2,1)} %get-tuple-element.21), channel_id=1, source_target_pairs={{0,96},{96,0},{1,97},{97,1},{2,98},{98,2},{3,99},{99,3},{4,100},{1... | collective-permute-start | bytes 4718600 | tf_op jit(solution)/shard_map/ppermute | solution.py:24
  21.0 35.0 %all-to-all-start = ((bf16[96,16,128]{2,1,0:T(8,128)(2,1)}), bf16[96,16,128]{2,1,0:T(8,128)(2,1)S(1)}, u32[]{:S(2)}, u32[]{:S(2)}) async-start(bf16[96,16,128]{2,1,0:T(8,128)(2,1)} %broadcast_in_dim.25), calls=%async_computation | async-start | bytes 786432 | tf_op jit(solution)/shard_map/all_to_all | solution.py:153
  36.7 19.3 %collective-permute-start.1 = (bf16[96,16,128]{2,1,0:T(8,128)(2,1)S(1)}, bf16[96,16,128]{2,1,0:T(8,128)(2,1)S(1)}, u32[]{:S(2)}, u32[]{:S(2)}) collective-permute-start(bf16[96,16,128]{2,1,0:T(8,128)(2,1)S(1)} %fusion.2), channel_id=1, source_target_pairs={{0,2},{1,3},{2,0},{3,1},{4,6},{5,7},{6,4},{7,5},{8,10},{9,11},{10,... | collective-permute-start | bytes 1179656 | tf_op jit(solution)/shard_map/ppermute | solution.py:28
  43.2 22.2 %collective-permute-start.8 = (bf16[96,16,128]{2,1,0:T(8,128)(2,1)}, bf16[96,16,128]{2,1,0:T(8,128)(2,1)}, u32[]{:S(2)}, u32[]{:S(2)}) collective-permute-start(bf16[96,16,128]{2,1,0:T(8,128)(2,1)} %fusion.4), channel_id=1, source_target_pairs={{0,3},{1,0},{2,1},{3,2},{4,7},{5,4},{6,5},{7,6},{8,11},{9,8},{10,9... | collective-permute-start | bytes 1179656 | tf_op jit(solution)/shard_map/ppermute | solution.py:28
  46.0 19.4 %collective-permute-start.7 = (bf16[96,16,128]{2,1,0:T(8,128)(2,1)}, bf16[96,16,128]{2,1,0:T(8,128)(2,1)}, u32[]{:S(2)}, u32[]{:S(2)}) collective-permute-start(bf16[96,16,128]{2,1,0:T(8,128)(2,1)} %fusion.3), channel_id=1, source_target_pairs={{0,1},{1,2},{2,3},{3,0},{4,5},{5,6},{6,7},{7,4},{8,9},{9,10},{10,1... | collective-permute-start | bytes 1179656 | tf_op jit(solution)/shard_map/ppermute | solution.py:28
  56.0 23.4 %collective-permute-start.4 = (bf16[96,16,128]{2,1,0:T(8,128)(2,1)S(1)}, bf16[96,16,128]{2,1,0:T(8,128)(2,1)S(1)}, u32[]{:S(2)}, u32[]{:S(2)}) collective-permute-start(bf16[96,16,128]{2,1,0:T(8,128)(2,1)S(1)} %all-to-all-done.refs_0_), channel_id=1, source_target_pairs={{0,3},{1,0},{2,1},{3,2},{4,7},{5,4},{6,5},{7,6},{8,11},{9,8},{10,9... | collective-permute-start | bytes 1179656 | tf_op jit(solution)/shard_map/ppermute | solution.py:28
  60.4 19.0 %collective-permute-start.3 = (bf16[96,16,128]{2,1,0:T(8,128)(2,1)S(1)}, bf16[96,16,128]{2,1,0:T(8,128)(2,1)S(1)}, u32[]{:S(2)}, u32[]{:S(2)}) collective-permute-start(bf16[96,16,128]{2,1,0:T(8,128)(2,1)S(1)} %all-to-all-done.refs_0_), channel_id=1, source_target_pairs={{0,2},{1,3},{2,0},{3,1},{4,6},{5,7},{6,4},{7,5},{8,10},{9,11},{10,... | collective-permute-start | bytes 1179656 | tf_op jit(solution)/shard_map/ppermute | solution.py:28
  62.8 20.4 %collective-permute-start.2 = (bf16[96,16,128]{2,1,0:T(8,128)(2,1)S(1)}, bf16[96,16,128]{2,1,0:T(8,128)(2,1)}, u32[]{:S(2)}, u32[]{:S(2)}) collective-permute-start(bf16[96,16,128]{2,1,0:T(8,128)(2,1)S(1)} %all-to-all-done.refs_0_), channel_id=1, source_target_pairs={{0,1},{1,2},{2,3},{3,0},{4,5},{5,6},{6,7},{7,4},{8,9},{9,10},{10,1... | collective-permute-start | bytes 1179656 | tf_op jit(solution)/shard_map/ppermute | solution.py:28
  69.8 28.3 %all-to-all-start.1 = ((bf16[96,16,128]{2,1,0:T(8,128)(2,1)}), bf16[96,16,128]{2,1,0:T(8,128)(2,1)}, u32[]{:S(2)}, u32[]{:S(2)}) async-start(bf16[96,16,128]{2,1,0:T(8,128)(2,1)} %select_convert_fusion), calls=%async_computation.1 | async-start | bytes 786432 | tf_op jit(solution)/shard_map/all_to_all | solution.py:186
  79.4 31.1 %copy-start.1 = (bf16[128,8192]{1,0:T(8,128)(2,1)S(1)}, bf16[128,8192]{1,0:T(8,128)(2,1)}, u32[]{:S(2)}) copy-start(bf16[128,8192]{1,0:T(8,128)(2,1)} %hidden_ref.3) | copy-start | bytes 6291460
  79.4 31.1 %copy-start.3 = (bf16[128,128]{1,0:T(8,128)(2,1)S(1)}, bf16[128,128]{1,0:T(8,128)(2,1)}, u32[]{:S(2)}) copy-start(bf16[128,128]{1,0:T(8,128)(2,1)} %cot_ref.3) | copy-start | bytes 98308
  85.3 25.2 %collective-permute-start.6 = (bf16[3,96,16,128]{3,2,1,0:T(8,128)(2,1)}, bf16[3,96,16,128]{3,2,1,0:T(8,128)(2,1)}, u32[]{:S(2)}, u32[]{:S(2)}) collective-permute-start(bf16[3,96,16,128]{3,2,1,0:T(8,128)(2,1)} %pad_maximum_fusion), channel_id=1, source_target_pairs={{0,96},{96,0},{1,97},{97,1},{2,98},{98,2},{3,99},{99,3},{4,100},{1... | collective-permute-start | bytes 3538952 | tf_op jit(solution)/shard_map/ppermute | solution.py:24
  87.9 22.6 %collective-permute-start.5 = (bf16[96,16,128]{2,1,0:T(8,128)(2,1)S(1)}, bf16[96,16,128]{2,1,0:T(8,128)(2,1)}, u32[]{:S(2)}, u32[]{:S(2)}) collective-permute-start(bf16[96,16,128]{2,1,0:T(8,128)(2,1)S(1)} %all-to-all-done.refs_0_), channel_id=1, source_target_pairs={{0,96},{96,0},{1,97},{97,1},{2,98},{98,2},{3,99},{99,3},{4,100},{1... | collective-permute-start | bytes 1179656 | tf_op jit(solution)/shard_map/ppermute | solution.py:24
  99.8 18.4 %all-to-all-start.2 = ((f32[8,4,128]{2,1,0:T(4,128)}), f32[8,4,128]{2,1,0:T(4,128)S(1)}, u32[]{:S(2)}, u32[]{:S(2)}) async-start(f32[8,4,128]{2,1,0:T(4,128)} %broadcast_in_dim.27), calls=%async_computation.2 | async-start | bytes 32768 | tf_op jit(solution)/shard_map/all_to_all | solution.py:204

commit v7 on v6

--- a/solution.py
+++ b/solution.py
@@ -43,7 +43,8 @@
             acc = acc + part[:, k * LANES : (k + 1) * LANES]
         return acc
 
-    acc = lax.fori_loop(0, width // STEP, squares, jnp.zeros((hidden_ref.shape[0], LANES), jnp.float32))
+    zero = jnp.zeros((hidden_ref.shape[0], LANES), jnp.float32)
+    acc = lax.fori_loop(0, width // STEP, squares, zero, unroll=2)
     inv = lax.rsqrt(jnp.sum(acc, axis=1, keepdims=True) / width + EPS)
     inv_ref[...] = jnp.broadcast_to(inv, inv_ref.shape)
     cots = (cot_ref[...].astype(jnp.float32) * inv).astype(jnp.bfloat16)
@@ -55,7 +56,7 @@
         )
         return 0
 
-    lax.fori_loop(0, width // STEP, outer, 0, unroll=2)
+    lax.fori_loop(0, width // STEP, outer, 0, unroll=4)
     u_ref[width:, :] = jnp.zeros((ROWS_PAD - width, LANES), jnp.float32)
 
     starts = [[GROUP_ROWS * lax.rem(x + k, 4) + first_row(yh, core) for yh in range(4)] for core in (c, 1 - c) for k in range(4)]
@@ -70,7 +71,7 @@
                     out[k, place + 2 * yh] = u_ref[pl.ds(row, BLK), :].astype(jnp.bfloat16)
         return 0
 
-    lax.fori_loop(0, 24, pack, 0)
+    lax.fori_loop(0, 24, pack, 0, unroll=2)
 
 
 def rows_kernel(pos_ref, hidden_ref, cot_ref, inv_ref, *refs):
@@ -99,7 +100,7 @@
                     s_ref[core, pl.ds(row + BLK, rest), :] = tail[:rest]
         return 0
 
-    lax.fori_loop(0, 24, assemble, 0)
+    lax.fori_loop(0, 24, assemble, 0, unroll=2)
     gain_ref[...] = s_ref[0, width : width + 64, :] + s_ref[1, width : width + 64, :]
     inv = inv_ref[...]
 
@@ -115,7 +116,7 @@
         return key + jnp.dot(jnp.concatenate(rows, axis=1), weight, preferred_element_type=jnp.float32)
 
     key = lax.fori_loop(
-        0, width // STEP, forward, jnp.zeros(key_ref.shape, jnp.float32), unroll=2
+        0, width // STEP, forward, jnp.zeros(key_ref.shape, jnp.float32), unroll=4
     )
     key_ref[...] = key.astype(jnp.bfloat16)
     cot = cot_ref[...]
@@ -134,7 +135,7 @@
             grad_ref[:, lanes] = grad.astype(jnp.bfloat16)
         return 0
 
-    lax.fori_loop(0, width // STEP, backward, 0, unroll=2)
+    lax.fori_loop(0, width // STEP, backward, 0, unroll=4)
 
 
 def local(hidden_in, cotangent, params):
@@ -174,7 +175,9 @@
 
     total = own[0].astype(f32) + got[0].astype(f32)
     total = total + moved[1].astype(f32) + moved[2].astype(f32) + moved[3].astype(f32)
-    gain_part = jnp.sum(mine.astype(f32) * total, axis=-1)[:, :USED].reshape(12, 8 * USED)
+    products = jnp.sum(mine.astype(f32) * total, axis=-1)
+    products, total = lax.optimization_barrier((products, total.astype(bf16)))
+    gain_part = products[:, :USED].reshape(12, 8 * USED)
     pays = [jnp.zeros((512,), f32)]
     for start in (0, 3, 7):
         pays.append(jnp.pad(gain_part[start : start + 5].reshape(-1), (0, 32)))
@@ -182,7 +185,7 @@
     pay = jnp.concatenate([jnp.zeros_like(pay), pay], axis=1).reshape(8, 4, LANES)
     pay = jnp.pad(pay, ((N_ZY - 8, 0), (USED, 0), (0, 0)))
     spare = lax.broadcasted_iota(jnp.int32, (1, BLK, 1), 1) >= USED
-    chunk = jnp.where(spare, pay, total).astype(bf16)
+    chunk = jnp.where(spare, pay.astype(bf16), total)
     received = lax.all_to_all(chunk, ZY, 0, 0, tiled=True)
 
     key_rows, input_grad, gains = pl.pallas_call(

time: 121 us -> 117 us (0.967)
  other arithmetic: 12.6 us -> 10.6 us
  starting transfers between devices: 69.1 us -> 67.1 us
    ppermute x6, waiting for transfers between devices: 3.77 us -> 5.75 us  [shift_x(): return lax.ppermute(a, 'x', [(i, (i + k) % 4) for i in range(4)])]
    all_to_all x1, waiting for transfers between devices: 8.2 us -> 6.23 us  [local(): received = lax.all_to_all(chunk, ZY, 0, 0, tiled=True)]
    reduce_sum x1 -> x0, other arithmetic: 1.63 us -> none  [local(): jnp.sum(mine.astype(f32) * total, axis=-1)[:, :USED].reshape(12, 8 * USED)]
    all_to_all x1, starting transfers between devices: 10.7 us -> 9.45 us  [local(): lax.all_to_all(jnp.broadcast_to(part, (8, 4, LANES)), ('c', 'x'), 0, 0, t...]
    unnamed x10 -> x12, local copies, waits for them, and re-layouts: 2.37 us -> 3.13 us
  transfers between devices with their start and end apart: 12 -> 12, of which waited for: 3 -> 3; matrix products, arithmetic and copies ran while one was open for 12% -> 10% of each run, Pallas kernels for 6% -> 6%
where the time goes in v7:
time: 117 us; the launch traced here: 116 us
  starting transfers between devices  67.1 us (57%)
  waiting for transfers between devices  20.3 us (17%)
  Pallas kernels  11.2 us (10%)
  other arithmetic  10.6 us (9%)
  local copies, waits for them, and re-layouts  6.15 us (5%)
    ppermute x6, starting transfers between devices, shift_x(): return lax.ppermute(a, 'x', [(i, (i + k) % 4) for i in range(4)])  19.2 us
    ppermute x3, starting transfers between devices, swap(): return lax.ppermute(a, 'c', [(0, 1), (1, 0)])  16.9 us
    all_to_all x1, starting transfers between devices, local(): lax.all_to_all(jnp.broadcast_to(block, (N_ZY, BLK, LANES)), ZY, 0, 0, til...  12.7 us
    all_to_all x1, starting transfers between devices, local(): lax.all_to_all(jnp.broadcast_to(part, (8, 4, LANES)), ('c', 'x'), 0, 0, t...  9.45 us
    all_to_all x1, starting transfers between devices, local(): received = lax.all_to_all(chunk, ZY, 0, 0, tiled=True)  8.84 us
    all_to_all x1, waiting for transfers between devices, local(): lax.all_to_all(jnp.broadcast_to(block, (N_ZY, BLK, LANES)), ZY, 0, 0, til...  8.28 us
    pallas_call x1, Pallas kernels, local(): pl.pallas_call(rows_kernel, out_shape=(jax.ShapeDtypeStruct((tokens, LANE...  7.16 us
    all_to_all x1, waiting for transfers between devices, local(): received = lax.all_to_all(chunk, ZY, 0, 0, tiled=True)  6.23 us
  transfers between devices with their start and end apart: 12, of which 3 were waited for; matrix products, arithmetic and copies ran while one was open for 10% of the time, Pallas kernels for 6%

profile of v7, /device:TPU:1, one launch (start us, length us, event | category | flops | bytes accessed | tf_op | source)
XLA Modules:
  0.0 116.3 jit_solution(9834961722536069311)
XLA Ops:
  0.6 0.1 pad_add_fusion.6.pos_ref
  0.7 1.6 %copy-done = bf16[128,8192]{1,0:T(8,128)(2,1)S(1)} copy-done((bf16[128,8192]{1,0:T(8,128)(2,1)S(1)}, bf16[128,8192]{1,0:T(8,128)(2,1)}, u32[]{:S(2)}) %copy-start) | copy-done | bytes 2097176
  2.3 0.8 copy-done.2
  3.1 4.0 %shard_map.58 = (bf16[4,96,16,128]{3,2,1,0:T(8,128)(2,1)S(1)}, bf16[4,96,16,128]{3,2,1,0:T(8,128)(2,1)}, f32[128,128]{1,0:T(8,128)S(1)}) custom-call(s32[2]{0:T(128)S(1)} %pad_add_fusion.6.pos_ref, bf16[128,8192]{1,0:T(8,128)(2,1)S(1)} %copy-done, bf16[128,128]{1,0:T(8,128)(2,1)S(1)} %copy-done.2), custom_call_target="tpu_custom_call" | custom-call | flops 536870912 | bytes 8388608 | tf_op jit(solution)/shard_map/pallas_call | solution.py:157
  7.1 12.4 %collective-permute-start = (bf16[4,96,16,128]{3,2,1,0:T(8,128)(2,1)}, bf16[4,96,16,128]{3,2,1,0:T(8,128)(2,1)}, u32[]{:S(2)}, u32[]{:S(2)}) collective-permute-start(bf16[4,96,16,128]{3,2,1,0:T(8,128)(2,1)} %get-tuple-element.23), channel_id=1, source_target_pairs={{0,96},{96,0},{1,97},{97,1},{2,98},{98,2},{3,99},{99,3},{4,100},{1... | collective-permute-start | bytes 4718600 | tf_op jit(solution)/shard_map/ppermute | solution.py:24
  19.6 0.1 fusion.9
  19.7 0.8 broadcast_in_dim.25
  20.5 12.7 %all-to-all-start = ((bf16[96,16,128]{2,1,0:T(8,128)(2,1)}), bf16[96,16,128]{2,1,0:T(8,128)(2,1)S(1)}, u32[]{:S(2)}, u32[]{:S(2)}) async-start(bf16[96,16,128]{2,1,0:T(8,128)(2,1)} %broadcast_in_dim.25), calls=%async_computation | async-start | bytes 786432 | tf_op jit(solution)/shard_map/all_to_all | solution.py:154
  33.2 1.1 fusion.2
  34.3 1.1 fusion.3
  35.4 4.6 %collective-permute-start.1 = (bf16[96,16,128]{2,1,0:T(8,128)(2,1)S(1)}, bf16[96,16,128]{2,1,0:T(8,128)(2,1)S(1)}, u32[]{:S(2)}, u32[]{:S(2)}) collective-permute-start(bf16[96,16,128]{2,1,0:T(8,128)(2,1)S(1)} %fusion.2), channel_id=1, source_target_pairs={{0,2},{1,3},{2,0},{3,1},{4,6},{5,7},{6,4},{7,5},{8,10},{9,11},{10,... | collective-permute-start | bytes 1179656 | tf_op jit(solution)/shard_map/ppermute | solution.py:28
  40.1 1.8 %fusion.4 = bf16[96,16,128]{2,1,0:T(8,128)(2,1)} fusion(bf16[4,96,16,128]{3,2,1,0:T(8,128)(2,1)} %collective-permute-done, bf16[4,96,16,128]{3,2,1,0:T(8,128)(2,1)S(1)} %get-tuple-element.22), kind=kLoop, calls=%fused_computation.11 | loop fusion | flops 786432 | bytes 1179648 | tf_op jit(solution)/shard_map/convert_element_type | solution.py:169
  41.9 2.8 %collective-permute-start.8 = (bf16[96,16,128]{2,1,0:T(8,128)(2,1)}, bf16[96,16,128]{2,1,0:T(8,128)(2,1)}, u32[]{:S(2)}, u32[]{:S(2)}) collective-permute-start(bf16[96,16,128]{2,1,0:T(8,128)(2,1)} %fusion.4), channel_id=1, source_target_pairs={{0,3},{1,0},{2,1},{3,2},{4,7},{5,4},{6,5},{7,6},{8,11},{9,8},{10,9... | collective-permute-start | bytes 1179656 | tf_op jit(solution)/shard_map/ppermute | solution.py:28
  44.7 2.5 %collective-permute-start.7 = (bf16[96,16,128]{2,1,0:T(8,128)(2,1)S(1)}, bf16[96,16,128]{2,1,0:T(8,128)(2,1)}, u32[]{:S(2)}, u32[]{:S(2)}) collective-permute-start(bf16[96,16,128]{2,1,0:T(8,128)(2,1)S(1)} %fusion.3), channel_id=1, source_target_pairs={{0,1},{1,2},{2,3},{3,0},{4,5},{5,6},{6,7},{7,4},{8,9},{9,10},{10,1... | collective-permute-start | bytes 1179656 | tf_op jit(solution)/shard_map/ppermute | solution.py:28
  47.2 8.3 %all-to-all-done.refs_0_ = bf16[96,16,128]{2,1,0:T(8,128)(2,1)S(1)} async-done(((bf16[96,16,128]{2,1,0:T(8,128)(2,1)}), bf16[96,16,128]{2,1,0:T(8,128)(2,1)S(1)}, u32[]{:S(2)}, u32[]{:S(2)}) %all-to-all-start) | async-done | bytes 393248 | tf_op jit(solution)/shard_map/all_to_all | solution.py:154
  55.5 0.8 copy-done.4
  56.3 4.4 %collective-permute-start.4 = (bf16[96,16,128]{2,1,0:T(8,128)(2,1)S(1)}, bf16[96,16,128]{2,1,0:T(8,128)(2,1)S(1)}, u32[]{:S(2)}, u32[]{:S(2)}) collective-permute-start(bf16[96,16,128]{2,1,0:T(8,128)(2,1)S(1)} %all-to-all-done.refs_0_), channel_id=1, source_target_pairs={{0,3},{1,0},{2,1},{3,2},{4,7},{5,4},{6,5},{7,6},{8,11},{9,8},{10,9... | collective-permute-start | bytes 1179656 | tf_op jit(solution)/shard_map/ppermute | solution.py:28
  60.7 2.4 %collective-permute-start.3 = (bf16[96,16,128]{2,1,0:T(8,128)(2,1)S(1)}, bf16[96,16,128]{2,1,0:T(8,128)(2,1)S(1)}, u32[]{:S(2)}, u32[]{:S(2)}) collective-permute-start(bf16[96,16,128]{2,1,0:T(8,128)(2,1)S(1)} %all-to-all-done.refs_0_), channel_id=1, source_target_pairs={{0,2},{1,3},{2,0},{3,1},{4,6},{5,7},{6,4},{7,5},{8,10},{9,11},{10,... | collective-permute-start | bytes 1179656 | tf_op jit(solution)/shard_map/ppermute | solution.py:28
  63.1 2.5 %collective-permute-start.2 = (bf16[96,16,128]{2,1,0:T(8,128)(2,1)S(1)}, bf16[96,16,128]{2,1,0:T(8,128)(2,1)}, u32[]{:S(2)}, u32[]{:S(2)}) collective-permute-start(bf16[96,16,128]{2,1,0:T(8,128)(2,1)S(1)} %all-to-all-done.refs_0_), channel_id=1, source_target_pairs={{0,1},{1,2},{2,3},{3,0},{4,5},{5,6},{6,7},{7,4},{8,9},{9,10},{10,1... | collective-permute-start | bytes 1179656 | tf_op jit(solution)/shard_map/ppermute | solution.py:28
  65.6 0.0 collective-permute-done.8
  65.6 0.0 collective-permute-done.7
  65.6 1.8 %fusion.10 = (bf16[96,16,128]{2,1,0:T(8,128)(2,1)S(1)}, bf16[96,16]{1,0:T(8,128)(2,1)S(1)}) fusion(bf16[96,16,128]{2,1,0:T(8,128)(2,1)} %collective-permute-done.8, bf16[96,16,128]{2,1,0:T(8,128)(2,1)} %copy-done.4, bf16[96,16,128]{2,1,0:T(8,128)(2,1)} %collective-permute-done.7, bf16[4,96,16,128]{3,2,1,0:T(8,128)(2,1)} %collective-permute-done, ...), kind=kLoop, calls=%fused_computation.42 | loop fusion | flops 2554368 | bytes 2755584 | tf_op jit(solution)/shard_map/convert_element_type | solution.py:179
  67.5 0.1 reshape.85
  67.6 0.1 reshape.86
  67.7 0.1 reshape.87
  67.8 0.1 pad_maximum_fusion.1
  67.9 0.9 pad_select_fusion
  68.8 8.8 %all-to-all-start.1 = ((bf16[96,16,128]{2,1,0:T(8,128)(2,1)}), bf16[96,16,128]{2,1,0:T(8,128)(2,1)}, u32[]{:S(2)}, u32[]{:S(2)}) async-start(bf16[96,16,128]{2,1,0:T(8,128)(2,1)} %pad_select_fusion), calls=%async_computation.1 | async-start | bytes 786432 | tf_op jit(solution)/shard_map/all_to_all | solution.py:189
  77.7 0.0 copy-start.1
  77.7 0.0 copy-start.3
  77.7 0.0 collective-permute-done.3.refs_2_
  77.7 5.7 %collective-permute-done.2.refs_1_ = bf16[96,16,128]{2,1,0:T(8,128)(2,1)} collective-permute-done((bf16[96,16,128]{2,1,0:T(8,128)(2,1)S(1)}, bf16[96,16,128]{2,1,0:T(8,128)(2,1)}, u32[]{:S(2)}, u32[]{:S(2)}) %collective-permute-start.2) | collective-permute-done | bytes 393248 | tf_op jit(solution)/shard_map/ppermute | solution.py:28
  83.5 2.1 %pad_maximum_fusion = bf16[3,96,16,128]{3,2,1,0:T(8,128)(2,1)} fusion(bf16[1,96,16,128]{3,2,1,0:T(8,128)(2,1)S(1)} %bitcast.67, bf16[1,96,16,128]{3,2,1,0:T(8,128)(2,1)S(1)} %bitcast.68, bf16[1,96,16,128]{3,2,1,0:T(8,128)(2,1)} %bitcast.4), kind=kLoop, calls=%fused_computation | loop fusion | flops 1179648 | bytes 2359296 | tf_op jit(solution)/shard_map/stack | solution.py:173
  85.6 2.6 %collective-permute-start.6 = (bf16[3,96,16,128]{3,2,1,0:T(8,128)(2,1)}, bf16[3,96,16,128]{3,2,1,0:T(8,128)(2,1)}, u32[]{:S(2)}, u32[]{:S(2)}) collective-permute-start(bf16[3,96,16,128]{3,2,1,0:T(8,128)(2,1)} %pad_maximum_fusion), channel_id=1, source_target_pairs={{0,96},{96,0},{1,97},{97,1},{2,98},{98,2},{3,99},{99,3},{4,100},{1... | collective-permute-start | bytes 3538952 | tf_op jit(solution)/shard_map/ppermute | solution.py:24
  88.2 1.9 %collective-permute-start.5 = (bf16[96,16,128]{2,1,0:T(8,128)(2,1)S(1)}, bf16[96,16,128]{2,1,0:T(8,128)(2,1)}, u32[]{:S(2)}, u32[]{:S(2)}) collective-permute-start(bf16[96,16,128]{2,1,0:T(8,128)(2,1)S(1)} %all-to-all-done.refs_0_), channel_id=1, source_target_pairs={{0,96},{96,0},{1,97},{97,1},{2,98},{98,2},{3,99},{99,3},{4,100},{1... | collective-permute-start | bytes 1179656 | tf_op jit(solution)/shard_map/ppermute | solution.py:24
  90.1 6.2 %all-to-all-done.1 = bf16[96,16,128]{2,1,0:T(8,128)(2,1)} async-done(((bf16[96,16,128]{2,1,0:T(8,128)(2,1)}), bf16[96,16,128]{2,1,0:T(8,128)(2,1)}, u32[]{:S(2)}, u32[]{:S(2)}) %all-to-all-start.1) | async-done | bytes 393248 | tf_op jit(solution)/shard_map/all_to_all | solution.py:189
  96.4 1.1 convert_reduce_fusion
  97.5 0.6 broadcast_in_dim.27
  98.1 9.4 %all-to-all-start.2 = ((f32[8,4,128]{2,1,0:T(4,128)}), f32[8,4,128]{2,1,0:T(4,128)S(1)}, u32[]{:S(2)}, u32[]{:S(2)}) async-start(f32[8,4,128]{2,1,0:T(4,128)} %broadcast_in_dim.27), calls=%async_computation.2 | async-start | bytes 32768 | tf_op jit(solution)/shard_map/all_to_all | solution.py:207
  107.6 7.2 %shard_map.59 = (bf16[128,128]{1,0:T(8,128)(2,1)}, bf16[128,8192]{1,0:T(8,128)(2,1)}, f32[64,128]{1,0:T(8,128)S(1)}) custom-call(s32[2]{0:T(128)S(1)} %pad_add_fusion.6.pos_ref, bf16[128,8192]{1,0:T(8,128)(2,1)S(1)} %copy-done.1, bf16[128,128]{1,0:T(8,128)(2,1)S(1)} %copy-done.3, f32[128,128]{1,0:T(8,128)S(1)} %get-tuple-element.21.inv_ref, ...), custom_call_target="tpu_custom_call" | custom-call | flops 536870912 | bytes 10485760 | tf_op jit(solution)/shard_map/pallas_call | solution.py:191
  114.7 0.1 pad_dynamic-slice_fusion
  114.8 0.1 fusion.8
  114.9 0.3 reshape.92
  115.2 0.1 slice_bitcast_fusion.7
  115.2 0.2 fusion.5
  115.5 0.1 reshape.93
  115.6 0.1 fusion.7
  115.7 0.6 reshape.94
  (23 shorter events, 0.1 us)
Async XLA Ops:
  0.6 18.9 %copy-start.5 = (bf16[1,1376]{1,0:T(2,128)(2,1)S(1)}, bf16[1,1376]{1,0:T(2,128)(2,1)}, u32[]{:S(2)}) copy-start(bf16[1,1376]{1,0:T(2,128)(2,1)} %param.5) | copy-start | bytes 8260
  0.7 1.6 %copy-start = (bf16[128,8192]{1,0:T(8,128)(2,1)S(1)}, bf16[128,8192]{1,0:T(8,128)(2,1)}, u32[]{:S(2)}) copy-start(bf16[128,8192]{1,0:T(8,128)(2,1)} %hidden_ref.3) | copy-start | bytes 6291460
  2.3 0.8 copy-start.2
  7.1 26.1 %collective-permute-start = (bf16[4,96,16,128]{3,2,1,0:T(8,128)(2,1)}, bf16[4,96,16,128]{3,2,1,0:T(8,128)(2,1)}, u32[]{:S(2)}, u32[]{:S(2)}) collective-permute-start(bf16[4,96,16,128]{3,2,1,0:T(8,128)(2,1)} %get-tuple-element.23), channel_id=1, source_target_pairs={{0,96},{96,0},{1,97},{97,1},{2,98},{98,2},{3,99},{99,3},{4,100},{1... | collective-permute-start | bytes 4718600 | tf_op jit(solution)/shard_map/ppermute | solution.py:24
  20.5 35.0 %all-to-all-start = ((bf16[96,16,128]{2,1,0:T(8,128)(2,1)}), bf16[96,16,128]{2,1,0:T(8,128)(2,1)S(1)}, u32[]{:S(2)}, u32[]{:S(2)}) async-start(bf16[96,16,128]{2,1,0:T(8,128)(2,1)} %broadcast_in_dim.25), calls=%async_computation | async-start | bytes 786432 | tf_op jit(solution)/shard_map/all_to_all | solution.py:154
  35.4 20.1 %collective-permute-start.1 = (bf16[96,16,128]{2,1,0:T(8,128)(2,1)S(1)}, bf16[96,16,128]{2,1,0:T(8,128)(2,1)S(1)}, u32[]{:S(2)}, u32[]{:S(2)}) collective-permute-start(bf16[96,16,128]{2,1,0:T(8,128)(2,1)S(1)} %fusion.2), channel_id=1, source_target_pairs={{0,2},{1,3},{2,0},{3,1},{4,6},{5,7},{6,4},{7,5},{8,10},{9,11},{10,... | collective-permute-start | bytes 1179656 | tf_op jit(solution)/shard_map/ppermute | solution.py:28
  41.9 23.7 %collective-permute-start.8 = (bf16[96,16,128]{2,1,0:T(8,128)(2,1)}, bf16[96,16,128]{2,1,0:T(8,128)(2,1)}, u32[]{:S(2)}, u32[]{:S(2)}) collective-permute-start(bf16[96,16,128]{2,1,0:T(8,128)(2,1)} %fusion.4), channel_id=1, source_target_pairs={{0,3},{1,0},{2,1},{3,2},{4,7},{5,4},{6,5},{7,6},{8,11},{9,8},{10,9... | collective-permute-start | bytes 1179656 | tf_op jit(solution)/shard_map/ppermute | solution.py:28
  44.7 20.9 %collective-permute-start.7 = (bf16[96,16,128]{2,1,0:T(8,128)(2,1)S(1)}, bf16[96,16,128]{2,1,0:T(8,128)(2,1)}, u32[]{:S(2)}, u32[]{:S(2)}) collective-permute-start(bf16[96,16,128]{2,1,0:T(8,128)(2,1)S(1)} %fusion.3), channel_id=1, source_target_pairs={{0,1},{1,2},{2,3},{3,0},{4,5},{5,6},{6,7},{7,4},{8,9},{9,10},{10,1... | collective-permute-start | bytes 1179656 | tf_op jit(solution)/shard_map/ppermute | solution.py:28
  55.5 0.8 copy-start.4
  56.3 21.4 %collective-permute-start.4 = (bf16[96,16,128]{2,1,0:T(8,128)(2,1)S(1)}, bf16[96,16,128]{2,1,0:T(8,128)(2,1)S(1)}, u32[]{:S(2)}, u32[]{:S(2)}) collective-permute-start(bf16[96,16,128]{2,1,0:T(8,128)(2,1)S(1)} %all-to-all-done.refs_0_), channel_id=1, source_target_pairs={{0,3},{1,0},{2,1},{3,2},{4,7},{5,4},{6,5},{7,6},{8,11},{9,8},{10,9... | collective-permute-start | bytes 1179656 | tf_op jit(solution)/shard_map/ppermute | solution.py:28
  60.7 17.1 %collective-permute-start.3 = (bf16[96,16,128]{2,1,0:T(8,128)(2,1)S(1)}, bf16[96,16,128]{2,1,0:T(8,128)(2,1)S(1)}, u32[]{:S(2)}, u32[]{:S(2)}) collective-permute-start(bf16[96,16,128]{2,1,0:T(8,128)(2,1)S(1)} %all-to-all-done.refs_0_), channel_id=1, source_target_pairs={{0,2},{1,3},{2,0},{3,1},{4,6},{5,7},{6,4},{7,5},{8,10},{9,11},{10,... | collective-permute-start | bytes 1179656 | tf_op jit(solution)/shard_map/ppermute | solution.py:28
  63.1 20.4 %collective-permute-start.2 = (bf16[96,16,128]{2,1,0:T(8,128)(2,1)S(1)}, bf16[96,16,128]{2,1,0:T(8,128)(2,1)}, u32[]{:S(2)}, u32[]{:S(2)}) collective-permute-start(bf16[96,16,128]{2,1,0:T(8,128)(2,1)S(1)} %all-to-all-done.refs_0_), channel_id=1, source_target_pairs={{0,1},{1,2},{2,3},{3,0},{4,5},{5,6},{6,7},{7,4},{8,9},{9,10},{10,1... | collective-permute-start | bytes 1179656 | tf_op jit(solution)/shard_map/ppermute | solution.py:28
  68.8 27.5 %all-to-all-start.1 = ((bf16[96,16,128]{2,1,0:T(8,128)(2,1)}), bf16[96,16,128]{2,1,0:T(8,128)(2,1)}, u32[]{:S(2)}, u32[]{:S(2)}) async-start(bf16[96,16,128]{2,1,0:T(8,128)(2,1)} %pad_select_fusion), calls=%async_computation.1 | async-start | bytes 786432 | tf_op jit(solution)/shard_map/all_to_all | solution.py:189
  77.7 29.9 %copy-start.1 = (bf16[128,8192]{1,0:T(8,128)(2,1)S(1)}, bf16[128,8192]{1,0:T(8,128)(2,1)}, u32[]{:S(2)}) copy-start(bf16[128,8192]{1,0:T(8,128)(2,1)} %hidden_ref.3) | copy-start | bytes 6291460
  77.7 29.9 %copy-start.3 = (bf16[128,128]{1,0:T(8,128)(2,1)S(1)}, bf16[128,128]{1,0:T(8,128)(2,1)}, u32[]{:S(2)}) copy-start(bf16[128,128]{1,0:T(8,128)(2,1)} %cot_ref.3) | copy-start | bytes 98308
  85.6 22.0 %collective-permute-start.6 = (bf16[3,96,16,128]{3,2,1,0:T(8,128)(2,1)}, bf16[3,96,16,128]{3,2,1,0:T(8,128)(2,1)}, u32[]{:S(2)}, u32[]{:S(2)}) collective-permute-start(bf16[3,96,16,128]{3,2,1,0:T(8,128)(2,1)} %pad_maximum_fusion), channel_id=1, source_target_pairs={{0,96},{96,0},{1,97},{97,1},{2,98},{98,2},{3,99},{99,3},{4,100},{1... | collective-permute-start | bytes 3538952 | tf_op jit(solution)/shard_map/ppermute | solution.py:24
  88.2 19.4 %collective-permute-start.5 = (bf16[96,16,128]{2,1,0:T(8,128)(2,1)S(1)}, bf16[96,16,128]{2,1,0:T(8,128)(2,1)}, u32[]{:S(2)}, u32[]{:S(2)}) collective-permute-start(bf16[96,16,128]{2,1,0:T(8,128)(2,1)S(1)} %all-to-all-done.refs_0_), channel_id=1, source_target_pairs={{0,96},{96,0},{1,97},{97,1},{2,98},{98,2},{3,99},{99,3},{4,100},{1... | collective-permute-start | bytes 1179656 | tf_op jit(solution)/shard_map/ppermute | solution.py:24
  98.1 16.6 %all-to-all-start.2 = ((f32[8,4,128]{2,1,0:T(4,128)}), f32[8,4,128]{2,1,0:T(4,128)S(1)}, u32[]{:S(2)}, u32[]{:S(2)}) async-start(f32[8,4,128]{2,1,0:T(4,128)} %broadcast_in_dim.27), calls=%async_computation.2 | async-start | bytes 32768 | tf_op jit(solution)/shard_map/all_to_all | solution.py:207

commit v8 on v7

--- a/solution.py
+++ b/solution.py
@@ -32,9 +32,17 @@
     return lax.div(43 * (2 * yh + core), 4)
 
 
-def sums_kernel(pos_ref, hidden_ref, cot_ref, own_ref, send_ref, inv_ref, u_ref):
+def sums_kernel(pos_ref, hidden_hbm, cot_hbm, own_ref, send_ref, inv_ref, u_ref, hidden_ref, cot_ref, sems):
     width = hidden_ref.shape[1]
     x, c = pos_ref[0], pos_ref[1]
+    quarter = width // 4
+    copies = []
+    for k in range(4):
+        lanes = pl.ds(k * quarter, quarter)
+        copies.append(pltpu.make_async_copy(hidden_hbm.at[:, lanes], hidden_ref.at[:, lanes], sems.at[k]))
+    copies.append(pltpu.make_async_copy(cot_hbm, cot_ref, sems.at[4]))
+    for copy in copies:
+        copy.start()
 
     def squares(m, acc):
         part = hidden_ref[:, pl.ds(pl.multiple_of(m * STEP, STEP), STEP)].astype(jnp.float32)
@@ -43,8 +51,11 @@
             acc = acc + part[:, k * LANES : (k + 1) * LANES]
         return acc
 
-    zero = jnp.zeros((hidden_ref.shape[0], LANES), jnp.float32)
-    acc = lax.fori_loop(0, width // STEP, squares, zero, unroll=2)
+    acc = jnp.zeros((hidden_ref.shape[0], LANES), jnp.float32)
+    for k in range(4):
+        copies[k].wait()
+        acc = lax.fori_loop(k * quarter // STEP, (k + 1) * quarter // STEP, squares, acc, unroll=True)
+    copies[4].wait()
     inv = lax.rsqrt(jnp.sum(acc, axis=1, keepdims=True) / width + EPS)
     inv_ref[...] = jnp.broadcast_to(inv, inv_ref.shape)
     cots = (cot_ref[...].astype(jnp.float32) * inv).astype(jnp.bfloat16)
@@ -157,10 +168,15 @@
     own, send, inv = pl.pallas_call(
         sums_kernel,
         out_shape=(half, half, jax.ShapeDtypeStruct((tokens, LANES), f32)),
-        in_specs=[smem, vmem, vmem],
+        in_specs=[smem, pl.BlockSpec(memory_space=pl.ANY), pl.BlockSpec(memory_space=pl.ANY)],
         out_specs=(vmem, vmem, vmem),
-        scratch_shapes=[pltpu.VMEM((ROWS_PAD, LANES), f32)],
-        compiler_params=pltpu.CompilerParams(vmem_limit_bytes=24 << 20),
+        scratch_shapes=[
+            pltpu.VMEM((ROWS_PAD, LANES), f32),
+            pltpu.VMEM((tokens, width), bf16),
+            pltpu.VMEM((tokens, LANES), bf16),
+            pltpu.SemaphoreType.DMA((5,)),
+        ],
+        compiler_params=pltpu.CompilerParams(vmem_limit_bytes=60 << 20),
         cost_estimate=pl.CostEstimate(flops=4 * tokens * width * LANES, bytes_accessed=8 << 20, transcendentals=0),
     )(pos, hidden_in, cotangent)
     got = swap(send)

time: 117 us -> 118 us (level)
  local copies, waits for them, and re-layouts: 6.15 us -> 3.06 us
  starting transfers between devices: 67.1 us -> 68.9 us
  Pallas kernels: 11.2 us -> 12.9 us
    unnamed x12, local copies, waits for them, and re-layouts: 3.13 us -> 0.03 us
    pallas_call x1, Pallas kernels: 4 us -> 5.8 us  [local(): pl.pallas_call(sums_kernel, out_shape=(half, half, jax.ShapeDtypeStruct((...]
    all_to_all x1, starting transfers between devices: 9.45 us -> 10.9 us  [local(): lax.all_to_all(jnp.broadcast_to(part, (8, 4, LANES)), ('c', 'x'), 0, 0, t...]
where the time goes in v8:
time: 118 us; the launch traced here: 117 us
  starting transfers between devices  68.9 us (58%)
  waiting for transfers between devices  20.1 us (17%)
  Pallas kernels  12.9 us (11%)
  other arithmetic  11.1 us (9%)
  local copies, waits for them, and re-layouts  3.06 us (3%)
    ppermute x6, starting transfers between devices, shift_x(): return lax.ppermute(a, 'x', [(i, (i + k) % 4) for i in range(4)])  19.3 us
    ppermute x3, starting transfers between devices, swap(): return lax.ppermute(a, 'c', [(0, 1), (1, 0)])  17 us
    all_to_all x1, starting transfers between devices, local(): lax.all_to_all(jnp.broadcast_to(block, (N_ZY, BLK, LANES)), ZY, 0, 0, til...  12.7 us
    all_to_all x1, starting transfers between devices, local(): lax.all_to_all(jnp.broadcast_to(part, (8, 4, LANES)), ('c', 'x'), 0, 0, t...  10.9 us
    all_to_all x1, starting transfers between devices, local(): received = lax.all_to_all(chunk, ZY, 0, 0, tiled=True)  8.97 us
    all_to_all x1, waiting for transfers between devices, local(): lax.all_to_all(jnp.broadcast_to(block, (N_ZY, BLK, LANES)), ZY, 0, 0, til...  8.13 us
    pallas_call x1, Pallas kernels, local(): pl.pallas_call(rows_kernel, out_shape=(jax.ShapeDtypeStruct((tokens, LANE...  7.13 us
    all_to_all x1, waiting for transfers between devices, local(): received = lax.all_to_all(chunk, ZY, 0, 0, tiled=True)  6.18 us
  transfers between devices with their start and end apart: 12, of which 3 were waited for; matrix products, arithmetic and copies ran while one was open for 10% of the time, Pallas kernels for 6%

profile of v8, /device:TPU:1, one launch (start us, length us, event | category | flops | bytes accessed | tf_op | source)
XLA Modules:
  0.0 117.1 jit_solution(2624479785920250051)
XLA Ops:
  0.6 0.7 pad_add_fusion.6.pos_ref
  1.3 5.8 %shard_map.58 = (bf16[4,96,16,128]{3,2,1,0:T(8,128)(2,1)}, bf16[4,96,16,128]{3,2,1,0:T(8,128)(2,1)}, f32[128,128]{1,0:T(8,128)}) custom-call(s32[2]{0:T(128)} %pad_add_fusion.6.pos_ref, bf16[128,8192]{1,0:T(8,128)(2,1)} %hidden_ref.1, bf16[128,128]{1,0:T(8,128)(2,1)} %cot_ref.1), custom_call_target="tpu_custom_call" | custom-call | flops 536870912 | bytes 8388608 | tf_op jit(solution)/shard_map/pallas_call | solution.py:168
  7.1 0.0 copy-start.4
  7.1 12.6 %collective-permute-start = (bf16[4,96,16,128]{3,2,1,0:T(8,128)(2,1)}, bf16[4,96,16,128]{3,2,1,0:T(8,128)(2,1)}, u32[]{:S(2)}, u32[]{:S(2)}) collective-permute-start(bf16[4,96,16,128]{3,2,1,0:T(8,128)(2,1)} %get-tuple-element.23), channel_id=1, source_target_pairs={{0,96},{96,0},{1,97},{97,1},{2,98},{98,2},{3,99},{99,3},{4,100},{1... | collective-permute-start | bytes 4718600 | tf_op jit(solution)/shard_map/ppermute | solution.py:24
  19.8 0.1 fusion.9
  19.9 0.8 broadcast_in_dim.25
  20.7 12.7 %all-to-all-start = ((bf16[96,16,128]{2,1,0:T(8,128)(2,1)}), bf16[96,16,128]{2,1,0:T(8,128)(2,1)S(1)}, u32[]{:S(2)}, u32[]{:S(2)}) async-start(bf16[96,16,128]{2,1,0:T(8,128)(2,1)} %broadcast_in_dim.25), calls=%async_computation | async-start | bytes 786432 | tf_op jit(solution)/shard_map/all_to_all | solution.py:165
  33.4 0.0 collective-permute-done
  33.4 1.2 %fusion.2 = bf16[96,16,128]{2,1,0:T(8,128)(2,1)S(1)} fusion(bf16[4,96,16,128]{3,2,1,0:T(8,128)(2,1)} %collective-permute-done, bf16[4,96,16,128]{3,2,1,0:T(8,128)(2,1)} %get-tuple-element.22), kind=kLoop, calls=%fused_computation.9 | loop fusion | flops 786432 | bytes 1179648 | tf_op jit(solution)/shard_map/convert_element_type | solution.py:185
  34.6 1.1 fusion.3
  35.8 4.7 %collective-permute-start.1 = (bf16[96,16,128]{2,1,0:T(8,128)(2,1)S(1)}, bf16[96,16,128]{2,1,0:T(8,128)(2,1)S(1)}, u32[]{:S(2)}, u32[]{:S(2)}) collective-permute-start(bf16[96,16,128]{2,1,0:T(8,128)(2,1)S(1)} %fusion.2), channel_id=1, source_target_pairs={{0,2},{1,3},{2,0},{3,1},{4,6},{5,7},{6,4},{7,5},{8,10},{9,11},{10,... | collective-permute-start | bytes 1179656 | tf_op jit(solution)/shard_map/ppermute | solution.py:28
  40.4 1.8 %fusion.4 = bf16[96,16,128]{2,1,0:T(8,128)(2,1)} fusion(bf16[4,96,16,128]{3,2,1,0:T(8,128)(2,1)} %collective-permute-done, bf16[4,96,16,128]{3,2,1,0:T(8,128)(2,1)S(1)} %copy-done.4), kind=kLoop, calls=%fused_computation.11 | loop fusion | flops 786432 | bytes 1179648 | tf_op jit(solution)/shard_map/convert_element_type | solution.py:185
  42.3 2.8 %collective-permute-start.8 = (bf16[96,16,128]{2,1,0:T(8,128)(2,1)}, bf16[96,16,128]{2,1,0:T(8,128)(2,1)}, u32[]{:S(2)}, u32[]{:S(2)}) collective-permute-start(bf16[96,16,128]{2,1,0:T(8,128)(2,1)} %fusion.4), channel_id=1, source_target_pairs={{0,3},{1,0},{2,1},{3,2},{4,7},{5,4},{6,5},{7,6},{8,11},{9,8},{10,9... | collective-permute-start | bytes 1179656 | tf_op jit(solution)/shard_map/ppermute | solution.py:28
  45.0 2.5 %collective-permute-start.7 = (bf16[96,16,128]{2,1,0:T(8,128)(2,1)S(1)}, bf16[96,16,128]{2,1,0:T(8,128)(2,1)}, u32[]{:S(2)}, u32[]{:S(2)}) collective-permute-start(bf16[96,16,128]{2,1,0:T(8,128)(2,1)S(1)} %fusion.3), channel_id=1, source_target_pairs={{0,1},{1,2},{2,3},{3,0},{4,5},{5,6},{6,7},{7,4},{8,9},{9,10},{10,1... | collective-permute-start | bytes 1179656 | tf_op jit(solution)/shard_map/ppermute | solution.py:28
  47.6 8.1 %all-to-all-done.refs_0_ = bf16[96,16,128]{2,1,0:T(8,128)(2,1)S(1)} async-done(((bf16[96,16,128]{2,1,0:T(8,128)(2,1)}), bf16[96,16,128]{2,1,0:T(8,128)(2,1)S(1)}, u32[]{:S(2)}, u32[]{:S(2)}) %all-to-all-start) | async-done | bytes 393248 | tf_op jit(solution)/shard_map/all_to_all | solution.py:165
  55.7 0.0 collective-permute-done.1
  55.7 4.4 %collective-permute-start.4 = (bf16[96,16,128]{2,1,0:T(8,128)(2,1)S(1)}, bf16[96,16,128]{2,1,0:T(8,128)(2,1)S(1)}, u32[]{:S(2)}, u32[]{:S(2)}) collective-permute-start(bf16[96,16,128]{2,1,0:T(8,128)(2,1)S(1)} %all-to-all-done.refs_0_), channel_id=1, source_target_pairs={{0,3},{1,0},{2,1},{3,2},{4,7},{5,4},{6,5},{7,6},{8,11},{9,8},{10,9... | collective-permute-start | bytes 1179656 | tf_op jit(solution)/shard_map/ppermute | solution.py:28
  60.1 2.4 %collective-permute-start.3 = (bf16[96,16,128]{2,1,0:T(8,128)(2,1)S(1)}, bf16[96,16,128]{2,1,0:T(8,128)(2,1)S(1)}, u32[]{:S(2)}, u32[]{:S(2)}) collective-permute-start(bf16[96,16,128]{2,1,0:T(8,128)(2,1)S(1)} %all-to-all-done.refs_0_), channel_id=1, source_target_pairs={{0,2},{1,3},{2,0},{3,1},{4,6},{5,7},{6,4},{7,5},{8,10},{9,11},{10,... | collective-permute-start | bytes 1179656 | tf_op jit(solution)/shard_map/ppermute | solution.py:28
  62.5 2.5 %collective-permute-start.2 = (bf16[96,16,128]{2,1,0:T(8,128)(2,1)S(1)}, bf16[96,16,128]{2,1,0:T(8,128)(2,1)}, u32[]{:S(2)}, u32[]{:S(2)}) collective-permute-start(bf16[96,16,128]{2,1,0:T(8,128)(2,1)S(1)} %all-to-all-done.refs_0_), channel_id=1, source_target_pairs={{0,1},{1,2},{2,3},{3,0},{4,5},{5,6},{6,7},{7,4},{8,9},{9,10},{10,1... | collective-permute-start | bytes 1179656 | tf_op jit(solution)/shard_map/ppermute | solution.py:28
  65.1 0.0 collective-permute-done.8
  65.1 0.0 collective-permute-done.7
  65.1 1.6 %fusion.10 = (bf16[96,16,128]{2,1,0:T(8,128)(2,1)S(1)}, bf16[96,16]{1,0:T(8,128)(2,1)S(1)}) fusion(bf16[96,16,128]{2,1,0:T(8,128)(2,1)} %collective-permute-done.8, bf16[96,16,128]{2,1,0:T(8,128)(2,1)S(1)} %collective-permute-done.1, bf16[96,16,128]{2,1,0:T(8,128)(2,1)} %collective-permute-done.7, bf16[4,96,16,128]{3,2,1,0:T(8,128)(2,1)} %collective-permute-done, ...), kind=kLoop, calls=%fused_computation.42 | loop fusion | flops 2554368 | bytes 2755584 | tf_op jit(solution)/shard_map/convert_element_type | solution.py:195
  66.7 0.1 reshape.85
  66.9 0.1 reshape.86
  67.0 0.1 reshape.87
  67.1 0.1 pad_maximum_fusion.1
  67.2 0.9 pad_select_fusion
  68.1 9.0 %all-to-all-start.1 = ((bf16[96,16,128]{2,1,0:T(8,128)(2,1)}), bf16[96,16,128]{2,1,0:T(8,128)(2,1)}, u32[]{:S(2)}, u32[]{:S(2)}) async-start(bf16[96,16,128]{2,1,0:T(8,128)(2,1)} %pad_select_fusion), calls=%async_computation.1 | async-start | bytes 786432 | tf_op jit(solution)/shard_map/all_to_all | solution.py:205
  77.1 0.0 copy-start
  77.1 0.0 copy-start.1
  77.1 0.0 collective-permute-done.3.refs_2_
  77.1 5.8 %collective-permute-done.2.refs_1_ = bf16[96,16,128]{2,1,0:T(8,128)(2,1)} collective-permute-done((bf16[96,16,128]{2,1,0:T(8,128)(2,1)S(1)}, bf16[96,16,128]{2,1,0:T(8,128)(2,1)}, u32[]{:S(2)}, u32[]{:S(2)}) %collective-permute-start.2) | collective-permute-done | bytes 393248 | tf_op jit(solution)/shard_map/ppermute | solution.py:28
  82.9 2.1 %pad_maximum_fusion = bf16[3,96,16,128]{3,2,1,0:T(8,128)(2,1)} fusion(bf16[1,96,16,128]{3,2,1,0:T(8,128)(2,1)S(1)} %bitcast.67, bf16[1,96,16,128]{3,2,1,0:T(8,128)(2,1)S(1)} %bitcast.68, bf16[1,96,16,128]{3,2,1,0:T(8,128)(2,1)} %bitcast.4), kind=kLoop, calls=%fused_computation | loop fusion | flops 1179648 | bytes 2359296 | tf_op jit(solution)/shard_map/stack | solution.py:189
  85.0 2.6 %collective-permute-start.6 = (bf16[3,96,16,128]{3,2,1,0:T(8,128)(2,1)}, bf16[3,96,16,128]{3,2,1,0:T(8,128)(2,1)}, u32[]{:S(2)}, u32[]{:S(2)}) collective-permute-start(bf16[3,96,16,128]{3,2,1,0:T(8,128)(2,1)} %pad_maximum_fusion), channel_id=1, source_target_pairs={{0,96},{96,0},{1,97},{97,1},{2,98},{98,2},{3,99},{99,3},{4,100},{1... | collective-permute-start | bytes 3538952 | tf_op jit(solution)/shard_map/ppermute | solution.py:24
  87.6 1.9 %collective-permute-start.5 = (bf16[96,16,128]{2,1,0:T(8,128)(2,1)S(1)}, bf16[96,16,128]{2,1,0:T(8,128)(2,1)}, u32[]{:S(2)}, u32[]{:S(2)}) collective-permute-start(bf16[96,16,128]{2,1,0:T(8,128)(2,1)S(1)} %all-to-all-done.refs_0_), channel_id=1, source_target_pairs={{0,96},{96,0},{1,97},{97,1},{2,98},{98,2},{3,99},{99,3},{4,100},{1... | collective-permute-start | bytes 1179656 | tf_op jit(solution)/shard_map/ppermute | solution.py:24
  89.6 6.2 %all-to-all-done.1 = bf16[96,16,128]{2,1,0:T(8,128)(2,1)} async-done(((bf16[96,16,128]{2,1,0:T(8,128)(2,1)}), bf16[96,16,128]{2,1,0:T(8,128)(2,1)}, u32[]{:S(2)}, u32[]{:S(2)}) %all-to-all-start.1) | async-done | bytes 393248 | tf_op jit(solution)/shard_map/all_to_all | solution.py:205
  95.8 1.1 convert_reduce_fusion
  96.9 0.6 broadcast_in_dim.27
  97.5 10.9 %all-to-all-start.2 = ((f32[8,4,128]{2,1,0:T(4,128)}), f32[8,4,128]{2,1,0:T(4,128)S(1)}, u32[]{:S(2)}, u32[]{:S(2)}) async-start(f32[8,4,128]{2,1,0:T(4,128)} %broadcast_in_dim.27), calls=%async_computation.2 | async-start | bytes 32768 | tf_op jit(solution)/shard_map/all_to_all | solution.py:223
  108.5 7.1 %shard_map.59 = (bf16[128,128]{1,0:T(8,128)(2,1)}, bf16[128,8192]{1,0:T(8,128)(2,1)}, f32[64,128]{1,0:T(8,128)S(1)}) custom-call(s32[2]{0:T(128)S(1)} %copy-done.3, bf16[128,8192]{1,0:T(8,128)(2,1)S(1)} %copy-done, bf16[128,128]{1,0:T(8,128)(2,1)S(1)} %copy-done.1, f32[128,128]{1,0:T(8,128)S(1)} %copy-done.2, bf16[96,16,128]{2,1,0:T(8,128)(2,1)S(1)} %all-to-all-done.refs_0_, ...), custom_call_target="tpu_custom_call" | custom-call | flops 536870912 | bytes 10485760 | tf_op jit(solution)/shard_map/pallas_call | solution.py:207
  115.6 0.1 pad_dynamic-slice_fusion
  115.7 0.1 fusion.8
  115.8 0.3 reshape.92
  116.0 0.1 slice_bitcast_fusion.7
  116.1 0.2 fusion.5
  116.3 0.1 reshape.93
  116.5 0.1 fusion.7
  116.5 0.6 reshape.94
  (23 shorter events, 0.1 us)
Async XLA Ops:
  0.6 19.1 %copy-start.5 = (bf16[1,1376]{1,0:T(2,128)(2,1)S(1)}, bf16[1,1376]{1,0:T(2,128)(2,1)}, u32[]{:S(2)}) copy-start(bf16[1,1376]{1,0:T(2,128)(2,1)} %param.5) | copy-start | bytes 8260
  7.1 27.5 %copy-start.4 = (bf16[4,96,16,128]{3,2,1,0:T(8,128)(2,1)S(1)}, bf16[4,96,16,128]{3,2,1,0:T(8,128)(2,1)}, u32[]{:S(2)}) copy-start(bf16[4,96,16,128]{3,2,1,0:T(8,128)(2,1)} %get-tuple-element.22) | copy-start | bytes 4718596
  7.1 26.3 %collective-permute-start = (bf16[4,96,16,128]{3,2,1,0:T(8,128)(2,1)}, bf16[4,96,16,128]{3,2,1,0:T(8,128)(2,1)}, u32[]{:S(2)}, u32[]{:S(2)}) collective-permute-start(bf16[4,96,16,128]{3,2,1,0:T(8,128)(2,1)} %get-tuple-element.23), channel_id=1, source_target_pairs={{0,96},{96,0},{1,97},{97,1},{2,98},{98,2},{3,99},{99,3},{4,100},{1... | collective-permute-start | bytes 4718600 | tf_op jit(solution)/shard_map/ppermute | solution.py:24
  20.7 35.0 %all-to-all-start = ((bf16[96,16,128]{2,1,0:T(8,128)(2,1)}), bf16[96,16,128]{2,1,0:T(8,128)(2,1)S(1)}, u32[]{:S(2)}, u32[]{:S(2)}) async-start(bf16[96,16,128]{2,1,0:T(8,128)(2,1)} %broadcast_in_dim.25), calls=%async_computation | async-start | bytes 786432 | tf_op jit(solution)/shard_map/all_to_all | solution.py:165
  35.8 20.0 %collective-permute-start.1 = (bf16[96,16,128]{2,1,0:T(8,128)(2,1)S(1)}, bf16[96,16,128]{2,1,0:T(8,128)(2,1)S(1)}, u32[]{:S(2)}, u32[]{:S(2)}) collective-permute-start(bf16[96,16,128]{2,1,0:T(8,128)(2,1)S(1)} %fusion.2), channel_id=1, source_target_pairs={{0,2},{1,3},{2,0},{3,1},{4,6},{5,7},{6,4},{7,5},{8,10},{9,11},{10,... | collective-permute-start | bytes 1179656 | tf_op jit(solution)/shard_map/ppermute | solution.py:28
  42.3 22.8 %collective-permute-start.8 = (bf16[96,16,128]{2,1,0:T(8,128)(2,1)}, bf16[96,16,128]{2,1,0:T(8,128)(2,1)}, u32[]{:S(2)}, u32[]{:S(2)}) collective-permute-start(bf16[96,16,128]{2,1,0:T(8,128)(2,1)} %fusion.4), channel_id=1, source_target_pairs={{0,3},{1,0},{2,1},{3,2},{4,7},{5,4},{6,5},{7,6},{8,11},{9,8},{10,9... | collective-permute-start | bytes 1179656 | tf_op jit(solution)/shard_map/ppermute | solution.py:28
  45.0 20.1 %collective-permute-start.7 = (bf16[96,16,128]{2,1,0:T(8,128)(2,1)S(1)}, bf16[96,16,128]{2,1,0:T(8,128)(2,1)}, u32[]{:S(2)}, u32[]{:S(2)}) collective-permute-start(bf16[96,16,128]{2,1,0:T(8,128)(2,1)S(1)} %fusion.3), channel_id=1, source_target_pairs={{0,1},{1,2},{2,3},{3,0},{4,5},{5,6},{6,7},{7,4},{8,9},{9,10},{10,1... | collective-permute-start | bytes 1179656 | tf_op jit(solution)/shard_map/ppermute | solution.py:28
  55.7 21.4 %collective-permute-start.4 = (bf16[96,16,128]{2,1,0:T(8,128)(2,1)S(1)}, bf16[96,16,128]{2,1,0:T(8,128)(2,1)S(1)}, u32[]{:S(2)}, u32[]{:S(2)}) collective-permute-start(bf16[96,16,128]{2,1,0:T(8,128)(2,1)S(1)} %all-to-all-done.refs_0_), channel_id=1, source_target_pairs={{0,3},{1,0},{2,1},{3,2},{4,7},{5,4},{6,5},{7,6},{8,11},{9,8},{10,9... | collective-permute-start | bytes 1179656 | tf_op jit(solution)/shard_map/ppermute | solution.py:28
  60.1 17.0 %collective-permute-start.3 = (bf16[96,16,128]{2,1,0:T(8,128)(2,1)S(1)}, bf16[96,16,128]{2,1,0:T(8,128)(2,1)S(1)}, u32[]{:S(2)}, u32[]{:S(2)}) collective-permute-start(bf16[96,16,128]{2,1,0:T(8,128)(2,1)S(1)} %all-to-all-done.refs_0_), channel_id=1, source_target_pairs={{0,2},{1,3},{2,0},{3,1},{4,6},{5,7},{6,4},{7,5},{8,10},{9,11},{10,... | collective-permute-start | bytes 1179656 | tf_op jit(solution)/shard_map/ppermute | solution.py:28
  62.5 20.4 %collective-permute-start.2 = (bf16[96,16,128]{2,1,0:T(8,128)(2,1)S(1)}, bf16[96,16,128]{2,1,0:T(8,128)(2,1)}, u32[]{:S(2)}, u32[]{:S(2)}) collective-permute-start(bf16[96,16,128]{2,1,0:T(8,128)(2,1)S(1)} %all-to-all-done.refs_0_), channel_id=1, source_target_pairs={{0,1},{1,2},{2,3},{3,0},{4,5},{5,6},{6,7},{7,4},{8,9},{9,10},{10,1... | collective-permute-start | bytes 1179656 | tf_op jit(solution)/shard_map/ppermute | solution.py:28
  68.1 27.7 %all-to-all-start.1 = ((bf16[96,16,128]{2,1,0:T(8,128)(2,1)}), bf16[96,16,128]{2,1,0:T(8,128)(2,1)}, u32[]{:S(2)}, u32[]{:S(2)}) async-start(bf16[96,16,128]{2,1,0:T(8,128)(2,1)} %pad_select_fusion), calls=%async_computation.1 | async-start | bytes 786432 | tf_op jit(solution)/shard_map/all_to_all | solution.py:205
  77.1 31.4 %copy-start = (bf16[128,8192]{1,0:T(8,128)(2,1)S(1)}, bf16[128,8192]{1,0:T(8,128)(2,1)}, u32[]{:S(2)}) copy-start(bf16[128,8192]{1,0:T(8,128)(2,1)} %hidden_ref.1) | copy-start | bytes 6291460
  77.1 31.4 %copy-start.1 = (bf16[128,128]{1,0:T(8,128)(2,1)S(1)}, bf16[128,128]{1,0:T(8,128)(2,1)}, u32[]{:S(2)}) copy-start(bf16[128,128]{1,0:T(8,128)(2,1)} %cot_ref.1) | copy-start | bytes 98308
  77.1 31.4 %copy-start.2 = (f32[128,128]{1,0:T(8,128)S(1)}, f32[128,128]{1,0:T(8,128)}, u32[]{:S(2)}) copy-start(f32[128,128]{1,0:T(8,128)} %get-tuple-element.21.inv_ref) | copy-start | bytes 196612
  77.1 31.4 %copy-start.3 = (s32[2]{0:T(128)S(1)}, s32[2]{0:T(128)}, u32[]{:S(2)}) copy-start(s32[2]{0:T(128)} %pad_add_fusion.6.pos_ref) | copy-start | bytes 28
  85.0 23.4 %collective-permute-start.6 = (bf16[3,96,16,128]{3,2,1,0:T(8,128)(2,1)}, bf16[3,96,16,128]{3,2,1,0:T(8,128)(2,1)}, u32[]{:S(2)}, u32[]{:S(2)}) collective-permute-start(bf16[3,96,16,128]{3,2,1,0:T(8,128)(2,1)} %pad_maximum_fusion), channel_id=1, source_target_pairs={{0,96},{96,0},{1,97},{97,1},{2,98},{98,2},{3,99},{99,3},{4,100},{1... | collective-permute-start | bytes 3538952 | tf_op jit(solution)/shard_map/ppermute | solution.py:24
  87.6 20.8 %collective-permute-start.5 = (bf16[96,16,128]{2,1,0:T(8,128)(2,1)S(1)}, bf16[96,16,128]{2,1,0:T(8,128)(2,1)}, u32[]{:S(2)}, u32[]{:S(2)}) collective-permute-start(bf16[96,16,128]{2,1,0:T(8,128)(2,1)S(1)} %all-to-all-done.refs_0_), channel_id=1, source_target_pairs={{0,96},{96,0},{1,97},{97,1},{2,98},{98,2},{3,99},{99,3},{4,100},{1... | collective-permute-start | bytes 1179656 | tf_op jit(solution)/shard_map/ppermute | solution.py:24
  97.5 18.1 %all-to-all-start.2 = ((f32[8,4,128]{2,1,0:T(4,128)}), f32[8,4,128]{2,1,0:T(4,128)S(1)}, u32[]{:S(2)}, u32[]{:S(2)}) async-start(f32[8,4,128]{2,1,0:T(4,128)} %broadcast_in_dim.27), calls=%async_computation.2 | async-start | bytes 32768 | tf_op jit(solution)/shard_map/all_to_all | solution.py:223
